TPU v7x, 128 devices: a whole 4x4x4 slice. The times are simulated.
128 devices in a mesh: ctx: 64 (over y, x, z_lo, core), fsdp: 2 (over z_hi).
Axes of the slice: x: 4, y: 4, z: 4 (z_hi: 2, z_lo: 2; z = z_hi * 2 + z_lo), core: 2. Of those that a mesh axis runs over, the one named last changes fastest.
Arguments:
- tokens: bfloat16 [2, 8192, 1024], P('fsdp', 'ctx'), may hold values from -6 to 6
- doc_lengths: int32 [2, 3], P('fsdp'), may hold values from 1 to 8064, as said below
- query_weight: bfloat16 [1024, 2048], P('fsdp'), may hold values from -0.1875 to 0.1875
- key_weight: bfloat16 [1024, 1024], P('fsdp'), may hold values from -0.1875 to 0.1875
- value_weight: bfloat16 [1024, 1024], P('fsdp'), may hold values from -0.1875 to 0.1875
- out_weight: bfloat16 [2048, 1024], P('fsdp'), may hold values from -0.125 to 0.125
- gate_weight: bfloat16 [1024, 3072], P('fsdp'), may hold values from -0.1875 to 0.1875
- up_weight: bfloat16 [1024, 3072], P('fsdp'), may hold values from -0.1875 to 0.1875
- down_weight: bfloat16 [3072, 1024], P('fsdp'), may hold values from -0.109375 to 0.109375
- query_gain: bfloat16 [2048], P('fsdp'), may hold values from 0.25 to 1.75
- key_gain: bfloat16 [1024], P('fsdp'), may hold values from 0.25 to 1.75
- attn_gain: bfloat16 [1024], P('fsdp'), may hold values from 0.25 to 1.75
- ffn_gain: bfloat16 [1024], P('fsdp'), may hold values from 0.25 to 1.75
- cotangent: bfloat16 [2, 8192, 1024], P('fsdp', 'ctx'), may hold values from -6 to 6
Outputs:
- output: bfloat16 [2, 8192, 1024], P('fsdp', 'ctx')
- tokens_grad: float32 [2, 8192, 1024], P('fsdp', 'ctx')
- query_weight_grad: float32 [1024, 2048], P('fsdp')
- key_weight_grad: float32 [1024, 1024], P('fsdp')
- value_weight_grad: float32 [1024, 1024], P('fsdp')
- out_weight_grad: float32 [2048, 1024], P('fsdp')
- gate_weight_grad: float32 [1024, 3072], P('fsdp')
- up_weight_grad: float32 [1024, 3072], P('fsdp')
- down_weight_grad: float32 [3072, 1024], P('fsdp')
- query_gain_grad: float32 [2048], P('fsdp')
- key_gain_grad: float32 [1024], P('fsdp')
- attn_gain_grad: float32 [1024], P('fsdp')
- ffn_gain_grad: float32 [1024], P('fsdp')
Inputs may be any that keep to these rules, and one draw needn't show every extreme that they name: `doc_lengths`: each row holds three document lengths in order; the middle one is 8064 and the outer two sum to 128.
All inputs are finite; a program needn't handle non-finite values.
Results may differ from a plain program's by a relative error of at most 0.035.
Values may be sent and summed in bfloat16 or wider, within the bound.
No kernel may reach another device: no remote copies, remote signals or barrier semaphores. Data moves between devices by JAX's collectives and lax.ppermute only.
A program may use at most 384 MiB of HBM per device.

v0:
```python
import math

import jax
import jax.numpy as jnp
from jax import lax
from jax.sharding import PartitionSpec as P

HEADS = 16
KVH = 8
HD = 128
HQ = 2048
HK = 1024


epsilon = 1e-06
rope_base = 1000000.0
masked_score = -1e30


def dot_plain(left_op, right_op):
    return jnp.dot(left_op, right_op, preferred_element_type=jnp.float32)


def dot_second(left_op, right_op):
    return lax.dot_general(
        left_op, right_op, (((1,), (1,)), ((), ())), preferred_element_type=jnp.float32
    )


def dot_first(left_op, right_op):
    return lax.dot_general(
        left_op, right_op, (((0,), (0,)), ((), ())), preferred_element_type=jnp.float32
    )


def rms_forward(tensor, gain_vec):
    inverse = lax.rsqrt(jnp.mean(tensor * tensor, axis=-1, keepdims=True) + epsilon)
    normed = tensor * inverse
    return (normed * gain_vec.astype(jnp.float32), normed, inverse)


def rms_backward(upstream, gain_vec, normed, inverse):
    scaled = upstream * gain_vec.astype(jnp.float32)
    gain_grad = jnp.sum(upstream * normed, axis=0)
    tensor_grad = inverse * (scaled - normed * jnp.mean(scaled * normed, axis=-1, keepdims=True))
    return (tensor_grad, gain_grad)


def stored_positions(stored, block_rows, total_rows):
    half_rows = block_rows // 2
    shard = stored // block_rows
    within = stored % block_rows
    return jnp.where(
        within < half_rows,
        shard * half_rows + within,
        total_rows - (shard + 2) * half_rows + within,
    )


def doc_layout(lengths, first_index, row_count, block_rows, total_rows):
    stored = first_index + jnp.arange(row_count, dtype=jnp.int32)
    positions = stored_positions(stored, block_rows, total_rows)
    first_end = lengths[0]
    second_end = lengths[0] + lengths[1]
    doc_ids = (positions >= first_end).astype(jnp.int32) + (positions >= second_end).astype(
        jnp.int32
    )
    return (positions, doc_ids)


def doc_place(lengths, positions, doc_ids):
    first_end = lengths[0]
    second_end = lengths[0] + lengths[1]
    doc_start = jnp.where(doc_ids == 0, 0, jnp.where(doc_ids == 1, first_end, second_end))
    return positions - doc_start


def rope_tables(places):
    half_size = HD // 2
    frequency = jnp.power(
        jnp.float32(rope_base), -jnp.arange(half_size, dtype=jnp.float32) * (2.0 / HD)
    )
    angles = places.astype(jnp.float32)[:, None] * frequency[None, :]
    return (jnp.cos(angles)[:, None, :], jnp.sin(angles)[:, None, :])


def rotate(tensor, cosine, sine_table):
    half_size = tensor.shape[-1] // 2
    first_half = tensor[..., :half_size]
    second = tensor[..., half_size:]
    return jnp.concatenate(
        [first_half * cosine - second * sine_table, second * cosine + first_half * sine_table],
        axis=-1,
    )


def allowed_pairs(query_pos, query_doc, key_pos, key_doc):
    same_doc = query_doc[:, None] == key_doc[None, :]
    return (same_doc & (key_pos[None, :] <= query_pos[:, None]))[:, None, None, :]


def score_grads(
    query_four, grad_four, key_four, value_four, log_total, row_delta, allowed, scaling
):
    scores = (
        jnp.einsum("qhgd,khd->qhgk", query_four, key_four, preferred_element_type=jnp.float32)
        * scaling
    )
    probabilities = jnp.where(allowed, jnp.exp(scores - log_total[..., None]), 0.0)
    prob_grad = jnp.einsum(
        "qhgd,khd->qhgk", grad_four, value_four, preferred_element_type=jnp.float32
    )
    score_low = (probabilities * (prob_grad - row_delta[..., None])).astype(jnp.bfloat16)
    return (probabilities, score_low)


def sweep_rows(step_fn, carried, pieces):
    row_count = pieces[0].shape[0]
    sub_rows = math.gcd(row_count, 512)

    def advance(number, running):
        offset = number * sub_rows
        sliced = tuple((lax.dynamic_slice_in_dim(member, offset, sub_rows, 0) for member in pieces))
        return step_fn(running, sliced, offset)

    return lax.fori_loop(0, row_count // sub_rows, advance, carried)


def per_device(
    tokens,
    doc_lengths,
    query_weight,
    key_weight,
    value_weight,
    out_weight,
    gate_weight,
    up_weight,
    down_weight,
    query_gain,
    key_gain,
    attn_gain,
    ffn_gain,
    cotangent,
):
    block_rows = tokens.shape[1]
    total_rows = block_rows * lax.axis_size("ctx")
    group_size = HEADS // KVH
    scaling = HD ** (-0.5)
    lengths = doc_lengths[0]
    first_row = lax.axis_index("ctx") * block_rows
    query_pos, query_doc = doc_layout(lengths, first_row, block_rows, block_rows, total_rows)
    query_max = jnp.max(query_pos)
    query_min = jnp.min(query_pos)
    cosine, sine_table = rope_tables(doc_place(lengths, query_pos, query_doc))
    source = tokens[0]
    shards = (
        query_weight,
        key_weight,
        value_weight,
        out_weight,
        gate_weight,
        up_weight,
        down_weight,
        query_gain,
        key_gain,
        attn_gain,
        ffn_gain,
    )
    gathered = (
        lax.all_gather(shards[0], "fsdp", axis=0, tiled=True),
        lax.all_gather(shards[1], "fsdp", axis=0, tiled=True),
        lax.all_gather(shards[2], "fsdp", axis=0, tiled=True),
        lax.all_gather(shards[3], "fsdp", axis=0, tiled=True),
        lax.all_gather(shards[4], "fsdp", axis=0, tiled=True),
        lax.all_gather(shards[5], "fsdp", axis=0, tiled=True),
        lax.all_gather(shards[6], "fsdp", axis=0, tiled=True),
        lax.all_gather(shards[7], "fsdp", axis=0, tiled=True),
        lax.all_gather(shards[8], "fsdp", axis=0, tiled=True),
        lax.all_gather(shards[9], "fsdp", axis=0, tiled=True),
        lax.all_gather(shards[10], "fsdp", axis=0, tiled=True),
    )
    (
        query_full,
        key_full,
        value_full,
        out_full,
        gate_full,
        up_full,
        down_full,
        query_scale,
        key_scale,
        attn_scale,
        ffn_scale,
    ) = gathered
    query_raw = dot_plain(source, query_full)
    key_raw = dot_plain(source, key_full)
    value_raw = dot_plain(source, value_full)
    query_out, query_normed, query_inverse = rms_forward(query_raw, query_scale)
    key_out, key_normed, key_inverse = rms_forward(key_raw, key_scale)
    query_four = rotate(query_out.reshape(block_rows, HEADS, HD), cosine, sine_table).astype(
        jnp.bfloat16
    )
    query_four = query_four.reshape(block_rows, KVH, group_size, HD)
    key_rows = rotate(key_out.reshape(block_rows, KVH, HD), cosine, sine_table).astype(jnp.bfloat16)
    key_rows = key_rows.reshape(block_rows, HK)
    value_rows = value_raw.astype(jnp.bfloat16)

    def forward_step(running, sliced, first_key):
        key_piece, value_piece = sliced
        row_count = key_piece.shape[0]
        key_pos, key_doc = doc_layout(lengths, first_key, row_count, block_rows, total_rows)

        def forward_compute(current):
            maximum, denominator, accumulated = current
            allowed = allowed_pairs(query_pos, query_doc, key_pos, key_doc)
            scores = (
                jnp.einsum(
                    "qhgd,khd->qhgk",
                    query_four,
                    key_piece.reshape(row_count, KVH, HD),
                    preferred_element_type=jnp.float32,
                )
                * scaling
            )
            scores = jnp.where(allowed, scores, masked_score)
            new_max = jnp.maximum(maximum, jnp.max(scores, axis=-1))
            weights = jnp.where(allowed, jnp.exp(scores - new_max[..., None]), 0.0)
            rescale = jnp.exp(maximum - new_max)
            denominator = denominator * rescale + jnp.sum(weights, axis=-1)
            accumulated = accumulated * rescale[..., None] + jnp.einsum(
                "qhgk,khd->qhgd",
                weights.astype(jnp.bfloat16),
                value_piece.reshape(row_count, KVH, HD),
                preferred_element_type=jnp.float32,
            )
            return (new_max, denominator, accumulated)

        return lax.cond(
            jnp.min(key_pos) <= query_max, forward_compute, lambda current: current, running
        )

    stats_shape = (block_rows, KVH, group_size)
    start_state = (
        jnp.full(stats_shape, masked_score, jnp.float32),
        jnp.zeros(stats_shape, jnp.float32),
        jnp.zeros(stats_shape + (HD,), jnp.float32),
    )
    maximum, denominator, accumulated = sweep_rows(
        forward_step,
        start_state,
        (
            lax.all_gather(key_rows, "ctx", axis=0, tiled=True),
            lax.all_gather(value_rows, "ctx", axis=0, tiled=True),
        ),
    )
    log_total = maximum + jnp.log(denominator)
    attended = (accumulated / denominator[..., None]).reshape(block_rows, HQ)
    attended_low = attended.astype(jnp.bfloat16)
    mixed_out = dot_plain(attended_low, out_full)
    attn_out, attn_normed, attn_inverse = rms_forward(mixed_out, attn_scale)
    hidden = source.astype(jnp.float32) + attn_out
    hidden_low = hidden.astype(jnp.bfloat16)
    gate_act = dot_plain(hidden_low, gate_full)
    up_act = dot_plain(hidden_low, up_full)
    sigmoid = jax.nn.sigmoid(gate_act)
    swish_act = gate_act * sigmoid
    inner_low = (swish_act * up_act).astype(jnp.bfloat16)
    down_out = dot_plain(inner_low, down_full)
    ffn_out, ffn_normed, ffn_inverse = rms_forward(down_out, ffn_scale)
    output = (hidden + ffn_out).astype(jnp.bfloat16)
    back_weights = (
        lax.all_gather(shards[0], "fsdp", axis=0, tiled=True),
        lax.all_gather(shards[1], "fsdp", axis=0, tiled=True),
        lax.all_gather(shards[2], "fsdp", axis=0, tiled=True),
        lax.all_gather(shards[3], "fsdp", axis=0, tiled=True),
        lax.all_gather(shards[4], "fsdp", axis=0, tiled=True),
        lax.all_gather(shards[5], "fsdp", axis=0, tiled=True),
        lax.all_gather(shards[6], "fsdp", axis=0, tiled=True),
        lax.all_gather(shards[7], "fsdp", axis=0, tiled=True),
        lax.all_gather(shards[8], "fsdp", axis=0, tiled=True),
        lax.all_gather(shards[9], "fsdp", axis=0, tiled=True),
        lax.all_gather(shards[10], "fsdp", axis=0, tiled=True),
    )
    (
        query_back,
        key_back,
        value_back,
        out_back,
        gate_back,
        up_back,
        down_back,
        query_scale_back,
        key_scale_back,
        attn_scale_back,
        ffn_scale_back,
    ) = back_weights
    upstream = cotangent[0].astype(jnp.float32)
    down_grad, ffn_gain_grad = rms_backward(upstream, ffn_scale_back, ffn_normed, ffn_inverse)
    down_low = down_grad.astype(jnp.bfloat16)
    down_weight_grad = dot_first(inner_low, down_low)
    inner_grad = dot_second(down_low, down_back)
    gate_low = (inner_grad * up_act * sigmoid * (1.0 + gate_act * (1.0 - sigmoid))).astype(
        jnp.bfloat16
    )
    up_low = (inner_grad * swish_act).astype(jnp.bfloat16)
    gate_weight_grad = dot_first(hidden_low, gate_low)
    up_weight_grad = dot_first(hidden_low, up_low)
    hidden_grad = upstream + dot_second(gate_low, gate_back) + dot_second(up_low, up_back)
    mixed_grad, attn_gain_grad = rms_backward(
        hidden_grad, attn_scale_back, attn_normed, attn_inverse
    )
    mixed_low = mixed_grad.astype(jnp.bfloat16)
    out_weight_grad = dot_first(attended_low, mixed_low)
    attended_grad = dot_second(mixed_low, out_back).astype(jnp.bfloat16)
    grad_four = attended_grad.reshape(block_rows, KVH, group_size, HD)
    row_delta = jnp.sum(
        grad_four.astype(jnp.float32) * attended.reshape(block_rows, KVH, group_size, HD), axis=-1
    )

    def query_step(running, sliced, first_key):
        key_piece, value_piece = sliced
        row_count = key_piece.shape[0]
        key_four = key_piece.reshape(row_count, KVH, HD)
        key_pos, key_doc = doc_layout(lengths, first_key, row_count, block_rows, total_rows)

        def query_compute(current):
            allowed = allowed_pairs(query_pos, query_doc, key_pos, key_doc)
            probabilities, score_low = score_grads(
                query_four,
                grad_four,
                key_four,
                value_piece.reshape(row_count, KVH, HD),
                log_total,
                row_delta,
                allowed,
                scaling,
            )
            return (
                current
                + jnp.einsum(
                    "qhgk,khd->qhgd", score_low, key_four, preferred_element_type=jnp.float32
                )
                * scaling
            )

        return lax.cond(
            jnp.min(key_pos) <= query_max, query_compute, lambda current: current, running
        )

    query_zero = jnp.zeros((block_rows, KVH, group_size, HD), jnp.float32)
    key_four_local = key_rows.reshape(block_rows, KVH, HD)
    value_four_local = value_rows.reshape(block_rows, KVH, HD)
    query_grad = sweep_rows(
        query_step,
        query_zero,
        (
            lax.all_gather(key_rows, "ctx", axis=0, tiled=True),
            lax.all_gather(value_rows, "ctx", axis=0, tiled=True),
        ),
    )
    total_all, delta_all = (
        lax.all_gather(log_total, "ctx", axis=0, tiled=True),
        lax.all_gather(row_delta, "ctx", axis=0, tiled=True),
    )

    def key_step(running, sliced, first_query):
        query_piece, grad_piece = sliced
        row_count = query_piece.shape[0]
        query_piece_four = query_piece.reshape(row_count, KVH, group_size, HD)
        grad_piece_four = grad_piece.reshape(row_count, KVH, group_size, HD)
        piece_pos, piece_doc = doc_layout(lengths, first_query, row_count, block_rows, total_rows)

        def key_compute(current):
            key_accum, value_accum = current
            allowed = allowed_pairs(piece_pos, piece_doc, query_pos, query_doc)
            piece_total = lax.dynamic_slice_in_dim(total_all, first_query, row_count, 0)
            piece_delta = lax.dynamic_slice_in_dim(delta_all, first_query, row_count, 0)
            probabilities, score_low = score_grads(
                query_piece_four,
                grad_piece_four,
                key_four_local,
                value_four_local,
                piece_total,
                piece_delta,
                allowed,
                scaling,
            )
            value_accum = value_accum + jnp.einsum(
                "qhgk,qhgd->khd",
                probabilities.astype(jnp.bfloat16),
                grad_piece_four,
                preferred_element_type=jnp.float32,
            )
            key_accum = (
                key_accum
                + jnp.einsum(
                    "qhgk,qhgd->khd",
                    score_low,
                    query_piece_four,
                    preferred_element_type=jnp.float32,
                )
                * scaling
            )
            return (key_accum, value_accum)

        return lax.cond(
            jnp.max(piece_pos) >= query_min, key_compute, lambda current: current, running
        )

    kv_zero = jnp.zeros((block_rows, KVH, HD), jnp.float32)
    key_grad, value_grad = sweep_rows(
        key_step,
        (kv_zero, kv_zero),
        (
            lax.all_gather(query_four.reshape(block_rows, HQ), "ctx", axis=0, tiled=True),
            lax.all_gather(attended_grad, "ctx", axis=0, tiled=True),
        ),
    )
    value_grad = value_grad.reshape(block_rows, HK)
    key_grad = rotate(key_grad, cosine, -sine_table).reshape(block_rows, HK)
    key_raw_grad, key_gain_grad = rms_backward(key_grad, key_scale_back, key_normed, key_inverse)
    query_grad = rotate(query_grad.reshape(block_rows, HEADS, HD), cosine, -sine_table).reshape(
        block_rows, HQ
    )
    query_raw_grad, query_gain_grad = rms_backward(
        query_grad, query_scale_back, query_normed, query_inverse
    )
    query_raw_low = query_raw_grad.astype(jnp.bfloat16)
    key_raw_low = key_raw_grad.astype(jnp.bfloat16)
    value_low = value_grad.astype(jnp.bfloat16)
    query_weight_grad = dot_first(source, query_raw_low)
    key_weight_grad = dot_first(source, key_raw_low)
    value_weight_grad = dot_first(source, value_low)
    tokens_grad = (
        hidden_grad
        + dot_second(query_raw_low, query_back)
        + dot_second(key_raw_low, key_back)
        + dot_second(value_low, value_back)
    )
    gradients = (
        query_weight_grad,
        key_weight_grad,
        value_weight_grad,
        out_weight_grad,
        gate_weight_grad,
        up_weight_grad,
        down_weight_grad,
        query_gain_grad,
        key_gain_grad,
        attn_gain_grad,
        ffn_gain_grad,
    )
    grad_shards = (
        lax.psum_scatter(
            gradients[0].astype(jnp.bfloat16), "fsdp", scatter_dimension=0, tiled=True
        ).astype(jnp.float32),
        lax.psum_scatter(
            gradients[1].astype(jnp.bfloat16), "fsdp", scatter_dimension=0, tiled=True
        ).astype(jnp.float32),
        lax.psum_scatter(
            gradients[2].astype(jnp.bfloat16), "fsdp", scatter_dimension=0, tiled=True
        ).astype(jnp.float32),
        lax.psum_scatter(
            gradients[3].astype(jnp.bfloat16), "fsdp", scatter_dimension=0, tiled=True
        ).astype(jnp.float32),
        lax.psum_scatter(
            gradients[4].astype(jnp.bfloat16), "fsdp", scatter_dimension=0, tiled=True
        ).astype(jnp.float32),
        lax.psum_scatter(
            gradients[5].astype(jnp.bfloat16), "fsdp", scatter_dimension=0, tiled=True
        ).astype(jnp.float32),
        lax.psum_scatter(
            gradients[6].astype(jnp.bfloat16), "fsdp", scatter_dimension=0, tiled=True
        ).astype(jnp.float32),
        lax.psum_scatter(
            gradients[7].astype(jnp.bfloat16), "fsdp", scatter_dimension=0, tiled=True
        ).astype(jnp.float32),
        lax.psum_scatter(
            gradients[8].astype(jnp.bfloat16), "fsdp", scatter_dimension=0, tiled=True
        ).astype(jnp.float32),
        lax.psum_scatter(
            gradients[9].astype(jnp.bfloat16), "fsdp", scatter_dimension=0, tiled=True
        ).astype(jnp.float32),
        lax.psum_scatter(
            gradients[10].astype(jnp.bfloat16), "fsdp", scatter_dimension=0, tiled=True
        ).astype(jnp.float32),
    )
    summed = lax.psum(
        (
            grad_shards[0],
            grad_shards[1],
            grad_shards[2],
            grad_shards[3],
            grad_shards[4],
            grad_shards[5],
            grad_shards[6],
            grad_shards[7],
            grad_shards[8],
            grad_shards[9],
            grad_shards[10],
        ),
        "ctx",
    )
    return (
        output[None],
        tokens_grad[None],
        summed[0],
        summed[1],
        summed[2],
        summed[3],
        summed[4],
        summed[5],
        summed[6],
        summed[7],
        summed[8],
        summed[9],
        summed[10],
    )


def solution(mesh):
    return jax.shard_map(
        per_device,
        mesh=mesh,
        in_specs=(
            P("fsdp", "ctx", None),
            P("fsdp", None),
            P("fsdp", None),
            P("fsdp", None),
            P("fsdp", None),
            P("fsdp", None),
            P("fsdp", None),
            P("fsdp", None),
            P("fsdp", None),
            P("fsdp"),
            P("fsdp"),
            P("fsdp"),
            P("fsdp"),
            P("fsdp", "ctx", None),
        ),
        out_specs=(
            P("fsdp", "ctx", None),
            P("fsdp", "ctx", None),
            P("fsdp", None),
            P("fsdp", None),
            P("fsdp", None),
            P("fsdp", None),
            P("fsdp", None),
            P("fsdp", None),
            P("fsdp", None),
            P("fsdp"),
            P("fsdp"),
            P("fsdp"),
            P("fsdp"),
        ),
        check_vma=False,
    )
```

profile of v0, /device:TPU:1, one launch (start us, length us, event | category | flops | bytes accessed | tf_op | source)
XLA Modules:
  0.0 2394.5 jit_solution(18040261954925244997)
XLA Ops:
  9.5 40.8 %all-gather.21.cloned.1.call-done = bf16[1024,1024]{1,0:T(8,128)(2,1)} async-done(((bf16[512,1024]{1,0:T(8,128)(2,1)}), bf16[1024,1024]{1,0:T(8,128)(2,1)}) %all-gather.21.cloned.1.call-update) | async-done | bytes 2097168 | tf_op jit(solution)/shard_map/all_gather | solution.py:172
  60.4 28.0 %all-gather.15.cloned.1.call-done = bf16[1024,1024]{1,0:T(8,128)(2,1)} async-done(((bf16[512,1024]{1,0:T(8,128)(2,1)}), bf16[1024,1024]{1,0:T(8,128)(2,1)}) %all-gather.15.cloned.1.call-update) | async-done | bytes 2097168 | tf_op jit(solution)/shard_map/all_gather | solution.py:171
  111.7 38.6 %all-gather.19.cloned.1.call-done = bf16[1024,2048]{1,0:T(8,128)(2,1)} async-done(((bf16[512,2048]{1,0:T(8,128)(2,1)}), bf16[1024,2048]{1,0:T(8,128)(2,1)}) %all-gather.19.cloned.1.call-update) | async-done | bytes 4194320 | tf_op jit(solution)/shard_map/all_gather | solution.py:170
  156.5 118.2 %all-gather.23.cloned.1.call-done = bf16[8192,1024]{1,0:T(8,128)(2,1)} async-done(((bf16[128,1024]{1,0:T(8,128)(2,1)}), bf16[8192,1024]{1,0:T(8,128)(2,1)}) %all-gather.23.cloned.1.call-update) | async-done | bytes 16777232 | tf_op jit(solution)/shard_map/all_gather | solution.py:253
  274.7 21.4 copy.169
  296.1 142.6 %all-gather.17.cloned.1.call-done = bf16[8192,1024]{0,1:T(8,128)(2,1)} async-done(((bf16[128,1024]{0,1:T(8,128)(2,1)}), bf16[8192,1024]{0,1:T(8,128)(2,1)}) %all-gather.17.cloned.1.call-update) | async-done | bytes 16777232 | tf_op jit(solution)/shard_map/all_gather | solution.py:252
  438.8 132.6 %while.60 = (s32[]{:T(128)}, f32[128,8,2]{0,2,1:T(2,128)S(1)}, f32[128,8,2]{0,2,1:T(2,128)S(1)}, f32[128,8,2,128]{3,0,2,1:T(8,128)S(1)}, s32[]{:T(128)}, /*index...) while((s32[]{:T(128)}, f32[128,8,2]{0,2,1:T(2,128)S(1)}, ...), condition=%wide.region_9.10_spmd.clone.clone, body=%wide.region_3.9_spmd.clone.clone.sunk | while | flops 551266944 | bytes 21909896 | solution.py:126
  591.0 80.5 %all-gather.29.cloned.1.call-done = bf16[1024,3072]{1,0:T(8,128)(2,1)} async-done(((bf16[512,3072]{1,0:T(8,128)(2,1)}), bf16[1024,3072]{1,0:T(8,128)(2,1)}) %all-gather.29.cloned.1.call-update) | async-done | bytes 6291472 | tf_op jit(solution)/shard_map/all_gather | solution.py:175
  677.1 79.9 %all-gather.31.cloned.1.call-done = bf16[3072,1024]{1,0:T(8,128)(2,1)} async-done(((bf16[1536,1024]{1,0:T(8,128)(2,1)}), bf16[3072,1024]{1,0:T(8,128)(2,1)}) %all-gather.31.cloned.1.call-update) | async-done | bytes 6291472 | tf_op jit(solution)/shard_map/all_gather | solution.py:176
  787.1 218.1 %while.61 = (s32[]{:T(128)}, f32[128,8,2,128]{3,0,2,1:T(8,128)}, s32[]{:T(128)}, s32[3]{0:T(128)S(1)}, s32[]{:T(128)}, /*index=5*/bf16[8192,1024]{0,1:T(8,128)(2...) while((s32[]{:T(128)}, f32[128,8,2,128]{3,0,2,1:T(8,128)}, ...), condition=%wide.region_19.20_spmd.clone.clone, body=%wide.region_15.19_spmd.clone.clone.sunk | while | flops 812358272 | bytes 19044740 | solution.py:126
  1037.2 84.0 %all_gather.80 = f32[8192,8,2]{0,1,2:T(8,128)S(1)} all-gather(f32[128,8,2]{0,1,2:T(8,128)S(1)} %copy.180), channel_id=1, replica_groups=mesh['ctx'=64,'fsdp'=2] {'ctx'}, dimensions={0}, use_global_device_ids=true | all-gather | bytes 532480 | tf_op jit(solution)/shard_map/all_gather | solution.py:363
  1122.4 83.6 %all_gather.78 = f32[8192,8,2]{0,2,1:T(2,128)} all-gather(f32[128,8,2]{0,2,1:T(2,128)S(1)} %copy-done.46), channel_id=1, replica_groups=mesh['ctx'=64,'fsdp'=2] {'ctx'}, dimensions={0}, use_global_device_ids=true | all-gather | bytes 532480 | tf_op jit(solution)/shard_map/all_gather | solution.py:362
  1206.0 40.7 %copy.182 = bf16[8192,2048]{0,1:T(8,128)(2,1)} copy(bf16[8192,2048]{1,0:T(8,128)(2,1)} %all-gather.35.cloned.1.call-done) | data formatting | bytes 67108864
  1247.6 367.9 %while.62 = (s32[]{:T(128)}, f32[128,8,128]{2,0,1:T(8,128)}, f32[128,8,128]{2,0,1:T(8,128)S(1)}, s32[]{:T(128)}, s32[3]{0:T(128)S(1)}, /*index=5*/s32[]{:T(128)}...) while((s32[]{:T(128)}, f32[128,8,128]{2,0,1:T(8,128)}, ...), condition=%wide.region_26.27_spmd.clone.clone, body=%wide.region_22.26_spmd.clone.clone.sunk | while | flops 1084856960 | bytes 32428444 | solution.py:126
  1250.2 20.2 conditional.14
  1273.1 20.1 conditional.14
  1295.8 20.3 conditional.14
  1318.7 20.2 conditional.14
  1341.5 20.8 conditional.14
  1364.9 20.6 conditional.14
  1388.1 20.1 conditional.14
  1410.9 21.2 conditional.14
  1434.7 20.3 conditional.14
  1457.6 20.6 conditional.14
  1480.8 20.1 conditional.14
  1503.6 20.6 conditional.14
  1526.8 20.2 conditional.14
  1549.6 20.4 conditional.14
  1572.6 20.1 conditional.14
  1595.4 20.1 conditional.14
  1651.7 37.7 %reduce-scatter.12.cloned.1.call-done = bf16[512,1024]{0,1:T(8,128)(2,1)} async-done(((bf16[1024,1024]{0,1:T(8,128)(2,1)}), bf16[512,1024]{0,1:T(8,128)(2,1)}) %reduce-scatter.12.cloned.1.call-update) | async-done | bytes 1048592 | tf_op jit(solution)/shard_map/reduce_scatter | solution.py:460
  1689.4 688.0 %all-reduce.7 = (f32[512,2048]{0,1:T(8,128)}, f32[512,1024]{0,1:T(8,128)}, f32[512,1024]{0,1:T(8,128)S(1)}, f32[1024,1024]{1,0:T(8,128)}, f32[512,3072]{1,0:T(8,...) all-reduce(bf16[512,2048]{0,1:T(8,128)(2,1)} %reduce-scatter.8.clon, ...), channel_id=1, replica_groups=mesh['ctx'=64,'fsdp'=2] {'ctx'}, use_global_device_ids=true, to_apply=%region_29.30 | all-reduce | flops 7866880 | bytes 47206400 | tf_op jit(solution)/shard_map/psum | solution.py:488
  (918 shorter events, 1085.0 us)
Async XLA Ops:
  7.2 43.1 %copy-start.1 = (bf16[1,128,1024]{2,1,0:T(8,128)(2,1)S(1)}, bf16[1,128,1024]{2,1,0:T(8,128)(2,1)}, u32[]{:S(2)}) copy-start(bf16[1,128,1024]{2,1,0:T(8,128)(2,1)} %param.26) | copy-start | bytes 786436
  7.2 45.9 %copy-start.56 = (bf16[512]{0:T(512)(128)(2,1)S(1)}, bf16[512]{0:T(512)(128)(2,1)}, u32[]{:S(2)}) copy-start(bf16[512]{0:T(512)(128)(2,1)} %param.36) | copy-start | bytes 3076
  7.2 50.6 %copy-start.40 = (s32[1,3]{1,0:T(1,128)S(1)}, s32[1,3]{1,0:T(1,128)}, u32[]{:S(2)}) copy-start(s32[1,3]{1,0:T(1,128)} %param.27) | copy-start | bytes 40
  7.2 43.0 %all-gather.21.cloned.1.call-start = ((), (), s32[]{:S(2)}) async-start(), calls=%async_computation.10 | async-start | bytes 3145728 | tf_op jit(solution)/shard_map/all_gather | solution.py:172
  7.9 80.5 %all-gather.15.cloned.1.call-start = ((), (), s32[]{:S(2)}) async-start(), calls=%async_computation.7 | async-start | bytes 3145728 | tf_op jit(solution)/shard_map/all_gather | solution.py:171
  8.7 141.7 %all-gather.19.cloned.1.call-start = ((), (), s32[]{:S(2)}) async-start(), calls=%async_computation.9 | async-start | bytes 6291456 | tf_op jit(solution)/shard_map/all_gather | solution.py:170
  9.4 265.2 %all-gather.23.cloned.1.call-start = ((), (), s32[]{:S(2)}) async-start(), calls=%async_computation.11 | async-start | bytes 17039360 | tf_op jit(solution)/shard_map/all_gather | solution.py:253
  53.0 385.7 %all-gather.17.cloned.1.call-start = ((), (), s32[]{:S(2)}) async-start(), calls=%async_computation.8 | async-start | bytes 17039360 | tf_op jit(solution)/shard_map/all_gather | solution.py:252
  57.8 35.3 %copy-start.43 = (f32[2,1,512]{2,1,0:T(1,128)}, f32[2,1,512]{2,1,0:T(1,128)S(1)}, u32[]{:S(2)}) copy-start(f32[2,1,512]{2,1,0:T(1,128)S(1)} %convert_element_type.350) | copy-start | bytes 12292
  60.4 35.1 %copy-start.35 = (f32[128,64]{0,1:T(8,128)}, f32[128,64]{0,1:T(8,128)S(1)}, u32[]{:S(2)}) copy-start(f32[128,64]{0,1:T(8,128)S(1)} %get-tuple-element.1920) | copy-start | bytes 98308
  60.4 719.0 %copy-start.37 = (f32[128,64]{0,1:T(8,128)}, f32[128,64]{0,1:T(8,128)S(1)}, u32[]{:S(2)}) copy-start(f32[128,64]{0,1:T(8,128)S(1)} %get-tuple-element.1918) | copy-start | bytes 98308
  92.5 481.6 %all-gather.25.cloned.1.call-start = ((), (), s32[]{:S(2)}) async-start(), calls=%async_computation.12 | async-start | bytes 6291456 | tf_op jit(solution)/shard_map/all_gather | solution.py:173
  93.1 492.9 %all-gather.27.cloned.1.call-start = ((), (), s32[]{:S(2)}) async-start(), calls=%async_computation.13 | async-start | bytes 9437184 | tf_op jit(solution)/shard_map/all_gather | solution.py:174
  93.9 577.6 %all-gather.29.cloned.1.call-start = ((), (), s32[]{:S(2)}) async-start(), calls=%async_computation.14 | async-start | bytes 9437184 | tf_op jit(solution)/shard_map/all_gather | solution.py:175
  94.7 662.3 %all-gather.31.cloned.1.call-start = ((), (), s32[]{:S(2)}) async-start(), calls=%async_computation.15 | async-start | bytes 9437184 | tf_op jit(solution)/shard_map/all_gather | solution.py:176
  95.4 1110.6 %all-gather.35.cloned.1.call-start = ((), (), s32[]{:S(2)}) async-start(), calls=%async_computation.17 | async-start | bytes 34078720 | tf_op jit(solution)/shard_map/all_gather | solution.py:416
  101.0 53.6 %copy-start.41 = (f32[2048]{0:T(1024)}, f32[2048]{0:T(1024)S(1)}, u32[]{:S(2)}) copy-start(f32[2048]{0:T(1024)S(1)} %convert_element_type.302) | copy-start | bytes 24580
  577.4 13.6 copy-start.11
  677.1 83.9 %copy-start.6 = (bf16[128,3072]{1,0:T(8,128)(2,1)}, bf16[128,3072]{1,0:T(8,128)(2,1)S(1)}, u32[]{:S(2)}) copy-start(bf16[128,3072]{1,0:T(8,128)(2,1)S(1)} %get-tuple-element.1929) | copy-start | bytes 2359300
  774.5 472.3 %all-gather.33.cloned.1.call-start = ((), (), s32[]{:S(2)}) async-start(), calls=%async_computation.16 | async-start | bytes 34078720 | tf_op jit(solution)/shard_map/all_gather | solution.py:415
  778.9 846.4 %reduce-scatter.8.cloned.1.call-start = ((), (), s32[]{:S(2)}) async-start(), calls=%async_computation.18 | async-start | bytes 6291456 | tf_op jit(solution)/shard_map/reduce_scatter | solution.py:454
  1014.0 611.4 %reduce-scatter.14.cloned.1.call-start = ((), (), s32[]{:S(2)}) async-start(), calls=%async_computation.21 | async-start | bytes 6291456 | tf_op jit(solution)/shard_map/reduce_scatter | solution.py:463
  1018.3 607.1 %reduce-scatter.20.cloned.1.call-start = ((), (), s32[]{:S(2)}) async-start(), calls=%async_computation.24 | async-start | bytes 9437184 | tf_op jit(solution)/shard_map/reduce_scatter | solution.py:472
  1024.0 601.4 %reduce-scatter.16.cloned.1.call-start = ((), (), s32[]{:S(2)}) async-start(), calls=%async_computation.22 | async-start | bytes 9437184 | tf_op jit(solution)/shard_map/reduce_scatter | solution.py:466
  1029.7 595.8 %reduce-scatter.18.cloned.1.call-start = ((), (), s32[]{:S(2)}) async-start(), calls=%async_computation.23 | async-start | bytes 9437184 | tf_op jit(solution)/shard_map/reduce_scatter | solution.py:469
  1035.3 87.1 %copy-start.46 = (f32[128,8,2]{0,2,1:T(2,128)S(1)}, f32[128,8,2]{0,2,1:T(2,128)}, u32[]{:S(2)}) copy-start(f32[128,8,2]{0,2,1:T(2,128)} %get-tuple-element.2450) | copy-start | bytes 24580
  1035.4 616.3 %reduce-scatter.10.cloned.1.call-start = ((), (), s32[]{:S(2)}) async-start(), calls=%async_computation.19 | async-start | bytes 3145728 | tf_op jit(solution)/shard_map/reduce_scatter | solution.py:457
  1247.6 369.4 %copy-start.36 = (f32[128,64]{0,1:T(8,128)S(1)}, f32[128,64]{0,1:T(8,128)}, u32[]{:S(2)}) copy-start(f32[128,64]{0,1:T(8,128)} %copy-done.35) | copy-start | bytes 98308
  1247.6 369.4 %copy-start.38 = (f32[128,64]{0,1:T(8,128)S(1)}, f32[128,64]{0,1:T(8,128)}, u32[]{:S(2)}) copy-start(f32[128,64]{0,1:T(8,128)} %copy-done.37) | copy-start | bytes 98308
  1619.9 69.5 %reduce-scatter.12.cloned.1.call-start = ((), (), s32[]{:S(2)}) async-start(), calls=%async_computation.20 | async-start | bytes 3145728 | tf_op jit(solution)/shard_map/reduce_scatter | solution.py:460
  1620.0 16.1 copy-start.8
  1623.4 13.6 copy-start.21
  (66 other events, 234.4 us)
Sparse Core Ops, SparseCore 0:
  9.7 40.5 all-gather.20
  51.9 36.4 all-gather.14
  90.1 60.2 all-gather.18
  151.9 122.6 all-gather.22
  276.1 162.5 all-gather.16
  440.2 60.3 all-gather.24
  502.2 83.7 all-gather.26
  587.7 83.7 all-gather.28
  673.1 83.7 all-gather.30
  774.6 186.8 all-gather.34
  963.1 240.1 all-gather.32
  1206.1 58.8 reduce-scatter.7
  1268.1 57.6 reduce-scatter.13
  1328.6 80.4 reduce-scatter.19
  1412.1 80.4 reduce-scatter.15
  1495.4 80.4 reduce-scatter.17
  1620.0 31.6 reduce-scatter.9
  1654.5 34.8 reduce-scatter.11
where the time goes:
time: 2410 us; the launch traced here: 2390 us
  blocking collectives  883 us (37%)
  waiting for transfers between devices  592 us (25%)
  matrix products  491 us (20%)
  local copies, waits for them, and re-layouts  232 us (10%)
  other arithmetic  112 us (5%)
  loops' own time  66.1 us (3%)
    psum x1, blocking collectives, per_device(): lax.psum((grad_shards[0], grad_shards[1], grad_shards[2], grad_shards[3],...  688 us
    all_gather x1, waiting for transfers between devices, per_device(): lax.all_gather(key_rows, 'ctx', axis=0, tiled=True)  143 us
    dot_general x16, matrix products, key_compute(): jnp.einsum('qhgk,qhgd->khd', score_low, query_piece_four, preferred_eleme...  127 us
    all_gather x1, waiting for transfers between devices, per_device(): lax.all_gather(value_rows, 'ctx', axis=0, tiled=True)  118 us
    dynamic_slice x48, local copies, waits for them, and re-layouts, advance(): lax.dynamic_slice_in_dim(member, offset, sub_rows, 0)  118 us
    dot_general x16, matrix products, query_compute(): jnp.einsum('qhgk,khd->qhgd', score_low, key_four, preferred_element_type=...  91.6 us
    dot_general x32, matrix products, score_grads(): jnp.einsum('qhgd,khd->qhgk', query_four, key_four, preferred_element_type...  90.1 us
    unnamed x142, local copies, waits for them, and re-layouts  86 us
  transfers between devices with their start and end apart: 18, of which 10 were waited for; matrix products, arithmetic and copies ran while one was open for 33% of the time, Pallas kernels for 0%

commit v1 on v0

v1 whole, which is shorter than its diff:
```python
import functools
import math

import jax
import jax.numpy as jnp
from jax import lax
from jax.experimental import pallas as pl
from jax.experimental.pallas import tpu as pltpu
from jax.sharding import Mesh
from jax.sharding import PartitionSpec as P

D = 1024
HEADS = 16
KVH = 8
HD = 128
FF = 3072
BLK = 128
HQ = 2048
HK = 1024
SEQ = 8192

epsilon = 1e-06
rope_base = 1000000.0
masked_score = -1e30
score_scale = HD**-0.5
log2_scale = score_scale * math.log2(math.e)
half_blk = BLK // 2
group_rows = 8 * half_blk

bf16 = jnp.bfloat16
f32 = jnp.float32

TOKEN_AXES = ("y", "x", "zl", "co")
HEAD_AXES = ("x", "zl")
HEAD_LINKS = ("x0", "x1", "zA")

edge_a = [(0, 1), (1, 0), (2, 3), (3, 2)]
edge_b = [(1, 2), (2, 1), (3, 0), (0, 3)]
swap = [(0, 1), (1, 0)]
LINKS = {
    "x0": ("x", edge_a),
    "x1": ("x", edge_b),
    "y0": ("y", edge_a),
    "y1": ("y", edge_b),
    "zA": ("zl", swap),
    "zB": (("zl", "zh"), [(0, 3), (3, 0), (1, 2), (2, 1)]),
    "co": ("co", swap),
    "zh": ("zh", swap),
}


def link_bit(link):
    if link in ("x0", "y0"):
        place = lax.axis_index(link[0])
        return ((place == 1) | (place == 2)).astype(jnp.int32)
    if link in ("x1", "y1"):
        return (lax.axis_index(link[0]) >= 2).astype(jnp.int32)
    if link == "zA":
        return lax.axis_index("zl") ^ lax.axis_index("zh")
    if link == "zB":
        return lax.axis_index("zh")
    return lax.axis_index(link)


def across(array, link):
    axis, pairs = LINKS[link]
    return lax.ppermute(array, axis, pairs)


def dot_plain(left_op, right_op):
    return jnp.dot(left_op, right_op, preferred_element_type=f32)


def dot_second(left_op, right_op):
    return lax.dot_general(
        left_op, right_op, (((1,), (1,)), ((), ())), preferred_element_type=f32
    )


def dot_first(left_op, right_op):
    return lax.dot_general(
        left_op, right_op, (((0,), (0,)), ((), ())), preferred_element_type=f32
    )


def rms_forward(tensor, gain_vec):
    inverse = lax.rsqrt(jnp.mean(tensor * tensor, axis=-1, keepdims=True) + epsilon)
    normed = tensor * inverse
    return (normed * gain_vec.astype(f32), normed, inverse)


def rms_backward(upstream, gain_vec, normed, inverse):
    scaled = upstream * gain_vec.astype(f32)
    gain_grad = jnp.sum(upstream * normed, axis=0)
    tensor_grad = inverse * (scaled - normed * jnp.mean(scaled * normed, axis=-1, keepdims=True))
    return (tensor_grad, gain_grad)


def halve(array, link):
    rows = array.shape[0] // 2
    bit = link_bit(link)
    sent = lax.dynamic_slice_in_dim(array, (1 - bit) * rows, rows, 0)
    kept = lax.dynamic_slice_in_dim(array, bit * rows, rows, 0)
    got = across(sent, link)
    return (kept.astype(f32) + got.astype(f32)).astype(bf16)


def double(array, link):
    got = across(array, link)
    return jnp.where(
        link_bit(link) == 0, jnp.concatenate([array, got]), jnp.concatenate([got, array])
    )


def double_in_place(array, link, axis=0):
    got = across(array, link)
    bit = {
        "x0": lambda: lax.axis_index("x") % 2,
        "x1": lambda: lax.axis_index("x") // 2,
        "zA": lambda: lax.axis_index("zl"),
    }[link]()
    return jnp.where(
        bit == 0,
        jnp.concatenate([array, got], axis=axis),
        jnp.concatenate([got, array], axis=axis),
    )


def sum_over(array, links):
    for link in links:
        array = array + across(array, link)
    return array


def high_low(values):
    high = values.astype(bf16)
    return jnp.stack([high, (values - high.astype(f32)).astype(bf16)])


def rotate(tensor, cosine, sine_table):
    half_size = HD // 2
    first_half = tensor[..., :half_size]
    second = tensor[..., half_size:]
    return jnp.concatenate(
        [first_half * cosine - second * sine_table, second * cosine + first_half * sine_table],
        axis=-1,
    )


def half_positions(index, y, co, half):
    block = 16 * y + 2 * (index // half_blk) + co
    inner = index % half_blk
    return jnp.where(half == 0, block * half_blk + inner, SEQ - (block + 1) * half_blk + inner)


def query_masks(info_ref, half):
    y, co, first_end, second_end = info_ref[0], info_ref[1], info_ref[2], info_ref[3]
    index = lax.broadcasted_iota(jnp.int32, (1, group_rows), 1)
    position = half_positions(index, y, co, half)
    start = jnp.where(position >= second_end, second_end, 0)
    start = jnp.where((position >= first_end) & (position < second_end), first_end, start)
    return position, start, position >= second_end


def pair_mask(group, key_half, query_pos, query_start):
    index = lax.broadcasted_iota(jnp.int32, (group_rows, 1), 0)
    key_pos = half_positions(index, group // 2, group % 2, key_half)
    return (key_pos >= query_start) & (key_pos <= query_pos)


def open_steps(y, half):
    count = jnp.where(half == 0, jnp.maximum(2 * y - 2, 0), 6 + 6 - 2 * y)

    def chunk(step):
        late = step >= 6
        group = jnp.where(late, step - 6 + 2 * y + 2, step + 2)
        return group, jnp.where(late, 1, 0)

    return count, chunk


def masked_steps(y, half):
    count = jnp.where((half == 0) & (y == 0), 2, 4)

    def chunk(step):
        own = step >= 2
        group = jnp.where(own, 2 * y + step - 2, step)
        return group, jnp.where(own, half, 0)

    return count, chunk


def slot_of(group, key_half, y, co):
    other_y = group // 2
    beside = (other_y ^ 1) == y
    across_ring = (3 - other_y) == y
    first = jnp.where(key_half == 0, beside, across_ring)
    second = jnp.where(key_half == 0, across_ring, beside)
    ring = jnp.where(other_y == y, 0, jnp.where(first, 1, jnp.where(second, 2, 3)))
    return (group % 2) ^ co, key_half, ring


def load_chunks(pieces, kvs, sems):
    copies = []
    for number, piece in enumerate(pieces):
        core, rest = divmod(number, 4)
        half, pair = divmod(rest, 2)
        copies.append(
            pltpu.make_async_copy(piece, kvs.at[core, half, pl.ds(2 * pair, 2)], sems.at[number])
        )
    for copy in copies:
        copy.start()
    return copies


def forward_kernel(info_ref, query_ref, *refs):
    pieces, (low_ref, full_ref, total_ref), (kvs, sems, qt, top, denom, acc) = (
        refs[:8],
        refs[8:11],
        refs[11:],
    )
    y, co = info_ref[0], info_ref[1]
    for copy in load_chunks(pieces, kvs, sems):
        copy.wait()

    def half_body(half, carry):
        query_pos, query_start, last_doc = query_masks(info_ref, half)
        for head in range(2):
            lanes = slice(head * HD, (head + 1) * HD)
            qt[head] = query_ref[half, :, lanes].astype(f32).T.astype(bf16)
            top[head] = jnp.full((1, group_rows), masked_score, f32)
            denom[head] = jnp.zeros((1, group_rows), f32)
            acc[head] = jnp.zeros((HD, group_rows), f32)

        def step(group, key_half, masked):
            slot = slot_of(group, key_half, y, co)
            keys = kvs[(*slot, slice(None), slice(0, HD))]
            values = kvs[(*slot, slice(None), slice(HD, 2 * HD))]
            if masked:
                mask = pair_mask(group, key_half, query_pos, query_start)
            for head in range(2):
                scores = dot_plain(keys, qt[head])
                if masked:
                    scores = jnp.where(mask, scores, masked_score)
                old_top = top[head]
                new_top = jnp.maximum(old_top, jnp.max(scores, axis=0, keepdims=True))
                weights = jnp.exp2(scores - new_top)
                rescale = jnp.exp2(old_top - new_top)
                denom[head] = denom[head] * rescale + jnp.sum(weights, axis=0, keepdims=True)
                acc[head] = acc[head] * rescale + dot_first(values, weights.astype(bf16))
                top[head] = new_top

        count, chunk = open_steps(y, half)

        def open_body(number, inner):
            step(*chunk(number), False)
            return inner

        lax.fori_loop(0, count, open_body, 0)
        for head in range(2):
            top[head] = jnp.where(last_doc, masked_score, top[head])
            denom[head] = jnp.where(last_doc, 0.0, denom[head])
            acc[head] = jnp.where(last_doc, 0.0, acc[head])
        masked_count, masked_chunk = masked_steps(y, half)

        def masked_body(number, inner):
            step(*masked_chunk(number), True)
            return inner

        lax.fori_loop(0, masked_count, masked_body, 0)
        for head in range(2):
            lanes = slice(head * HD, (head + 1) * HD)
            attended = acc[head] / denom[head]
            full_ref[half, head] = attended
            total_ref[half, head] = top[head] + jnp.log2(denom[head])
            rows = attended.T.astype(bf16)
            for owner in range(8):
                low_ref[owner, half, :, lanes] = rows[owner * half_blk : (owner + 1) * half_blk]
        return carry

    lax.fori_loop(0, 2, half_body, 0)


def backward_kernel(info_ref, query_ref, grad_ref, full_ref, total_ref, *refs):
    pieces, (dq_ref, sent_ref, kept_ref), (kvs, sems, qt, gt, delta, dqt, dkv) = (
        refs[:8],
        refs[8:11],
        refs[11:],
    )
    y, co = info_ref[0], info_ref[1]
    copies = load_chunks(pieces, kvs, sems)
    dkv[...] = jnp.zeros_like(dkv)
    for copy in copies:
        copy.wait()

    def half_body(half, carry):
        query_pos, query_start, last_doc = query_masks(info_ref, half)
        for head in range(2):
            lanes = slice(head * HD, (head + 1) * HD)
            qt[head] = query_ref[half, :, lanes].astype(f32).T.astype(bf16)
            grad_t = grad_ref[half, :, lanes].astype(f32).T
            gt[head] = grad_t.astype(bf16)
            delta[head] = jnp.sum(grad_t * full_ref[half, head], axis=0, keepdims=True)
            dqt[head] = jnp.zeros((HD, group_rows), f32)

        def step(group, key_half, masked):
            slot = slot_of(group, key_half, y, co)
            key_lanes = (*slot, slice(None), slice(0, HD))
            value_lanes = (*slot, slice(None), slice(HD, 2 * HD))
            keys = kvs[key_lanes]
            values = kvs[value_lanes]
            if masked:
                mask = pair_mask(group, key_half, query_pos, query_start)
            key_total = dkv[key_lanes]
            value_total = dkv[value_lanes]
            for head in range(2):
                lanes = slice(head * HD, (head + 1) * HD)
                scores = dot_plain(keys, qt[head])
                total = total_ref[half, head]
                if masked:
                    scores = jnp.where(mask, scores, masked_score)
                else:
                    total = jnp.where(last_doc, -masked_score, total)
                probs = jnp.exp2(scores - total)
                value_total += dot_plain(probs.astype(bf16), grad_ref[half, :, lanes])
                prob_grad = dot_plain(values, gt[head])
                low = (probs * (prob_grad - delta[head])).astype(bf16)
                key_total += dot_plain(low, query_ref[half, :, lanes])
                dqt[head] += dot_first(keys, low)
            dkv[key_lanes] = key_total
            dkv[value_lanes] = value_total

        count, chunk = open_steps(y, half)

        def open_body(number, inner):
            step(*chunk(number), False)
            return inner

        lax.fori_loop(0, count, open_body, 0)
        masked_count, masked_chunk = masked_steps(y, half)

        def masked_body(number, inner):
            step(*masked_chunk(number), True)
            return inner

        lax.fori_loop(0, masked_count, masked_body, 0)
        for head in range(2):
            lanes = slice(head * HD, (head + 1) * HD)
            dq_ref[half, :, lanes] = dqt[head].T * score_scale
        return carry

    lax.fori_loop(0, 2, half_body, 0)

    def store_body(number, carry):
        half, ring = number // 4, number % 4
        for core, ref in enumerate((kept_ref, sent_ref)):
            ref[half, ring, :, :HD] = (dkv[core, half, ring, :, :HD] * math.log(2.0)).astype(bf16)
            ref[half, ring, :, HD:] = dkv[core, half, ring, :, HD:].astype(bf16)
        return carry

    lax.fori_loop(0, 8, store_body, 0)


smem = pl.BlockSpec(memory_space=pltpu.SMEM)
vmem = pl.BlockSpec(memory_space=pltpu.VMEM)
anywhere = pl.BlockSpec(memory_space=pl.ANY)
PAIRS = 4 * 2 * group_rows * 9 * group_rows
CHUNKS = (2, 2, 4, group_rows, 2 * HD)


def attention_forward(info, queries, pieces):
    return pl.pallas_call(
        forward_kernel,
        name="attention_forward",
        out_shape=(
            jax.ShapeDtypeStruct((8, 2, half_blk, 2 * HD), bf16),
            jax.ShapeDtypeStruct((2, 2, HD, group_rows), f32),
            jax.ShapeDtypeStruct((2, 2, 1, group_rows), f32),
        ),
        in_specs=[smem, vmem] + [anywhere] * 8,
        out_specs=[vmem] * 3,
        scratch_shapes=[
            pltpu.VMEM(CHUNKS, bf16),
            pltpu.SemaphoreType.DMA((8,)),
            pltpu.VMEM((2, HD, group_rows), bf16),
            pltpu.VMEM((2, 1, group_rows), f32),
            pltpu.VMEM((2, 1, group_rows), f32),
            pltpu.VMEM((2, HD, group_rows), f32),
        ],
        compiler_params=pltpu.CompilerParams(vmem_limit_bytes=40 << 20),
        cost_estimate=pl.CostEstimate(
            flops=2 * 2 * HD * PAIRS, bytes_accessed=8 << 20, transcendentals=PAIRS
        ),
    )(info, queries, *pieces)


def attention_backward(info, queries, pieces, grads, full, total):
    return pl.pallas_call(
        backward_kernel,
        name="attention_backward",
        out_shape=(
            jax.ShapeDtypeStruct((2, group_rows, 2 * HD), f32),
            jax.ShapeDtypeStruct(CHUNKS[1:], bf16),
            jax.ShapeDtypeStruct(CHUNKS[1:], bf16),
        ),
        in_specs=[smem] + [vmem] * 4 + [anywhere] * 8,
        out_specs=[vmem] * 3,
        scratch_shapes=[
            pltpu.VMEM(CHUNKS, bf16),
            pltpu.SemaphoreType.DMA((8,)),
            pltpu.VMEM((2, HD, group_rows), bf16),
            pltpu.VMEM((2, HD, group_rows), bf16),
            pltpu.VMEM((2, 1, group_rows), f32),
            pltpu.VMEM((2, HD, group_rows), f32),
            pltpu.VMEM(CHUNKS, f32),
        ],
        compiler_params=pltpu.CompilerParams(vmem_limit_bytes=56 << 20),
        cost_estimate=pl.CostEstimate(
            flops=5 * 2 * HD * PAIRS, bytes_accessed=12 << 20, transcendentals=PAIRS
        ),
    )(info, queries, grads, full, total, *pieces)


def gather_pieces(shard, order):
    rows = shard.shape[0]
    co, zh = lax.axis_index("co"), lax.axis_index("zh")
    chunk = rows // 16
    place = co
    for link in order[::-1]:
        place = place * 2 + link_bit(link)
    mine = across(lax.dynamic_slice_in_dim(shard, place * chunk, chunk, 0), "zB")
    for link in order:
        mine = double(mine, link)
    other = across(mine, "co")
    base = (1 - zh) * rows
    return (
        (shard, zh * rows),
        (mine, base + co * (rows // 2)),
        (other, base + (1 - co) * (rows // 2)),
    )


def dot_pieces(left_op, pieces):
    total = None
    for piece, start in pieces:
        part = dot_plain(lax.dynamic_slice_in_dim(left_op, start, piece.shape[0], 1), piece)
        total = part if total is None else total + part
    return total


def dot_pieces_t(left_op, pieces):
    out = jnp.zeros((left_op.shape[0], 2 * pieces[0][0].shape[0]), f32)
    for piece, start in pieces:
        out = lax.dynamic_update_slice(out, dot_second(left_op, piece), (0, start))
    return out


GATHERS = {
    "gate": ("x0", "y0", "x1"),
    "up": ("y0", "x1", "y1"),
    "down": ("x1", "y1", "x0"),
    "out": ("y1", "x0", "y0"),
}
ORDERS = {
    "gate": ("zB", "x0", "y0", "zA", "x1", "y1"),
    "up": ("x1", "zB", "zA", "y1", "y0", "x0"),
    "out": ("zA", "y1", "zB", "x0", "x1", "y0"),
    "down": ("y0", "x1", "zB", "y1", "zA", "x0"),
}


def scatter_weight_grad(left_op, right_op, order, extra=None):
    rows = left_op.shape[1]
    depth = max(order.index("zB") + 1, 2)
    near, far = order[:depth], order[depth:]
    size = rows // 4 // 2 ** (depth - 1)
    co = lax.axis_index("co")

    def columns(side, number):
        zh, place = 0, 0
        for step, link in enumerate(near):
            bit = link_bit(link) ^ ((number >> (depth - 1 - step)) & 1)
            if link == "zB":
                zh = bit
            else:
                place = place * 2 + bit
        start = zh * (rows // 2) + side * (rows // 4) + place * size
        return lax.dynamic_slice_in_dim(left_op, start, size, 1)

    def blocks(side, numbers):
        return jnp.concatenate([columns(side, number) for number in numbers], axis=1)

    count = 2**depth

    def with_extra(array):
        return array if extra is None else jnp.concatenate([array, high_low(extra).reshape(-1, D)])

    def take_extra(got, extra):
        if extra is None:
            return got, None
        body = got.shape[0] - 2 * extra.shape[0]
        more = got[body:].astype(f32).reshape(2, *extra.shape)
        return got[:body], extra + more[0] + more[1]

    got = across(
        with_extra(dot_first(blocks(1 - co, range(count)), right_op).astype(bf16)), "co"
    )
    got, extra = take_extra(got, extra)
    middle = got.shape[0] // 2
    sent = dot_first(blocks(co, range(count // 2, count)), right_op) + got[middle:].astype(f32)
    kept = dot_first(blocks(co, range(count // 2)), right_op) + got[:middle].astype(f32)
    more = across(with_extra(sent.astype(bf16)), near[0])
    more, extra = take_extra(more, extra)
    array = (kept + more.astype(f32)).astype(bf16)
    for link in near[1:]:
        middle = array.shape[0] // 2
        more = across(with_extra(array[middle:]), link)
        more, extra = take_extra(more, extra)
        array = (array[:middle].astype(f32) + more.astype(f32)).astype(bf16)
    for link in far:
        middle = array.shape[0] // 2
        bit = link_bit(link)
        sent = lax.dynamic_slice_in_dim(array, (1 - bit) * middle, middle, 0)
        kept = lax.dynamic_slice_in_dim(array, bit * middle, middle, 0)
        more = across(with_extra(sent), link)
        more, extra = take_extra(more, extra)
        array = (kept.astype(f32) + more.astype(f32)).astype(bf16)
    return array if extra is None else (array, extra)


def place_kernel(where_ref, *refs):
    pieces, out_ref = refs[:4], refs[4]
    for number, piece in enumerate(pieces):

        @pl.when(pl.program_id(0) // 2 == number)
        def _():
            out_ref[...] = piece[0].astype(f32)


def spread_rows(chunk, order):
    links = [link for link in order if link != "zB"]
    for link in links[:1:-1]:
        chunk = double(chunk, link)
    pair = jnp.stack([chunk, across(chunk, links[1])])
    pieces = [pair, across(pair, links[0])]
    pieces += [across(piece, "co") for piece in pieces]
    co, first, second = lax.axis_index("co"), link_bit(links[0]), link_bit(links[1])
    where = jnp.stack(
        [
            ((co ^ (number >> 2)) * 2 + (first ^ ((number >> 1) & 1))) * 2
            + (second ^ (number & 1))
            for number in range(8)
        ]
    ).astype(jnp.int32)
    rows, width = chunk.shape

    def piece_spec(number):
        return pl.BlockSpec(
            (1, rows, width), lambda step, where: (jnp.clip(step - 2 * number, 0, 1), 0, 0)
        )

    return pl.pallas_call(
        place_kernel,
        name="place_rows",
        out_shape=jax.ShapeDtypeStruct((8 * rows, width), f32),
        grid_spec=pltpu.PrefetchScalarGridSpec(
            num_scalar_prefetch=1,
            grid=(8,),
            in_specs=[piece_spec(number) for number in range(4)],
            out_specs=pl.BlockSpec((rows, width), lambda step, where: (where[step], 0)),
        ),
        compiler_params=pltpu.CompilerParams(vmem_limit_bytes=32 << 20),
        cost_estimate=pl.CostEstimate(
            flops=8 * rows * width, bytes_accessed=48 * rows * width, transcendentals=0
        ),
    )(where, *pieces)


def per_device(
    tokens,
    doc_lengths,
    query_weight,
    key_weight,
    value_weight,
    out_weight,
    gate_weight,
    up_weight,
    down_weight,
    query_gain,
    key_gain,
    attn_gain,
    ffn_gain,
    cotangent,
):
    y, x, zl, co, zh = (lax.axis_index(name) for name in ("y", "x", "zl", "co", "zh"))
    head = x * 2 + zl
    lengths = doc_lengths[0]
    first_end = lengths[0]
    second_end = lengths[0] + lengths[1]
    info = jnp.stack([y, co, first_end, second_end]).astype(jnp.int32)
    source = tokens[0]

    gains = jnp.concatenate([query_gain, key_gain, attn_gain, ffn_gain])
    other_gains = across(gains, "zh")

    def whole_gain(start, size):
        own = gains[start : start + size]
        got = other_gains[start : start + size]
        return jnp.where(zh == 0, jnp.concatenate([own, got]), jnp.concatenate([got, own]))

    query_scale = lax.dynamic_slice_in_dim(whole_gain(0, 1024), head * 2 * HD, 2 * HD).astype(f32)
    key_scale = lax.dynamic_slice_in_dim(whole_gain(1024, 512), head * HD, HD).astype(f32)
    attn_scale = whole_gain(1536, 512)
    ffn_scale = whole_gain(2048, 512)

    def head_slice(which):
        return jnp.concatenate(
            [
                lax.dynamic_slice_in_dim(query_weight, which * 2 * HD, 2 * HD, 1),
                lax.dynamic_slice_in_dim(key_weight, which * HD, HD, 1),
                lax.dynamic_slice_in_dim(value_weight, which * HD, HD, 1),
            ],
            axis=1,
        )

    own_slice = head_slice(head)
    got_slice = across(own_slice, "zh")
    head_weight = jnp.where(
        zh == 0,
        jnp.concatenate([own_slice, got_slice]),
        jnp.concatenate([got_slice, own_slice]),
    )
    left_cols, right_cols = source[None, :, : D // 2], source[None, :, D // 2 :]
    for link in ("x0", "x1"):
        left_cols = double_in_place(left_cols, link)
    left_cols = double_in_place(left_cols.reshape(4, 1, BLK, D // 2), "zA", axis=1)
    right_cols = double_in_place(right_cols, "zA")[None]
    for link in ("x0", "x1"):
        right_cols = double_in_place(right_cols, link)
    group_tokens = (
        jnp.concatenate([left_cols.reshape(8, BLK, -1), right_cols.reshape(8, BLK, -1)], axis=2)
        .reshape(8, 2, half_blk, D)
        .transpose(1, 0, 2, 3)
        .reshape(2 * group_rows, D)
    )
    out_pieces = gather_pieces(out_weight, GATHERS["out"])
    gate_pieces = gather_pieces(gate_weight, GATHERS["gate"])
    up_pieces = gather_pieces(up_weight, GATHERS["up"])
    down_pieces = gather_pieces(down_weight, GATHERS["down"])

    index = jnp.arange(group_rows, dtype=jnp.int32)
    positions = jnp.concatenate(
        [half_positions(index, y, co, 0), half_positions(index, y, co, 1)]
    )
    doc_start = jnp.where(
        positions >= second_end, second_end, jnp.where(positions >= first_end, first_end, 0)
    )
    frequency = jnp.power(
        f32(rope_base), -jnp.arange(HD // 2, dtype=f32) * (2.0 / HD)
    )
    angles = (positions - doc_start).astype(f32)[:, None] * frequency[None, :]
    cosine, sine_table = jnp.cos(angles), jnp.sin(angles)

    raw = dot_plain(group_tokens, head_weight)
    query_raw, key_raw, value_raw = raw[:, : 2 * HD], raw[:, 2 * HD : 3 * HD], raw[:, 3 * HD :]
    squares = sum_over(
        jnp.stack([jnp.sum(query_raw * query_raw, axis=-1), jnp.sum(key_raw * key_raw, axis=-1)]),
        HEAD_LINKS,
    )
    query_inverse = lax.rsqrt(squares[0][:, None] / HQ + epsilon)
    key_inverse = lax.rsqrt(squares[1][:, None] / HK + epsilon)
    query_normed = query_raw * query_inverse
    key_normed = key_raw * key_inverse
    query_out = query_normed * query_scale
    queries = (
        jnp.concatenate(
            [
                rotate(query_out[:, :HD], cosine, sine_table),
                rotate(query_out[:, HD:], cosine, sine_table),
            ],
            axis=1,
        )
        * log2_scale
    ).astype(bf16)
    keys = rotate(key_normed * key_scale, cosine, sine_table).astype(bf16)
    kv = jnp.concatenate([keys, value_raw.astype(bf16)], axis=1).reshape(2, group_rows, 2 * HD)
    pieces = []
    for half, (first, second) in enumerate((("y0", "y1"), ("y1", "y0"))):
        pair = jnp.stack([kv[half], across(kv[half], first)])
        pieces += [pair, across(pair, second)]
    pieces += [across(piece, "co") for piece in pieces]
    queries = queries.reshape(2, group_rows, 2 * HD)

    attended_low, attended_full, log_total = attention_forward(info, queries, pieces)
    attended_low = (
        lax.all_to_all(attended_low, HEAD_AXES, 0, 0, tiled=True)
        .transpose(1, 2, 0, 3)
        .reshape(BLK, HQ)
    )

    mixed_out = dot_pieces(attended_low, out_pieces)
    attn_out, attn_normed, attn_inverse = rms_forward(mixed_out, attn_scale)
    hidden = source.astype(f32) + attn_out
    hidden_low = hidden.astype(bf16)
    gate_act = dot_pieces(hidden_low, gate_pieces)
    up_act = dot_pieces(hidden_low, up_pieces)
    sigmoid = jax.nn.sigmoid(gate_act)
    swish_act = gate_act * sigmoid
    inner_low = (swish_act * up_act).astype(bf16)
    down_out = dot_pieces(inner_low, down_pieces)
    ffn_out, ffn_normed, ffn_inverse = rms_forward(down_out, ffn_scale)
    output = (hidden + ffn_out).astype(bf16)

    upstream = cotangent[0].astype(f32)
    down_grad, ffn_gain_grad = rms_backward(upstream, ffn_scale, ffn_normed, ffn_inverse)
    down_low = down_grad.astype(bf16)
    inner_grad = dot_pieces_t(down_low, down_pieces)
    gate_low = (inner_grad * up_act * sigmoid * (1.0 + gate_act * (1.0 - sigmoid))).astype(bf16)
    up_low = (inner_grad * swish_act).astype(bf16)
    hidden_grad = (
        upstream + dot_pieces_t(gate_low, gate_pieces) + dot_pieces_t(up_low, up_pieces)
    )
    mixed_grad, attn_gain_grad = rms_backward(hidden_grad, attn_scale, attn_normed, attn_inverse)
    mixed_low = mixed_grad.astype(bf16)
    attended_grad = dot_pieces_t(mixed_low, out_pieces).astype(bf16)

    grads = lax.all_to_all(
        attended_grad.reshape(2, half_blk, 8, 2 * HD).transpose(2, 0, 1, 3),
        HEAD_AXES,
        0,
        0,
        tiled=True,
    )
    grads = grads.transpose(1, 0, 2, 3).reshape(2, group_rows, 2 * HD)

    gate_chunk = scatter_weight_grad(hidden_low, gate_low, ORDERS["gate"])
    up_chunk = scatter_weight_grad(hidden_low, up_low, ORDERS["up"])
    down_chunk = scatter_weight_grad(inner_low, down_low, ORDERS["down"])
    norm_gain_grads = jnp.pad(jnp.stack([attn_gain_grad, ffn_gain_grad]), ((0, 6), (0, 0)))
    out_chunk, norm_gain_grads = scatter_weight_grad(
        attended_low, mixed_low, ORDERS["out"], norm_gain_grads
    )

    query_grad, sent, kept = attention_backward(
        info, queries, pieces, grads, attended_full, log_total
    )

    got = across(sent, "co")
    parts = []
    for half, (first, second) in enumerate((("y1", "y0"), ("y0", "y1"))):
        both = kept[half].astype(f32) + got[half].astype(f32)
        more = across(both[2:].astype(bf16), first)
        both = (both[:2] + more.astype(f32)).astype(bf16)
        more = across(both[1], second)
        parts.append(both[0].astype(f32) + more.astype(f32))
    kv_grad = jnp.concatenate(parts)
    key_grad, value_grad = kv_grad[:, :HD], kv_grad[:, HD:]
    query_grad = query_grad.reshape(2 * group_rows, 2 * HD)

    back_sine = -sine_table
    key_up = rotate(key_grad, cosine, back_sine)
    query_up = jnp.concatenate(
        [
            rotate(query_grad[:, :HD], cosine, back_sine),
            rotate(query_grad[:, HD:], cosine, back_sine),
        ],
        axis=1,
    )
    query_scaled = query_up * query_scale
    key_scaled = key_up * key_scale
    means = sum_over(
        jnp.stack(
            [
                jnp.sum(query_scaled * query_normed, axis=-1),
                jnp.sum(key_scaled * key_normed, axis=-1),
            ]
        ),
        HEAD_LINKS,
    )
    query_raw_grad = query_inverse * (query_scaled - query_normed * (means[0][:, None] / HQ))
    key_raw_grad = key_inverse * (key_scaled - key_normed * (means[1][:, None] / HK))
    query_gain_grad = jnp.sum(query_up * query_normed, axis=0)
    key_gain_grad = jnp.sum(key_up * key_normed, axis=0)
    raw_low = jnp.concatenate([query_raw_grad, key_raw_grad, value_grad], axis=1).astype(bf16)

    by_owner = (
        raw_low.reshape(2, 8, half_blk, 4 * HD).transpose(1, 0, 2, 3).reshape(8, BLK, 4 * HD)
    )
    x_high, x_low = x // 2, x % 2
    halves = []
    for part in range(2):
        columns = head_weight[part * (D // 2) : (part + 1) * (D // 2)]

        def product(rows):
            return dot_second(rows.reshape(4 * BLK, 4 * HD), columns)

        if part == 0:
            sent = lax.dynamic_slice_in_dim(by_owner, (1 - x_high) * 4, 4, 0)
            kept = lax.dynamic_slice_in_dim(by_owner, x_high * 4, 4, 0)
            got = across(product(sent).astype(bf16), "x1")
            both = (product(kept) + got.astype(f32)).astype(bf16).reshape(2, 2 * BLK, D // 2)
            sent = lax.dynamic_index_in_dim(both, 1 - x_low, 0, keepdims=False)
            kept = lax.dynamic_index_in_dim(both, x_low, 0, keepdims=False)
            got = across(sent, "x0")
            both = (kept.astype(f32) + got.astype(f32)).astype(bf16).reshape(2, BLK, D // 2)
            sent = lax.dynamic_index_in_dim(both, 1 - zl, 0, keepdims=False)
            kept = lax.dynamic_index_in_dim(both, zl, 0, keepdims=False)
            got = across(sent, "zA")
        else:
            by_side = by_owner.reshape(4, 2, BLK, 4 * HD)
            sent = lax.dynamic_index_in_dim(by_side, 1 - zl, 1, keepdims=False)
            kept = lax.dynamic_index_in_dim(by_side, zl, 1, keepdims=False)
            got = across(product(sent).astype(bf16), "zA")
            both = (product(kept) + got.astype(f32)).astype(bf16).reshape(2, 2 * BLK, D // 2)
            sent = lax.dynamic_index_in_dim(both, 1 - x_high, 0, keepdims=False)
            kept = lax.dynamic_index_in_dim(both, x_high, 0, keepdims=False)
            got = across(sent, "x1")
            both = (kept.astype(f32) + got.astype(f32)).astype(bf16).reshape(2, BLK, D // 2)
            sent = lax.dynamic_index_in_dim(both, 1 - x_low, 0, keepdims=False)
            kept = lax.dynamic_index_in_dim(both, x_low, 0, keepdims=False)
            got = across(sent, "x0")
        halves.append(kept.astype(f32) + got.astype(f32))
    tokens_grad = hidden_grad + jnp.concatenate(halves, axis=1)

    def token_columns(side):
        return jnp.concatenate(
            [
                lax.dynamic_slice_in_dim(group_tokens, part * 512 + side * 256, 256, 1)
                for part in range(2)
            ],
            axis=1,
        )

    gain_sums = jnp.pad(
        jnp.concatenate([query_gain_grad, key_gain_grad])[None], ((0, 7), (0, HD))
    )

    def with_gains(array, sums):
        return jnp.concatenate([array, high_low(sums).reshape(16, 4 * HD)])

    def take_gains(got, sums):
        more = got[-16:].astype(f32).reshape(2, 8, 4 * HD)
        return got[:-16].astype(f32), sums + more[0] + more[1]

    got = across(
        with_gains(dot_first(token_columns(1 - co), raw_low).astype(bf16), gain_sums), "co"
    )
    got, gain_sums = take_gains(got, gain_sums)
    head_chunk = (dot_first(token_columns(co), raw_low) + got).astype(bf16)
    for link in ("zh", "y1", "y0"):
        middle = head_chunk.shape[0] // 2
        bit = link_bit(link)
        sent = lax.dynamic_slice_in_dim(head_chunk, (1 - bit) * middle, middle, 0)
        kept = lax.dynamic_slice_in_dim(head_chunk, bit * middle, middle, 0)
        got, gain_sums = take_gains(across(with_gains(sent, gain_sums), link), gain_sums)
        head_chunk = (kept.astype(f32) + got).astype(bf16)
    gain_rows = high_low(gain_sums).reshape(1, 16, 4 * HD)
    query_part = head_chunk[None, :, : 2 * HD]
    rest_part = head_chunk[None, :, 2 * HD :]
    for link in ("y0", "y1"):
        query_part = double(query_part, link)
    query_part = query_part.reshape(1, 256, 2 * HD)
    query_part = jnp.concatenate([query_part, gain_rows[:, :, : 2 * HD]], axis=1)
    rest_part = jnp.concatenate([rest_part, gain_rows[:, :, 2 * HD :]], axis=1)[None]
    for link in ("x0", "x1"):
        query_part = double_in_place(query_part, link)
        rest_part = double_in_place(rest_part, link)
    query_part = double_in_place(query_part[:, None], "zA", axis=1).reshape(8, 272, 2 * HD)
    rest_part = double_in_place(rest_part.reshape(4, 1, 80, 2 * HD), "zA", axis=1)
    rest_part = rest_part.reshape(8, 80, 2 * HD)
    key_gain_grad = rest_part[:, 64, :HD].astype(f32) + rest_part[:, 72, :HD].astype(f32)
    query_gain_grad = query_part[:, 256].astype(f32) + query_part[:, 264].astype(f32)
    rest_part = rest_part[None, :, :64]
    for link in ("y0", "y1"):
        rest_part = double(rest_part, link)
    query_part = query_part[:, :256].transpose(1, 0, 2).reshape(256, HQ)
    rest_part = rest_part.reshape(4, 8, 64, 2 * HD).transpose(0, 2, 1, 3).reshape(256, HQ)

    def both_cores(array):
        other = across(array, "co")
        return jnp.where(
            co == 0, jnp.concatenate([array, other]), jnp.concatenate([other, array])
        ).astype(f32)

    query_weight_grad = both_cores(query_part)
    rest_part = both_cores(rest_part).reshape(512, 8, 2, HD)
    key_weight_grad = rest_part[:, :, 0].reshape(512, HK)
    value_weight_grad = rest_part[:, :, 1].reshape(512, HK)

    out_weight_grad = spread_rows(out_chunk, ORDERS["out"])
    gate_weight_grad = spread_rows(gate_chunk, ORDERS["gate"])
    up_weight_grad = spread_rows(up_chunk, ORDERS["up"])
    down_weight_grad = spread_rows(down_chunk, ORDERS["down"])

    def own_gain(gain_grad):
        size = gain_grad.shape[0] // 2
        return lax.dynamic_slice_in_dim(gain_grad, zh * size, size)

    return (
        output[None],
        tokens_grad[None],
        query_weight_grad,
        key_weight_grad,
        value_weight_grad,
        out_weight_grad,
        gate_weight_grad,
        up_weight_grad,
        down_weight_grad,
        own_gain(query_gain_grad.reshape(HQ)),
        own_gain(key_gain_grad.reshape(HK)),
        own_gain(norm_gain_grads[0]),
        own_gain(norm_gain_grads[1]),
    )


def solution(mesh):
    fine = Mesh(mesh.devices.reshape(4, 4, 2, 2, 2), ("y", "x", "zl", "co", "zh"))
    rows = P("zh", TOKEN_AXES, None)
    weight = P("zh", None)
    gain = P("zh")
    return jax.shard_map(
        per_device,
        mesh=fine,
        in_specs=(rows, weight) + (weight,) * 7 + (gain,) * 4 + (rows,),
        out_specs=(rows, rows) + (weight,) * 7 + (gain,) * 4,
        check_vma=False,
    )
```

time: 2410 us -> 612 us (0.25)
  blocking collectives: 883 us -> 0 us
  waiting for transfers between devices: 592 us -> 138 us
  matrix products: 491 us -> 58.8 us
  starting transfers between devices: 1.3 us -> 187 us
  local copies, waits for them, and re-layouts: 232 us -> 57.1 us
  Pallas kernels: 0 us -> 85.6 us
  loops' own time: 66.1 us -> 0 us
  other arithmetic: 112 us -> 69.4 us
    psum x1 -> x0, blocking collectives: 688 us -> none  [per_device(): lax.psum((grad_shards[0], grad_shards[1], grad_shards[2], grad_shards[3],...]
    all_gather x11 -> x0, waiting for transfers between devices: 537 us -> none  [the longest x1 143 us: per_device(): lax.all_gather(key_rows, 'ctx', axis=0, tiled=True)]
    dot_general x119 -> x13, matrix products: 451 us -> 18 us  [dot_plain(): return jnp.dot(left_op, right_op, preferred_element_type=f32)]
    all_gather x6 -> x0, blocking collectives: 187 us -> none  [the longest x1 84 us: per_device(): lax.all_gather(row_delta, 'ctx', axis=0, tiled=True)]
    ppermute x0 -> x125, starting transfers between devices: none -> 178 us  [across(): return lax.ppermute(array, axis, pairs)]
    ppermute x0 -> x125, waiting for transfers between devices: none -> 137 us  [across(): return lax.ppermute(array, axis, pairs)]
    dynamic_slice x64 -> x33, local copies, waits for them, and re-layouts: 130 us -> 14.9 us  [the longest x4 5.6 us: gather_pieces(): lax.dynamic_slice_in_dim(shard, place * chunk, chunk, 0)]
    pallas_call x0 -> x6, Pallas kernels: none -> 85.6 us  [the longest x1 36.6 us: attention_backward(): pl.pallas_call(backward_kernel, name='attention_backward', out_shape=(jax...]
  transfers between devices with their start and end apart: 18 -> 127, of which waited for: 10 -> 56; matrix products, arithmetic and copies ran while one was open for 33% -> 24% of each run, Pallas kernels for 0% -> 13%
where the time goes in v1:
time: 612 us; the launch traced here: 602 us
  starting transfers between devices  187 us (31%)
  waiting for transfers between devices  138 us (23%)
  Pallas kernels  85.6 us (14%)
  other arithmetic  69.4 us (11%)
  matrix products  58.8 us (10%)
  local copies, waits for them, and re-layouts  57.1 us (9%)
    ppermute x125, starting transfers between devices, across(): return lax.ppermute(array, axis, pairs)  178 us
    ppermute x125, waiting for transfers between devices, across(): return lax.ppermute(array, axis, pairs)  137 us
    pallas_call x1, Pallas kernels, attention_backward(): pl.pallas_call(backward_kernel, name='attention_backward', out_shape=(jax...  36.6 us
    pallas_call x4, Pallas kernels, spread_rows(): pl.pallas_call(place_kernel, name='place_rows', out_shape=jax.ShapeDtypeS...  26.2 us
    pallas_call x1, Pallas kernels, attention_forward(): pl.pallas_call(forward_kernel, name='attention_forward', out_shape=(jax.S...  22.8 us
    dot_general x16, matrix products, dot_second(): lax.dot_general(left_op, right_op, (((1,), (1,)), ((), ())), preferred_el...  22.1 us
    unnamed x219, local copies, waits for them, and re-layouts  20.3 us
    dot_general x14, matrix products, dot_first(): lax.dot_general(left_op, right_op, (((0,), (0,)), ((), ())), preferred_el...  18.7 us
  transfers between devices with their start and end apart: 127, of which 56 were waited for; matrix products, arithmetic and copies ran while one was open for 24% of the time, Pallas kernels for 13%

profile of v1, /device:TPU:1, one launch (start us, length us, event | category | flops | bytes accessed | tf_op | source)
XLA Modules:
  0.0 601.9 jit_solution(8244338646741120402)
XLA Ops:
  7.5 3.3 collective-permute-start.10
  52.4 4.6 collective-permute-done.6
  57.5 8.7 %collective-permute-done.2 = bf16[4,1,128,512]{3,2,0,1:T(8,128)(2,1)S(1)} collective-permute-done((bf16[4,1,128,512]{3,2,0,1:T(8,128)(2,1)S(1)}, bf16[4,1,128,512]{3,2,0,1:T(8,128)(2,1)S(1)}, u32[]{:S(2)}, u32[]{:S(2)}) %collective-permute-start.2) | collective-permute-done | bytes 524320 | tf_op jit(solution)/shard_map/ppermute | solution.py:67
  86.8 5.0 collective-permute-done.11
  99.6 9.7 %collective-permute-start.15 = (bf16[2,512,256]{2,1,0:T(8,128)(2,1)S(1)}, bf16[2,512,256]{2,1,0:T(8,128)(2,1)S(1)}, u32[]{:S(2)}, u32[]{:S(2)}) collective-permute-start(bf16[2,512,256]{2,1,0:T(8,128)(2,1)S(1)} %pad_maximum_fusion.13.refs_0_), channel_id=1, source_target_pairs={{0,2},{2,0},{1,3},{3,1},{4,6},{6,4},{5,7},{7,5},{8,10},{10,8},{9,1... | collective-permute-start | bytes 1572872 | tf_op jit(solution)/shard_map/ppermute | solution.py:67
  119.5 22.8 %attention_forward.1 = (bf16[8,2,64,256]{3,2,1,0:T(8,128)(2,1)S(1)}, f32[2,2,128,512]{3,2,1,0:T(8,128)S(1)}, f32[2,2,1,512]{3,2,1,0:T(1,128)S(1)}) custom-call(s32[4]{0:T(128)S(1)} %pad_add_fusion.2.info_ref, bf16[2,512,256]{2,1,0:T(8,128)(2,1)S(1)} %fusion.9.query_ref, bf16[2,512,256]{2,1,0:T(8,128)(2,1)S(1)} %pad_maximum_fusion.13.refs_0_, ...), custom_call_target="tpu_custom_call" | custom-call | flops 9663676416 | bytes 8388608 | tf_op jit(solution)/shard_map/attention_forward/pallas_call | solution.py:372
  144.7 4.2 all-to-all-start
  149.0 3.9 maximum_select_fusion.3
  153.6 3.8 maximum_select_fusion.4
  206.1 4.8 all-to-all-start.1
  220.9 36.6 %attention_backward.1 = (f32[2,512,256]{2,1,0:T(8,128)}, bf16[2,4,512,256]{3,2,1,0:T(8,128)(2,1)}, bf16[2,4,512,256]{3,2,1,0:T(8,128)(2,1)}) custom-call(s32[4]{0:T(128)} %copy-done.12, bf16[2,512,256]{2,1,0:T(8,128)(2,1)} %copy-done.8, bf16[2,512,256]{2,1,0:T(8,128)(2,1)} %bitcast.413, f32[2,2,128,512]{3,2,1,0:T(8,128)} %copy-done.19, ...), custom_call_target="tpu_custom_call" | custom-call | flops 24159191040 | bytes 12582912 | tf_op jit(solution)/shard_map/attention_backward/pallas_call | solution.py:398
  273.1 10.1 %collective-permute-done.42 = bf16[2,512,256]{2,1,0:T(8,128)(2,1)S(1)} collective-permute-done((bf16[2,512,256]{2,1,0:T(8,128)(2,1)S(1)}, bf16[2,512,256]{2,1,0:T(8,128)(2,1)S(1)}, u32[]{:S(2)}, u32[]{:S(2)}) %collective-permute-start.42) | collective-permute-done | bytes 524320 | tf_op jit(solution)/shard_map/ppermute | solution.py:67
  297.6 9.7 %collective-permute-done.70 = bf16[528,1024]{1,0:T(8,128)(2,1)S(1)} collective-permute-done((bf16[528,1024]{1,0:T(8,128)(2,1)S(1)}, bf16[528,1024]{1,0:T(8,128)(2,1)S(1)}, u32[]{:S(2)}, u32[]{:S(2)}) %collective-permute-start.70) | collective-permute-done | bytes 1081376 | tf_op jit(solution)/shard_map/ppermute | solution.py:67
  322.4 7.4 %collective-permute-done.45 = f32[2,1024]{1,0:T(2,128)S(1)} collective-permute-done((f32[2,1024]{1,0:T(2,128)S(1)}, f32[2,1024]{1,0:T(2,128)S(1)}, u32[]{:S(2)}, u32[]{:S(2)}) %collective-permute-start.45) | collective-permute-done | bytes 8224 | tf_op jit(solution)/shard_map/ppermute | solution.py:67
  340.5 5.1 collective-permute-done.50
  345.5 4.8 collective-permute-start.53
  360.5 3.5 collective-permute-done.48
  369.5 3.6 collective-permute-done.52
  416.5 3.8 collective-permute-done.61
  426.1 18.6 %collective-permute-start.81 = (bf16[2,128,1024]{2,1,0:T(8,128)(2,1)S(1)}, bf16[2,128,1024]{2,1,0:T(8,128)(2,1)S(1)}, u32[]{:S(2)}, u32[]{:S(2)}) collective-permute-start(bf16[2,128,1024]{2,1,0:T(8,128)(2,1)S(1)} %pad_maximum_fusion.16.refs_0_), channel_id=1, source_target_pairs={{0,2},{2,0},{1,3},{3,1},{4,6},{6,4},{5,7},{7,5},{8,10},{10,8},{9,1... | collective-permute-start | bytes 1572872 | tf_op jit(solution)/shard_map/ppermute | solution.py:67
  454.1 5.7 collective-permute-done.86
  463.7 6.9 %collective-permute-done.114 = bf16[192,1024]{1,0:T(8,128)(2,1)S(1)} collective-permute-done((bf16[192,1024]{1,0:T(8,128)(2,1)S(1)}, bf16[192,1024]{1,0:T(8,128)(2,1)S(1)}, u32[]{:S(2)}, u32[]{:S(2)}) %collective-permute-start.114) | collective-permute-done | bytes 393248 | tf_op jit(solution)/shard_map/ppermute | solution.py:67
  511.9 3.2 collective-permute-done.93
  519.3 12.8 %collective-permute-start.68 = (bf16[256,2048]{1,0:T(8,128)(2,1)S(1)}, bf16[256,2048]{1,0:T(8,128)(2,1)S(1)}, u32[]{:S(2)}, u32[]{:S(2)}) collective-permute-start(bf16[256,2048]{1,0:T(8,128)(2,1)S(1)} %bitcast.398), channel_id=1, source_target_pairs={{0,2},{2,0},{1,3},{3,1},{4,6},{6,4},{5,7},{7,5},{8,10},{10,8},{9,1... | collective-permute-start | bytes 3145736 | tf_op jit(solution)/shard_map/ppermute | solution.py:67
  532.3 4.3 collective-permute-start.95
  541.6 4.1 place_rows.4
  547.1 5.2 collective-permute-start.123
  553.2 3.9 collective-permute-done.108.refs_1_
  560.8 5.3 copy.82
  577.5 7.1 %place_rows.5 = f32[512,3072]{1,0:T(8,128)} custom-call(s32[8]{0:T(128)S(1)} %stack.367.where_ref, bf16[2,64,3072]{2,1,0:T(8,128)(2,1)S(1)} %pad_maximum_fusion.5.refs_0_, bf16[2,64,3072]{2,1,0:T(8,128)(2,1)} %collective-permute-done.94.refs_1_, bf16[2,64,3072]{2,1,0:T(8,128)(2,1)S(1)} %copy-done.5, bf16[2,64,3072]{2,1,0:T(8,128)(2,1)} %collective-permute-done.96.refs_3_), custom_call_target="tpu_custom_call" | custom-call | flops 1572864 | bytes 9437184 | tf_op jit(solution)/shard_map/place_rows/pallas_call | solution.py:562
  584.7 7.6 %place_rows.6 = f32[512,3072]{1,0:T(8,128)} custom-call(s32[8]{0:T(128)S(1)} %stack.378.where_ref, bf16[2,64,3072]{2,1,0:T(8,128)(2,1)S(1)} %pad_maximum_fusion.6.refs_0_, bf16[2,64,3072]{2,1,0:T(8,128)(2,1)} %collective-permute-done.108.refs_1_, bf16[2,64,3072]{2,1,0:T(8,128)(2,1)} %collective-permute-done.109.refs_2_, ...), custom_call_target="tpu_custom_call" | custom-call | flops 1572864 | bytes 9437184 | tf_op jit(solution)/shard_map/place_rows/pallas_call | solution.py:562
  594.3 7.4 %place_rows.7 = f32[1536,1024]{1,0:T(8,128)} custom-call(s32[8]{0:T(128)S(1)} %stack.389.where_ref, bf16[2,192,1024]{2,1,0:T(8,128)(2,1)S(1)} %copy-done.3, bf16[2,192,1024]{2,1,0:T(8,128)(2,1)} %collective-permute-done.122.refs_1_, bf16[2,192,1024]{2,1,0:T(8,128)(2,1)S(1)} %copy-done.7, bf16[2,192,1024]{2,1,0:T(8,128)(2,1)} %collective-permute-done.124.refs_3_), custom_call_target="tpu_custom_call" | custom-call | flops 1572864 | bytes 9437184 | tf_op jit(solution)/shard_map/place_rows/pallas_call | solution.py:562
  (772 shorter events, 348.7 us)
Async XLA Ops:
  2.5 30.3 %collective-permute-start.3 = (bf16[1,128,512]{2,1,0:T(8,128)(2,1)}, bf16[1,128,512]{2,1,0:T(8,128)(2,1)}, u32[]{:S(2)}, u32[]{:S(2)}) collective-permute-start(bf16[1,128,512]{2,1,0:T(8,128)(2,1)} %get-tuple-element.153), channel_id=1, source_target_pairs={{0,4},{4,0},{1,5},{5,1},{2,6},{6,2},{3,7},{7,3},{8,12},{12,8},{9,1... | collective-permute-start | bytes 393224 | tf_op jit(solution)/shard_map/ppermute | solution.py:67
  5.0 34.4 %collective-permute-start = (bf16[1,128,512]{2,1,0:T(8,128)(2,1)S(1)}, bf16[1,128,512]{2,1,0:T(8,128)(2,1)}, u32[]{:S(2)}, u32[]{:S(2)}) collective-permute-start(bf16[1,128,512]{2,1,0:T(8,128)(2,1)S(1)} %get-tuple-element.151), channel_id=1, source_target_pairs={{0,8},{8,0},{16,24},{24,16},{1,9},{9,1},{17,25},{25,17},{2,10},{10... | collective-permute-start | bytes 393224 | tf_op jit(solution)/shard_map/ppermute | solution.py:67
  14.0 31.4 %collective-permute-start.24 = (bf16[32,3072]{1,0:T(8,128)(2,1)}, bf16[32,3072]{1,0:T(8,128)(2,1)}, u32[]{:S(2)}, u32[]{:S(2)}) collective-permute-start(bf16[32,3072]{1,0:T(8,128)(2,1)} %constant_dynamic-slice_fusion.69), channel_id=1, source_target_pairs={{0,5},{5,0},{1,4},{4,1},{2,7},{7,2},{3,6},{6,3},{8,13},{13,8},{9,1... | collective-permute-start | bytes 589832 | tf_op jit(solution)/shard_map/ppermute | solution.py:67
  45.8 26.4 %collective-permute-start.35 = (bf16[96,1024]{1,0:T(8,128)(2,1)S(1)}, bf16[96,1024]{1,0:T(8,128)(2,1)S(1)}, u32[]{:S(2)}, u32[]{:S(2)}) collective-permute-start(bf16[96,1024]{1,0:T(8,128)(2,1)S(1)} %collective-permute-done.34), channel_id=1, source_target_pairs={{8,16},{16,8},{24,0},{0,24},{9,17},{17,9},{25,1},{1,25},{10,18},{1... | collective-permute-start | bytes 589832 | tf_op jit(solution)/shard_map/ppermute | solution.py:67
  69.1 28.0 %collective-permute-start.31 = (bf16[64,3072]{1,0:T(8,128)(2,1)S(1)}, bf16[64,3072]{1,0:T(8,128)(2,1)S(1)}, u32[]{:S(2)}, u32[]{:S(2)}) collective-permute-start(bf16[64,3072]{1,0:T(8,128)(2,1)S(1)} %maximum_select_fusion.20), channel_id=1, source_target_pairs={{8,16},{16,8},{24,0},{0,24},{9,17},{17,9},{25,1},{1,25},{10,18},{1... | collective-permute-start | bytes 1179656 | tf_op jit(solution)/shard_map/ppermute | solution.py:67
  78.2 31.2 %collective-permute-start.22 = (bf16[256,1024]{1,0:T(8,128)(2,1)S(1)}, bf16[256,1024]{1,0:T(8,128)(2,1)S(1)}, u32[]{:S(2)}, u32[]{:S(2)}) collective-permute-start(bf16[256,1024]{1,0:T(8,128)(2,1)S(1)} %maximum_select_fusion.17), channel_id=1, source_target_pairs={{0,32},{32,0},{64,96},{96,64},{1,33},{33,1},{65,97},{97,65},{2,34}... | collective-permute-start | bytes 1572872 | tf_op jit(solution)/shard_map/ppermute | solution.py:67
  115.7 33.2 %collective-permute-start.32 = (bf16[128,3072]{1,0:T(8,128)(2,1)}, bf16[128,3072]{1,0:T(8,128)(2,1)}, u32[]{:S(2)}, u32[]{:S(2)}) collective-permute-start(bf16[128,3072]{1,0:T(8,128)(2,1)} %maximum_select_fusion.12), channel_id=1, source_target_pairs={{32,64},{64,32},{96,0},{0,96},{33,65},{65,33},{97,1},{1,97},{34,66... | collective-permute-start | bytes 2359304 | tf_op jit(solution)/shard_map/ppermute | solution.py:67
  118.2 35.5 %collective-permute-start.37 = (bf16[384,1024]{1,0:T(8,128)(2,1)}, bf16[384,1024]{1,0:T(8,128)(2,1)}, u32[]{:S(2)}, u32[]{:S(2)}) collective-permute-start(bf16[384,1024]{1,0:T(8,128)(2,1)} %maximum_select_fusion.13), channel_id=1, source_target_pairs={{0,8},{8,0},{16,24},{24,16},{1,9},{9,1},{17,25},{25,17},{2,10},{10... | collective-permute-start | bytes 2359304 | tf_op jit(solution)/shard_map/ppermute | solution.py:67
  118.4 43.6 %collective-permute-start.23 = (bf16[512,1024]{1,0:T(8,128)(2,1)}, bf16[512,1024]{1,0:T(8,128)(2,1)}, u32[]{:S(2)}, u32[]{:S(2)}) collective-permute-start(bf16[512,1024]{1,0:T(8,128)(2,1)} %maximum_select_fusion.9), channel_id=1, source_target_pairs={{0,2},{2,0},{1,3},{3,1},{4,6},{6,4},{5,7},{7,5},{8,10},{10,8},{9,1... | collective-permute-start | bytes 3145736 | tf_op jit(solution)/shard_map/ppermute | solution.py:67
  119.4 52.6 %collective-permute-start.28 = (bf16[256,3072]{1,0:T(8,128)(2,1)}, bf16[256,3072]{1,0:T(8,128)(2,1)}, u32[]{:S(2)}, u32[]{:S(2)}) collective-permute-start(bf16[256,3072]{1,0:T(8,128)(2,1)} %maximum_select_fusion.2), channel_id=1, source_target_pairs={{0,2},{2,0},{1,3},{3,1},{4,6},{6,4},{5,7},{7,5},{8,10},{10,8},{9,1... | collective-permute-start | bytes 4718600 | tf_op jit(solution)/shard_map/ppermute | solution.py:67
  213.3 52.0 %collective-permute-start.69 = (bf16[1040,1024]{1,0:T(8,128)(2,1)}, bf16[1040,1024]{1,0:T(8,128)(2,1)}, u32[]{:S(2)}, u32[]{:S(2)}) collective-permute-start(bf16[1040,1024]{1,0:T(8,128)(2,1)} %pad_maximum_fusion), channel_id=1, source_target_pairs={{0,2},{2,0},{1,3},{3,1},{4,6},{6,4},{5,7},{7,5},{8,10},{10,8},{9,1... | collective-permute-start | bytes 6389768 | tf_op jit(solution)/shard_map/ppermute | solution.py:67
  216.7 70.5 %collective-permute-start.83 = (bf16[512,3072]{1,0:T(8,128)(2,1)}, bf16[512,3072]{1,0:T(8,128)(2,1)}, u32[]{:S(2)}, u32[]{:S(2)}) collective-permute-start(bf16[512,3072]{1,0:T(8,128)(2,1)} %convolution_convert_fusion.1), channel_id=1, source_target_pairs={{0,2},{2,0},{1,3},{3,1},{4,6},{6,4},{5,7},{7,5},{8,10},{10,8},{9,1... | collective-permute-start | bytes 9437192 | tf_op jit(solution)/shard_map/ppermute | solution.py:67
  219.4 69.9 %collective-permute-start.97 = (bf16[512,3072]{1,0:T(8,128)(2,1)}, bf16[512,3072]{1,0:T(8,128)(2,1)}, u32[]{:S(2)}, u32[]{:S(2)}) collective-permute-start(bf16[512,3072]{1,0:T(8,128)(2,1)} %convolution_convert_fusion), channel_id=1, source_target_pairs={{0,2},{2,0},{1,3},{3,1},{4,6},{6,4},{5,7},{7,5},{8,10},{10,8},{9,1... | collective-permute-start | bytes 9437192 | tf_op jit(solution)/shard_map/ppermute | solution.py:67
  262.6 31.9 %collective-permute-start.111 = (bf16[1536,1024]{1,0:T(8,128)(2,1)S(1)}, bf16[1536,1024]{1,0:T(8,128)(2,1)S(1)}, u32[]{:S(2)}, u32[]{:S(2)}) collective-permute-start(bf16[1536,1024]{1,0:T(8,128)(2,1)S(1)} %convolution_convert_fusion.2), channel_id=1, source_target_pairs={{0,2},{2,0},{1,3},{3,1},{4,6},{6,4},{5,7},{7,5},{8,10},{10,8},{9,1... | collective-permute-start | bytes 9437192 | tf_op jit(solution)/shard_map/ppermute | solution.py:67
  285.1 25.1 %collective-permute-start.43 = (bf16[512,256]{1,0:T(8,128)(2,1)S(1)}, bf16[512,256]{1,0:T(8,128)(2,1)S(1)}, u32[]{:S(2)}, u32[]{:S(2)}) collective-permute-start(bf16[512,256]{1,0:T(8,128)(2,1)S(1)} %slice_bitcast_fusion.4), channel_id=1, source_target_pairs={{32,64},{64,32},{96,0},{0,96},{33,65},{65,33},{97,1},{1,97},{34,66... | collective-permute-start | bytes 786440 | tf_op jit(solution)/shard_map/ppermute | solution.py:67
  287.2 25.0 %collective-permute-start.41 = (bf16[512,256]{1,0:T(8,128)(2,1)S(1)}, bf16[512,256]{1,0:T(8,128)(2,1)S(1)}, u32[]{:S(2)}, u32[]{:S(2)}) collective-permute-start(bf16[512,256]{1,0:T(8,128)(2,1)S(1)} %slice_bitcast_fusion.6), channel_id=1, source_target_pairs={{0,32},{32,0},{64,96},{96,64},{1,33},{33,1},{65,97},{97,65},{2,34}... | collective-permute-start | bytes 786440 | tf_op jit(solution)/shard_map/ppermute | solution.py:67
  289.4 113.5 %collective-permute-start.84 = (bf16[256,3072]{1,0:T(8,128)(2,1)S(1)}, bf16[256,3072]{1,0:T(8,128)(2,1)S(1)}, u32[]{:S(2)}, u32[]{:S(2)}) collective-permute-start(bf16[256,3072]{1,0:T(8,128)(2,1)S(1)} %add_convert_fusion.5), channel_id=1, source_target_pairs={{0,5},{5,0},{1,4},{4,1},{2,7},{7,2},{3,6},{6,3},{8,13},{13,8},{9,1... | collective-permute-start | bytes 4718600 | tf_op jit(solution)/shard_map/ppermute | solution.py:67
  294.5 111.6 %collective-permute-start.98 = (bf16[256,3072]{1,0:T(8,128)(2,1)S(1)}, bf16[256,3072]{1,0:T(8,128)(2,1)S(1)}, u32[]{:S(2)}, u32[]{:S(2)}) collective-permute-start(bf16[256,3072]{1,0:T(8,128)(2,1)S(1)} %add_convert_fusion.3), channel_id=1, source_target_pairs={{8,16},{16,8},{24,0},{0,24},{9,17},{17,9},{25,1},{1,25},{10,18},{1... | collective-permute-start | bytes 4718600 | tf_op jit(solution)/shard_map/ppermute | solution.py:67
  307.3 104.3 %collective-permute-start.112 = (bf16[768,1024]{1,0:T(8,128)(2,1)S(1)}, bf16[768,1024]{1,0:T(8,128)(2,1)S(1)}, u32[]{:S(2)}, u32[]{:S(2)}) collective-permute-start(bf16[768,1024]{1,0:T(8,128)(2,1)S(1)} %add_convert_fusion.1), channel_id=1, source_target_pairs={{0,32},{32,0},{64,96},{96,64},{1,33},{33,1},{65,97},{97,65},{2,34}... | collective-permute-start | bytes 4718600 | tf_op jit(solution)/shard_map/ppermute | solution.py:67
  310.2 27.2 %collective-permute-start.71 = (bf16[272,1024]{1,0:T(8,128)(2,1)S(1)}, bf16[272,1024]{1,0:T(8,128)(2,1)S(1)}, u32[]{:S(2)}, u32[]{:S(2)}) collective-permute-start(bf16[272,1024]{1,0:T(8,128)(2,1)S(1)} %pad_maximum_fusion.8), channel_id=1, source_target_pairs={{32,64},{64,32},{96,0},{0,96},{33,65},{65,33},{97,1},{1,97},{34,66... | collective-permute-start | bytes 1671176 | tf_op jit(solution)/shard_map/ppermute | solution.py:67
  406.0 41.1 %collective-permute-start.85 = (bf16[128,3072]{1,0:T(8,128)(2,1)}, bf16[128,3072]{1,0:T(8,128)(2,1)}, u32[]{:S(2)}, u32[]{:S(2)}) collective-permute-start(bf16[128,3072]{1,0:T(8,128)(2,1)} %slice.651), channel_id=1, source_target_pairs={{0,8},{8,0},{16,24},{24,16},{1,9},{9,1},{17,25},{25,17},{2,10},{10... | collective-permute-start | bytes 2359304 | tf_op jit(solution)/shard_map/ppermute | solution.py:67
  409.4 39.9 %collective-permute-start.99 = (bf16[128,3072]{1,0:T(8,128)(2,1)}, bf16[128,3072]{1,0:T(8,128)(2,1)}, u32[]{:S(2)}, u32[]{:S(2)}) collective-permute-start(bf16[128,3072]{1,0:T(8,128)(2,1)} %slice.655), channel_id=1, source_target_pairs={{0,5},{5,0},{1,4},{4,1},{2,7},{7,2},{3,6},{6,3},{8,13},{13,8},{9,1... | collective-permute-start | bytes 2359304 | tf_op jit(solution)/shard_map/ppermute | solution.py:67
  411.6 33.2 %collective-permute-start.67 = (bf16[2,8,64,256]{3,2,1,0:T(8,128)(2,1)S(1)}, bf16[2,8,64,256]{3,2,1,0:T(8,128)(2,1)}, u32[]{:S(2)}, u32[]{:S(2)}) collective-permute-start(bf16[2,8,64,256]{3,2,1,0:T(8,128)(2,1)S(1)} %maximum_select_fusion.18), channel_id=1, source_target_pairs={{32,64},{64,32},{96,0},{0,96},{33,65},{65,33},{97,1},{1,97},{34,66... | collective-permute-start | bytes 1572872 | tf_op jit(solution)/shard_map/ppermute | solution.py:67
  420.3 30.5 %collective-permute-start.113 = (bf16[384,1024]{1,0:T(8,128)(2,1)}, bf16[384,1024]{1,0:T(8,128)(2,1)}, u32[]{:S(2)}, u32[]{:S(2)}) collective-permute-start(bf16[384,1024]{1,0:T(8,128)(2,1)} %slice.659), channel_id=1, source_target_pairs={{8,16},{16,8},{24,0},{0,24},{9,17},{17,9},{25,1},{1,25},{10,18},{1... | collective-permute-start | bytes 2359304 | tf_op jit(solution)/shard_map/ppermute | solution.py:67
  426.1 106.2 %collective-permute-start.81 = (bf16[2,128,1024]{2,1,0:T(8,128)(2,1)S(1)}, bf16[2,128,1024]{2,1,0:T(8,128)(2,1)S(1)}, u32[]{:S(2)}, u32[]{:S(2)}) collective-permute-start(bf16[2,128,1024]{2,1,0:T(8,128)(2,1)S(1)} %pad_maximum_fusion.16.refs_0_), channel_id=1, source_target_pairs={{0,2},{2,0},{1,3},{3,1},{4,6},{6,4},{5,7},{7,5},{8,10},{10,8},{9,1... | collective-permute-start | bytes 1572872 | tf_op jit(solution)/shard_map/ppermute | solution.py:67
  444.8 91.9 %collective-permute-start.82 = (bf16[2,128,1024]{2,1,0:T(8,128)(2,1)S(1)}, bf16[2,128,1024]{2,1,0:T(8,128)(2,1)S(1)}, u32[]{:S(2)}, u32[]{:S(2)}) collective-permute-start(bf16[2,128,1024]{2,1,0:T(8,128)(2,1)S(1)} %collective-permute-done.80.refs_1_), channel_id=1, source_target_pairs={{0,2},{2,0},{1,3},{3,1},{4,6},{6,4},{5,7},{7,5},{8,10},{10,8},{9,1... | collective-permute-start | bytes 1572872 | tf_op jit(solution)/shard_map/ppermute | solution.py:67
  447.4 90.2 %collective-permute-start.62 = (bf16[256,2048]{0,1:T(8,128)(2,1)S(1)}, bf16[256,2048]{0,1:T(8,128)(2,1)S(1)}, u32[]{:S(2)}, u32[]{:S(2)}) collective-permute-start(bf16[256,2048]{0,1:T(8,128)(2,1)S(1)} %bitcast.371), channel_id=1, source_target_pairs={{0,2},{2,0},{1,3},{3,1},{4,6},{6,4},{5,7},{7,5},{8,10},{10,8},{9,1... | collective-permute-start | bytes 3145736 | tf_op jit(solution)/shard_map/ppermute | solution.py:67
  519.3 26.4 %collective-permute-start.68 = (bf16[256,2048]{1,0:T(8,128)(2,1)S(1)}, bf16[256,2048]{1,0:T(8,128)(2,1)S(1)}, u32[]{:S(2)}, u32[]{:S(2)}) collective-permute-start(bf16[256,2048]{1,0:T(8,128)(2,1)S(1)} %bitcast.398), channel_id=1, source_target_pairs={{0,2},{2,0},{1,3},{3,1},{4,6},{6,4},{5,7},{7,5},{8,10},{10,8},{9,1... | collective-permute-start | bytes 3145736 | tf_op jit(solution)/shard_map/ppermute | solution.py:67
  545.7 39.0 %collective-permute-start.109 = (bf16[2,64,3072]{2,1,0:T(8,128)(2,1)S(1)}, bf16[2,64,3072]{2,1,0:T(8,128)(2,1)}, u32[]{:S(2)}, u32[]{:S(2)}) collective-permute-start(bf16[2,64,3072]{2,1,0:T(8,128)(2,1)S(1)} %pad_maximum_fusion.6.refs_0_), channel_id=1, source_target_pairs={{0,2},{2,0},{1,3},{3,1},{4,6},{6,4},{5,7},{7,5},{8,10},{10,8},{9,1... | collective-permute-start | bytes 2359304 | tf_op jit(solution)/shard_map/ppermute | solution.py:67
  547.1 45.1 %collective-permute-start.123 = (bf16[2,192,1024]{2,1,0:T(8,128)(2,1)S(1)}, bf16[2,192,1024]{2,1,0:T(8,128)(2,1)S(1)}, u32[]{:S(2)}, u32[]{:S(2)}) collective-permute-start(bf16[2,192,1024]{2,1,0:T(8,128)(2,1)S(1)} %pad_maximum_fusion.7.refs_0_), channel_id=1, source_target_pairs={{0,2},{2,0},{1,3},{3,1},{4,6},{6,4},{5,7},{7,5},{8,10},{10,8},{9,1... | collective-permute-start | bytes 2359304 | tf_op jit(solution)/shard_map/ppermute | solution.py:67
  557.1 27.6 %collective-permute-start.110 = (bf16[2,64,3072]{2,1,0:T(8,128)(2,1)}, bf16[2,64,3072]{2,1,0:T(8,128)(2,1)}, u32[]{:S(2)}, u32[]{:S(2)}) collective-permute-start(bf16[2,64,3072]{2,1,0:T(8,128)(2,1)} %collective-permute-done.108.refs_1_), channel_id=1, source_target_pairs={{0,2},{2,0},{1,3},{3,1},{4,6},{6,4},{5,7},{7,5},{8,10},{10,8},{9,1... | collective-permute-start | bytes 2359304 | tf_op jit(solution)/shard_map/ppermute | solution.py:67
  557.9 35.2 %collective-permute-start.124 = (bf16[2,192,1024]{2,1,0:T(8,128)(2,1)}, bf16[2,192,1024]{2,1,0:T(8,128)(2,1)}, u32[]{:S(2)}, u32[]{:S(2)}) collective-permute-start(bf16[2,192,1024]{2,1,0:T(8,128)(2,1)} %collective-permute-done.122.refs_1_), channel_id=1, source_target_pairs={{0,2},{2,0},{1,3},{3,1},{4,6},{6,4},{5,7},{7,5},{8,10},{10,8},{9,1... | collective-permute-start | bytes 2359304 | tf_op jit(solution)/shard_map/ppermute | solution.py:67
  (198 other events, 1744.8 us)

commit v2 on v1

v2 whole, which is shorter than its diff:
```python
import functools
import math

import jax
import jax.numpy as jnp
from jax import lax
from jax.experimental import pallas as pl
from jax.experimental.pallas import tpu as pltpu
from jax.sharding import Mesh
from jax.sharding import PartitionSpec as P

D = 1024
HEADS = 16
KVH = 8
HD = 128
FF = 3072
BLK = 128
HQ = 2048
HK = 1024
SEQ = 8192

epsilon = 1e-06
rope_base = 1000000.0
masked_score = -1e30
score_scale = HD**-0.5
log2_scale = score_scale * math.log2(math.e)
half_blk = BLK // 2
group_rows = 8 * half_blk

bf16 = jnp.bfloat16
f32 = jnp.float32

TOKEN_AXES = ("y", "x", "zl", "co")
HEAD_AXES = ("x", "zl")

edge_a = [(0, 1), (1, 0), (2, 3), (3, 2)]
edge_b = [(1, 2), (2, 1), (3, 0), (0, 3)]
swap = [(0, 1), (1, 0)]
LINKS = {
    "x0": ("x", edge_a),
    "x1": ("x", edge_b),
    "y0": ("y", edge_a),
    "y1": ("y", edge_b),
    "zA": ("zl", swap),
    "zB": (("zl", "zh"), [(0, 3), (3, 0), (1, 2), (2, 1)]),
    "co": ("co", swap),
    "zh": ("zh", swap),
}


def link_bit(link):
    if link in ("x0", "y0"):
        place = lax.axis_index(link[0])
        return ((place == 1) | (place == 2)).astype(jnp.int32)
    if link in ("x1", "y1"):
        return (lax.axis_index(link[0]) >= 2).astype(jnp.int32)
    if link == "zA":
        return lax.axis_index("zl") ^ lax.axis_index("zh")
    if link == "zB":
        return lax.axis_index("zh")
    return lax.axis_index(link)


def across(array, link):
    axis, pairs = LINKS[link]
    return lax.ppermute(array, axis, pairs)


def dot_plain(left_op, right_op):
    return jnp.dot(left_op, right_op, preferred_element_type=f32)


def dot_second(left_op, right_op):
    return lax.dot_general(
        left_op, right_op, (((1,), (1,)), ((), ())), preferred_element_type=f32
    )


def dot_first(left_op, right_op):
    return lax.dot_general(
        left_op, right_op, (((0,), (0,)), ((), ())), preferred_element_type=f32
    )


def exchange(array, axes):
    return lax.all_to_all(array, axes, 0, 0, tiled=True)


def gather_all(array, axes, count):
    return exchange(jnp.broadcast_to(array[None], (count, *array.shape)), axes)


def high_low(values):
    high = values.astype(bf16)
    return jnp.stack([high, (values - high.astype(f32)).astype(bf16)])


def half_positions(index, y, co, half):
    block = 16 * y + 2 * (index // half_blk) + co
    inner = index % half_blk
    return jnp.where(half == 0, block * half_blk + inner, SEQ - (block + 1) * half_blk + inner)


def query_masks(info_ref, half):
    y, co, first_end, second_end = info_ref[0], info_ref[1], info_ref[2], info_ref[3]
    index = lax.broadcasted_iota(jnp.int32, (1, group_rows), 1)
    position = half_positions(index, y, co, half)
    start = jnp.where(position >= second_end, second_end, 0)
    start = jnp.where((position >= first_end) & (position < second_end), first_end, start)
    return position, start, position >= second_end


def pair_mask(group, key_half, query_pos, query_start):
    index = lax.broadcasted_iota(jnp.int32, (group_rows, 1), 0)
    key_pos = half_positions(index, group // 2, group % 2, key_half)
    return (key_pos >= query_start) & (key_pos <= query_pos)


def open_steps(y, half):
    count = jnp.where(half == 0, jnp.maximum(2 * y - 2, 0), 6 + 6 - 2 * y)

    def chunk(step):
        late = step >= 6
        group = jnp.where(late, step - 6 + 2 * y + 2, step + 2)
        return group, jnp.where(late, 1, 0)

    return count, chunk


def masked_steps(y, half):
    count = jnp.where((half == 0) & (y == 0), 2, 4)

    def chunk(step):
        own = step >= 2
        group = jnp.where(own, 2 * y + step - 2, step)
        return group, jnp.where(own, half, 0)

    return count, chunk


def slot_of(group, key_half, y, co):
    other_y = group // 2
    beside, over = other_y == (y ^ 1), other_y == 3 - y
    first = jnp.where(key_half == 0, beside, over)
    second = jnp.where(key_half == 0, over, beside)
    ring = jnp.where(other_y == y, 0, jnp.where(first, 1, jnp.where(second, 2, 3)))
    return (group % 2) ^ co, key_half, ring


def load_chunks(pieces, kvs, sems):
    copies = []
    for number, piece in enumerate(pieces):
        core, half, pair = number // 4, number // 2 % 2, number % 2
        target = kvs.at[core, half, pl.ds(2 * pair, 2)]
        copies.append(pltpu.make_async_copy(piece, target, sems.at[number]))
    for copy in copies:
        copy.start()
    return copies


def forward_kernel(info_ref, query_ref, *refs):
    pieces, (low_ref, full_ref, total_ref), (kvs, sems, qt, top, denom, acc) = (
        refs[:8],
        refs[8:11],
        refs[11:],
    )
    y, co = info_ref[0], info_ref[1]
    for copy in load_chunks(pieces, kvs, sems):
        copy.wait()

    def half_body(half, carry):
        query_pos, query_start, last_doc = query_masks(info_ref, half)
        for head in range(2):
            lanes = slice(head * HD, (head + 1) * HD)
            qt[head] = query_ref[half, :, lanes].astype(f32).T.astype(bf16)
            top[head] = jnp.full((1, group_rows), masked_score, f32)
            denom[head] = jnp.zeros((1, group_rows), f32)
            acc[head] = jnp.zeros((HD, group_rows), f32)

        def step(group, key_half, masked):
            slot = slot_of(group, key_half, y, co)
            keys = kvs[(*slot, slice(None), slice(0, HD))]
            values = kvs[(*slot, slice(None), slice(HD, 2 * HD))]
            if masked:
                mask = pair_mask(group, key_half, query_pos, query_start)
            for head in range(2):
                scores = dot_plain(keys, qt[head])
                if masked:
                    scores = jnp.where(mask, scores, masked_score)
                old_top = top[head]
                new_top = jnp.maximum(old_top, jnp.max(scores, axis=0, keepdims=True))
                weights = jnp.exp2(scores - new_top)
                rescale = jnp.exp2(old_top - new_top)
                denom[head] = denom[head] * rescale + jnp.sum(weights, axis=0, keepdims=True)
                acc[head] = acc[head] * rescale + dot_first(values, weights.astype(bf16))
                top[head] = new_top

        count, chunk = open_steps(y, half)

        def open_body(number, inner):
            step(*chunk(number), False)
            return inner

        lax.fori_loop(0, count, open_body, 0)
        for head in range(2):
            top[head] = jnp.where(last_doc, masked_score, top[head])
            denom[head] = jnp.where(last_doc, 0.0, denom[head])
            acc[head] = jnp.where(last_doc, 0.0, acc[head])
        masked_count, masked_chunk = masked_steps(y, half)

        def masked_body(number, inner):
            step(*masked_chunk(number), True)
            return inner

        lax.fori_loop(0, masked_count, masked_body, 0)
        for head in range(2):
            lanes = slice(head * HD, (head + 1) * HD)
            attended = acc[head] / denom[head]
            full_ref[half, head] = attended
            total_ref[half, head] = top[head] + jnp.log2(denom[head])
            rows = attended.T.astype(bf16)
            for owner in range(8):
                low_ref[owner, half, :, lanes] = rows[owner * half_blk : (owner + 1) * half_blk]
        return carry

    lax.fori_loop(0, 2, half_body, 0)


def backward_kernel(info_ref, query_ref, grad_ref, full_ref, total_ref, *refs):
    pieces, (dq_ref, sent_hbm, kept_hbm), (kvs, sems, qt, gt, delta, dqt, dkv) = (
        refs[:8],
        refs[8:11],
        refs[11:],
    )
    y, co = info_ref[0], info_ref[1]

    def grads_of(half, lanes):
        return grad_ref[:, half, :, lanes].reshape(group_rows, HD)

    copies = load_chunks(pieces, kvs, sems)
    dkv[...] = jnp.zeros_like(dkv)
    for copy in copies:
        copy.wait()

    def half_body(half, carry):
        query_pos, query_start, last_doc = query_masks(info_ref, half)
        for head in range(2):
            lanes = slice(head * HD, (head + 1) * HD)
            qt[head] = query_ref[half, :, lanes].astype(f32).T.astype(bf16)
            grad_t = grads_of(half, lanes).astype(f32).T
            gt[head] = grad_t.astype(bf16)
            delta[head] = jnp.sum(grad_t * full_ref[half, head], axis=0, keepdims=True)
            dqt[head] = jnp.zeros((HD, group_rows), f32)

        def step(group, key_half, masked):
            slot = slot_of(group, key_half, y, co)
            key_lanes = (*slot, slice(None), slice(0, HD))
            value_lanes = (*slot, slice(None), slice(HD, 2 * HD))
            keys = kvs[key_lanes]
            values = kvs[value_lanes]
            if masked:
                mask = pair_mask(group, key_half, query_pos, query_start)
            key_total = dkv[key_lanes]
            value_total = dkv[value_lanes]
            for head in range(2):
                lanes = slice(head * HD, (head + 1) * HD)
                scores = dot_plain(keys, qt[head])
                total = total_ref[half, head]
                if masked:
                    scores = jnp.where(mask, scores, masked_score)
                else:
                    total = jnp.where(last_doc, -masked_score, total)
                probs = jnp.exp2(scores - total)
                value_total += dot_plain(probs.astype(bf16), grads_of(half, lanes))
                prob_grad = dot_plain(values, gt[head])
                low = (probs * (prob_grad - delta[head])).astype(bf16)
                key_total += dot_plain(low, query_ref[half, :, lanes])
                dqt[head] += dot_first(keys, low)
            dkv[key_lanes] = key_total
            dkv[value_lanes] = value_total

        count, chunk = open_steps(y, half)

        def open_body(number, inner):
            step(*chunk(number), False)
            return inner

        lax.fori_loop(0, count, open_body, 0)
        masked_count, masked_chunk = masked_steps(y, half)

        def masked_body(number, inner):
            step(*masked_chunk(number), True)
            return inner

        lax.fori_loop(0, masked_count, masked_body, 0)
        for head in range(2):
            lanes = slice(head * HD, (head + 1) * HD)
            dq_ref[half, :, lanes] = dqt[head].T * score_scale
        return carry

    lax.fori_loop(0, 2, half_body, 0)

    def store(core):
        def store_body(number, carry):
            half, ring = number // 4, number % 4
            rows = (core, half, ring)
            kvs[(*rows, slice(None), slice(0, HD))] = (
                dkv[(*rows, slice(None), slice(0, HD))] * math.log(2.0)
            ).astype(bf16)
            kvs[(*rows, slice(None), slice(HD, 2 * HD))] = dkv[
                (*rows, slice(None), slice(HD, 2 * HD))
            ].astype(bf16)
            return carry

        lax.fori_loop(0, 8, store_body, 0)

    stores = [
        pltpu.make_async_copy(kvs.at[1], sent_hbm, sems.at[0]),
        pltpu.make_async_copy(kvs.at[0], kept_hbm, sems.at[1]),
    ]
    store(1)
    stores[0].start()
    store(0)
    stores[1].start()
    for copy in stores:
        copy.wait()


smem = pl.BlockSpec(memory_space=pltpu.SMEM)
vmem = pl.BlockSpec(memory_space=pltpu.VMEM)
hbm = pl.BlockSpec(memory_space=pltpu.HBM)


def in_hbm(*arrays):
    return [pltpu.with_memory_space_constraint(array, pltpu.HBM) for array in arrays]


PAIRS = 4 * 2 * group_rows * 9 * group_rows
CHUNKS = (2, 2, 4, group_rows, 2 * HD)


def attention_forward(info, queries, pieces):
    return pl.pallas_call(
        forward_kernel,
        name="attention_forward",
        out_shape=(
            jax.ShapeDtypeStruct((8, 2, half_blk, 2 * HD), bf16),
            jax.ShapeDtypeStruct((2, 2, HD, group_rows), f32),
            jax.ShapeDtypeStruct((2, 2, 1, group_rows), f32),
        ),
        in_specs=[smem, vmem] + [hbm] * 8,
        out_specs=[vmem] * 3,
        scratch_shapes=[
            pltpu.VMEM(CHUNKS, bf16),
            pltpu.SemaphoreType.DMA((8,)),
            pltpu.VMEM((2, HD, group_rows), bf16),
            pltpu.VMEM((2, 1, group_rows), f32),
            pltpu.VMEM((2, 1, group_rows), f32),
            pltpu.VMEM((2, HD, group_rows), f32),
        ],
        compiler_params=pltpu.CompilerParams(vmem_limit_bytes=24 << 20),
        cost_estimate=pl.CostEstimate(
            flops=2 * 2 * HD * PAIRS, bytes_accessed=8 << 20, transcendentals=PAIRS
        ),
    )(info, queries, *in_hbm(*pieces))


def attention_backward(info, queries, pieces, grads, full, total):
    return pl.pallas_call(
        backward_kernel,
        name="attention_backward",
        out_shape=(
            jax.ShapeDtypeStruct((2, group_rows, 2 * HD), f32),
            pltpu.HBM((2, 4, group_rows, 2 * HD), bf16),
            pltpu.HBM((2, 4, group_rows, 2 * HD), bf16),
        ),
        in_specs=[smem] + [vmem] * 4 + [hbm] * 8,
        out_specs=[vmem, hbm, hbm],
        scratch_shapes=[
            pltpu.VMEM(CHUNKS, bf16),
            pltpu.SemaphoreType.DMA((8,)),
            pltpu.VMEM((2, HD, group_rows), bf16),
            pltpu.VMEM((2, HD, group_rows), bf16),
            pltpu.VMEM((2, 1, group_rows), f32),
            pltpu.VMEM((2, HD, group_rows), f32),
            pltpu.VMEM(CHUNKS, f32),
        ],
        compiler_params=pltpu.CompilerParams(vmem_limit_bytes=36 << 20),
        cost_estimate=pl.CostEstimate(
            flops=5 * 2 * HD * PAIRS, bytes_accessed=12 << 20, transcendentals=PAIRS
        ),
    )(info, queries, grads, full, total, *in_hbm(*pieces))


OUT_ROWS, GATE_ROWS, DOWN_ROWS = HQ // 64, D // 64, FF // 64
BLOCKS = FF // D
GATE_AT = OUT_ROWS
UP_AT = GATE_AT + BLOCKS * GATE_ROWS
DOWN_AT = UP_AT + BLOCKS * GATE_ROWS
CHUNK_ROWS = DOWN_AT + DOWN_ROWS


def run_copies(copies):
    for copy in copies:
        copy.start()
    for copy in copies:
        copy.wait()


def collect_kernel(
    info_ref, query_ref, key_ref, value_ref, out_ref, gate_ref, up_ref, down_ref, gain_ref,
    own_ref, sent_ref, chunk_ref, sems,
):
    place = info_ref[0]
    numbers = iter(range(15))
    copies = []

    def copy(source, target):
        copies.append(pltpu.make_async_copy(source, target, sems.at[next(numbers)]))

    for target, head in ((sent_ref, info_ref[2]), (own_ref, info_ref[1])):
        lanes = pl.ds(pl.multiple_of(head * 2 * HD, 2 * HD), 2 * HD)
        copy(query_ref.at[:, lanes], target.at[:, pl.ds(0, 2 * HD)])
        lanes = pl.ds(pl.multiple_of(head * HD, HD), HD)
        copy(key_ref.at[:, lanes], target.at[:, pl.ds(2 * HD, HD)])
        copy(value_ref.at[:, lanes], target.at[:, pl.ds(3 * HD, HD)])
    copy(out_ref.at[place], chunk_ref.at[pl.ds(0, OUT_ROWS)])
    copy(down_ref.at[place], chunk_ref.at[pl.ds(DOWN_AT, DOWN_ROWS)])
    copy(gain_ref, chunk_ref.at[pl.ds(CHUNK_ROWS, 16)])
    for ref, start in ((gate_ref, GATE_AT), (up_ref, UP_AT)):
        for block in range(BLOCKS):
            copy(
                ref.at[place, :, pl.ds(block * D, D)],
                chunk_ref.at[pl.ds(start + block * GATE_ROWS, GATE_ROWS)],
            )
    run_copies(copies)


def collect(info, projections, shards, gains):
    gain_rows = jnp.pad(gains, (0, 16 * D - gains.shape[0])).reshape(16, D)
    return pl.pallas_call(
        collect_kernel,
        name="collect_chunk",
        out_shape=(
            jax.ShapeDtypeStruct((D // 2, 4 * HD), bf16),
            jax.ShapeDtypeStruct((D // 2, 4 * HD), bf16),
            jax.ShapeDtypeStruct((CHUNK_ROWS + 16, D), bf16),
        ),
        in_specs=[smem] + [hbm] * 8,
        out_specs=[vmem] * 3,
        scratch_shapes=[pltpu.SemaphoreType.DMA((15,))],
        compiler_params=pltpu.CompilerParams(vmem_limit_bytes=60 << 20),
    )(info, *in_hbm(*projections, *shards, gain_rows))


ROWS = 2 * group_rows


def as_lanes(column):
    return jnp.broadcast_to(column, (ROWS, HD)).T[0:1]


def as_rows(row):
    return jnp.broadcast_to(row, (HD, ROWS)).T


def turn(tensor, cosine, sine):
    return tensor * cosine + pltpu.roll(tensor, HD // 2, 1) * sine


def project_kernel(info_ref, tokens_ref, own_ref, got_ref, raw_ref, weight_ref, squares_ref):
    zh = info_ref[0]
    weight_ref[pl.ds(pl.multiple_of(zh * (D // 2), D // 2), D // 2)] = own_ref[...]
    weight_ref[pl.ds(pl.multiple_of((1 - zh) * (D // 2), D // 2), D // 2)] = got_ref[...]
    for owner in range(8):
        raw = dot_plain(tokens_ref[owner], weight_ref[...])
        for half in range(2):
            start = half * group_rows + owner * half_blk
            raw_ref[start : start + half_blk] = raw[half * half_blk : (half + 1) * half_blk]
    raw = raw_ref[:, : 3 * HD]
    squares = raw * raw
    query = jnp.sum(squares[:, :HD] + squares[:, HD : 2 * HD], axis=1, keepdims=True)
    key = jnp.sum(squares[:, 2 * HD :], axis=1, keepdims=True)
    sums = jnp.concatenate([as_lanes(query), as_lanes(key)])
    for owner in range(8):
        squares_ref[owner] = sums


def project(info, tokens, own_slice, got_slice):
    return pl.pallas_call(
        project_kernel,
        name="project",
        out_shape=(
            jax.ShapeDtypeStruct((ROWS, 4 * HD), f32),
            jax.ShapeDtypeStruct((D, 4 * HD), bf16),
            jax.ShapeDtypeStruct((8, 2, ROWS), f32),
        ),
        in_specs=[smem] + [vmem] * 3,
        out_specs=[vmem] * 3,
        compiler_params=pltpu.CompilerParams(vmem_limit_bytes=32 << 20),
        cost_estimate=pl.CostEstimate(
            flops=2 * ROWS * D * 4 * HD, bytes_accessed=6 << 20, transcendentals=0
        ),
    )(info, tokens, own_slice, got_slice)


def inverses(squares_ref):
    total = jnp.sum(squares_ref[...], axis=0)
    return (
        as_rows(lax.rsqrt(total[0:1] / HQ + epsilon)),
        as_rows(lax.rsqrt(total[1:2] / HK + epsilon)),
    )


def prepare_kernel(raw_ref, squares_ref, cos_ref, sin_ref, gain_ref, query_ref, kv_ref):
    query_inverse, key_inverse = inverses(squares_ref)
    cosine, sine = cos_ref[...], sin_ref[...]
    for head in range(3):
        lanes = slice(head * HD, (head + 1) * HD)
        inverse = query_inverse if head < 2 else key_inverse
        turned = turn(raw_ref[:, lanes] * inverse * gain_ref[:, lanes], cosine, sine)
        if head < 2:
            turned = (turned * log2_scale).astype(bf16)
            query_ref[0, :, lanes] = turned[:group_rows]
            query_ref[1, :, lanes] = turned[group_rows:]
        else:
            turned = turned.astype(bf16)
            values = raw_ref[:, 3 * HD :].astype(bf16)
            for half in range(2):
                rows = slice(half * group_rows, (half + 1) * group_rows)
                kv_ref[half, :, :HD] = turned[rows]
                kv_ref[half, :, HD:] = values[rows]


def prepare(raw, squares, tables, gain):
    return pl.pallas_call(
        prepare_kernel,
        name="prepare",
        out_shape=(
            jax.ShapeDtypeStruct((2, group_rows, 2 * HD), bf16),
            jax.ShapeDtypeStruct((2, group_rows, 2 * HD), bf16),
        ),
        in_specs=[vmem] * 5,
        out_specs=[vmem] * 2,
        compiler_params=pltpu.CompilerParams(vmem_limit_bytes=32 << 20),
        cost_estimate=pl.CostEstimate(flops=8 << 20, bytes_accessed=6 << 20, transcendentals=0),
    )(raw, squares, *tables, gain)


def turned_back(raw_ref, squares_ref, cos_ref, sin_ref, dq_ref, dkv_ref):
    query_inverse, key_inverse = inverses(squares_ref)
    cosine, sine = cos_ref[...], -sin_ref[...]
    for head in range(3):
        lanes = slice(head * HD, (head + 1) * HD)
        inverse = query_inverse if head < 2 else key_inverse
        grad = dq_ref[:, lanes] if head < 2 else dkv_ref[:, :HD]
        yield head, lanes, turn(grad, cosine, sine), raw_ref[:, lanes] * inverse, inverse


def means_kernel(raw_ref, squares_ref, cos_ref, sin_ref, gain_ref, dq_ref, dkv_ref, means_ref):
    products = []
    for _, lanes, upstream, normed, _ in turned_back(
        raw_ref, squares_ref, cos_ref, sin_ref, dq_ref, dkv_ref
    ):
        products.append(upstream * gain_ref[:, lanes] * normed)
    query = jnp.sum(products[0] + products[1], axis=1, keepdims=True)
    key = jnp.sum(products[2], axis=1, keepdims=True)
    means_ref[...] = jnp.concatenate([as_lanes(query), as_lanes(key)])


def raw_grad_kernel(
    raw_ref, squares_ref, cos_ref, sin_ref, gain_ref, dq_ref, dkv_ref, means_ref,
    low_ref, gain_grad_ref,
):
    means = (as_rows(means_ref[0:1]) / HQ, as_rows(means_ref[1:2]) / HK)

    def place(lanes, low):
        for owner in range(8):
            for half in range(2):
                start = half * group_rows + owner * half_blk
                low_ref[owner, half * half_blk : (half + 1) * half_blk, lanes] = low[
                    start : start + half_blk
                ]

    for head, lanes, upstream, normed, inverse in turned_back(
        raw_ref, squares_ref, cos_ref, sin_ref, dq_ref, dkv_ref
    ):
        mean = means[0] if head < 2 else means[1]
        place(lanes, (inverse * (upstream * gain_ref[:, lanes] - normed * mean)).astype(bf16))
        gain_grad_ref[:, lanes] = jnp.sum(upstream * normed, axis=0, keepdims=True)
    place(slice(3 * HD, 4 * HD), dkv_ref[:, HD:].astype(bf16))
    gain_grad_ref[:, 3 * HD :] = jnp.zeros((1, HD), f32)


def projection_means(*operands):
    return pl.pallas_call(
        means_kernel,
        name="projection_means",
        out_shape=jax.ShapeDtypeStruct((2, ROWS), f32),
        in_specs=[vmem] * 7,
        out_specs=vmem,
        compiler_params=pltpu.CompilerParams(vmem_limit_bytes=32 << 20),
        cost_estimate=pl.CostEstimate(flops=8 << 20, bytes_accessed=6 << 20, transcendentals=0),
    )(*operands)


def projection_grads(*operands):
    return pl.pallas_call(
        raw_grad_kernel,
        name="projection_grads",
        out_shape=(
            jax.ShapeDtypeStruct((8, BLK, 4 * HD), bf16),
            jax.ShapeDtypeStruct((1, 4 * HD), f32),
        ),
        in_specs=[vmem] * 8,
        out_specs=[vmem] * 2,
        compiler_params=pltpu.CompilerParams(vmem_limit_bytes=32 << 20),
        cost_estimate=pl.CostEstimate(flops=8 << 20, bytes_accessed=6 << 20, transcendentals=0),
    )(*operands)


INNER_AT = 0
DOWN_LOW_AT = INNER_AT + FF // 2
ATT_AT = DOWN_LOW_AT + D
HIDDEN_AT = ATT_AT + HQ // 2
GATE_LOW_AT = HIDDEN_AT + D
UP_LOW_AT = GATE_LOW_AT + FF // 2
MIXED_LOW_AT = UP_LOW_AT + FF // 2
PACK = MIXED_LOW_AT + D


def rows_kernel(
    info_ref, att_ref, tokens_ref, cot_ref, attn_gain_ref, ffn_gain_ref,
    out_own, gate_own, up_own, down_own, mine, other,
    output_ref, own_hbm, sent_hbm, att_grad_ref, hidden_grad_ref, gain_grad_ref,
    own_ref, sent_ref, out_v, gate_v, up_v, down_v, gate_act, up_act, inner_ref, hidden_ref, down_out, sems,
):
    zh, co = info_ref[0], info_ref[1]
    numbers = iter(range(22))

    def copy(source, target):
        return pltpu.make_async_copy(source, target, sems.at[next(numbers)])

    def pieces(own, rows_at, rows, scratch, blocks):
        copies = [copy(own, scratch.at[pl.ds(zh * 32, 32)])]
        for half, core in ((mine, co), (other, 1 - co)):
            at = (1 - zh) * 32 + core * 16
            for block in range(blocks):
                target = scratch.at[pl.ds(at, 16)]
                if blocks > 1:
                    target = scratch.at[pl.ds(at, 16), :, pl.ds(block * D, D)]
                copies.append(
                    copy(half.at[:, pl.ds(rows_at + block * rows, rows), :], target)
                )
        return copies

    out_copies = pieces(out_own, 0, OUT_ROWS, out_v, 1)
    gate_copies = pieces(gate_own, GATE_AT, GATE_ROWS, gate_v, BLOCKS)
    up_copies = pieces(up_own, UP_AT, GATE_ROWS, up_v, BLOCKS)
    down_copies = pieces(down_own, DOWN_AT, DOWN_ROWS, down_v, 1)
    for item in out_copies + gate_copies + up_copies + down_copies:
        item.start()

    def put(core, lanes, value):
        @pl.when(core == co)
        def _():
            own_ref[:, lanes] = value

        @pl.when(core != co)
        def _():
            sent_ref[:, lanes] = value

    def put_both(start, value):
        own_ref[:, start : start + D] = value
        sent_ref[:, start : start + D] = value

    for item in out_copies:
        item.wait()
    hidden_grad_ref[...] = jnp.zeros((BLK, D), f32)

    def mixed_body(head, carry):
        rows = att_ref[head].reshape(BLK, 2 * HD)
        column = (head // 4) * 2 + head % 2
        put((head // 2) % 2, pl.ds(pl.multiple_of(ATT_AT + column * 2 * HD, HD), 2 * HD), rows)
        hidden_grad_ref[...] += dot_plain(rows, out_v[pl.ds(head * 8, 8)].reshape(2 * HD, D))
        return carry

    lax.fori_loop(0, 8, mixed_body, 0)
    attn_gain = attn_gain_ref[...]
    mixed = hidden_grad_ref[...]
    attn_inverse = lax.rsqrt(jnp.mean(mixed * mixed, axis=-1, keepdims=True) + epsilon)
    hidden = tokens_ref[...].astype(f32) + mixed * attn_inverse * attn_gain
    hidden_ref[...] = hidden
    put_both(HIDDEN_AT, hidden.astype(bf16))
    for item in gate_copies + up_copies:
        item.wait()
    tile = 8 * DOWN_ROWS

    def act_body(step, carry):
        lanes = pl.ds(step * tile, tile)
        low = own_ref[:, HIDDEN_AT : HIDDEN_AT + D]
        gate = dot_plain(low, gate_v[:, :, lanes].reshape(D, tile))
        up = dot_plain(low, up_v[:, :, lanes].reshape(D, tile))
        gate_act[:, lanes] = gate
        up_act[:, lanes] = up
        inner = (gate * (1.0 / (1.0 + jnp.exp(-gate))) * up).astype(bf16)
        inner_ref[:, lanes] = inner
        column = (step // 4) * 2 + step % 2
        put((step // 2) % 2, pl.ds(pl.multiple_of(INNER_AT + column * tile, HD), tile), inner)
        return carry

    lax.fori_loop(0, FF // tile, act_body, 0)
    for item in down_copies:
        item.wait()
    down_out[...] = jnp.zeros((BLK, D), f32)

    def down_body(step, carry):
        rows = down_v[pl.ds(step * 8, 8)].reshape(tile, D)
        down_out[...] += dot_plain(inner_ref[:, pl.ds(step * tile, tile)], rows)
        return carry

    lax.fori_loop(0, FF // tile, down_body, 0)
    ffn_gain = ffn_gain_ref[...]
    down = down_out[...]
    ffn_inverse = lax.rsqrt(jnp.mean(down * down, axis=-1, keepdims=True) + epsilon)
    normed = down * ffn_inverse
    output_ref[...] = (hidden_ref[...] + normed * ffn_gain).astype(bf16)
    upstream = cot_ref[...].astype(f32)
    scaled = upstream * ffn_gain
    gain_grad_ref[1:2, :] = jnp.sum(upstream * normed, axis=0, keepdims=True)
    down_low = ffn_inverse * (scaled - normed * jnp.mean(scaled * normed, axis=-1, keepdims=True))
    put_both(DOWN_LOW_AT, down_low.astype(bf16))
    down_out[...] = upstream

    def back_body(step, carry):
        lanes = pl.ds(step * tile, tile)
        rows = down_v[pl.ds(step * 8, 8)].reshape(tile, D)
        inner_grad = dot_second(own_ref[:, DOWN_LOW_AT : DOWN_LOW_AT + D], rows)
        gate, up = gate_act[:, lanes], up_act[:, lanes]
        sigmoid = 1.0 / (1.0 + jnp.exp(-gate))
        gate_low = (inner_grad * up * sigmoid * (1.0 + gate * (1.0 - sigmoid))).astype(bf16)
        up_low = (inner_grad * (gate * sigmoid)).astype(bf16)
        column = (step % 4) * tile
        put(step // 4, pl.ds(pl.multiple_of(GATE_LOW_AT + column, HD), tile), gate_low)
        put(step // 4, pl.ds(pl.multiple_of(UP_LOW_AT + column, HD), tile), up_low)
        down_out[...] += dot_second(gate_low, gate_v[:, :, lanes].reshape(D, tile)) + dot_second(
            up_low, up_v[:, :, lanes].reshape(D, tile)
        )
        return carry

    lax.fori_loop(0, FF // tile, back_body, 0)
    mixed = hidden_grad_ref[...]
    attn_inverse = lax.rsqrt(jnp.mean(mixed * mixed, axis=-1, keepdims=True) + epsilon)
    normed = mixed * attn_inverse
    hidden_grad = down_out[...]
    scaled = hidden_grad * attn_gain_ref[...]
    gain_grad_ref[0:1, :] = jnp.sum(hidden_grad * normed, axis=0, keepdims=True)
    mixed_low = (
        attn_inverse * (scaled - normed * jnp.mean(scaled * normed, axis=-1, keepdims=True))
    ).astype(bf16)
    put_both(MIXED_LOW_AT, mixed_low)
    packs = [copy(sent_ref, sent_hbm), copy(own_ref, own_hbm)]
    for item in packs:
        item.start()
    hidden_grad_ref[...] = hidden_grad

    def grad_body(head, carry):
        rows = out_v[pl.ds(head * 8, 8)].reshape(2 * HD, D)
        mixed_low = own_ref[:, MIXED_LOW_AT : MIXED_LOW_AT + D]
        grad = dot_second(mixed_low, rows).astype(bf16)
        att_grad_ref[head] = grad.reshape(2, half_blk, 2 * HD)
        return carry

    lax.fori_loop(0, 8, grad_body, 0)
    for item in packs:
        item.wait()


def own_rows(info, attended, tokens, cotangent, attn_gain, ffn_gain, shards, mine, other):
    def shape(*dims, dtype=bf16):
        return jax.ShapeDtypeStruct(dims, dtype)

    return pl.pallas_call(
        rows_kernel,
        name="own_rows",
        out_shape=(
            shape(BLK, D),
            pltpu.HBM((BLK, PACK), bf16),
            pltpu.HBM((BLK, PACK), bf16),
            shape(8, 2, half_blk, 2 * HD),
            shape(BLK, D, dtype=f32),
            shape(2, D, dtype=f32),
        ),
        in_specs=[smem] + [vmem] * 5 + [hbm] * 6,
        out_specs=[vmem, hbm, hbm, vmem, vmem, vmem],
        scratch_shapes=[
            pltpu.VMEM((BLK, PACK), bf16),
            pltpu.VMEM((BLK, PACK), bf16),
            pltpu.VMEM((64, OUT_ROWS, D), bf16),
            pltpu.VMEM((64, GATE_ROWS, FF), bf16),
            pltpu.VMEM((64, GATE_ROWS, FF), bf16),
            pltpu.VMEM((64, DOWN_ROWS, D), bf16),
            pltpu.VMEM((BLK, FF), f32),
            pltpu.VMEM((BLK, FF), f32),
            pltpu.VMEM((BLK, FF), bf16),
            pltpu.VMEM((BLK, D), f32),
            pltpu.VMEM((BLK, D), f32),
            pltpu.SemaphoreType.DMA((22,)),
        ],
        compiler_params=pltpu.CompilerParams(vmem_limit_bytes=44 << 20),
        cost_estimate=pl.CostEstimate(
            flops=4 * BLK * (3 * D * FF + HQ * D),
            bytes_accessed=26 << 20,
            transcendentals=2 * BLK * FF,
        ),
    )(info, attended, tokens, cotangent, attn_gain, ffn_gain, *in_hbm(*shards, mine, other))


def wide_rows(array):
    return jnp.concatenate(
        [array[:, start : start + D] for start in range(0, array.shape[1], D)]
    )


def ring_place(bits):
    return bits[0] * 2 + (bits[0] ^ bits[1])


PRODUCTS = (
    (FF // 2, INNER_AT, D, DOWN_LOW_AT, "y", "01"),
    (D, HIDDEN_AT, FF // 2, GATE_LOW_AT, "x", "01"),
    (D, HIDDEN_AT, FF // 2, UP_LOW_AT, "x", "10"),
    (HQ // 2, ATT_AT, D, MIXED_LOW_AT, "y", "10"),
)


def products_kernel(places_ref, own_ref, got_ref, *refs):
    outs, (both, left, sems), scratch = refs[:8], refs[8:11], refs[11:]
    run_copies(
        [
            pltpu.make_async_copy(ref, both.at[pl.ds(core * BLK, BLK)], sems.at[8 + core])
            for core, ref in enumerate((own_ref, got_ref))
        ]
    )
    copies = [
        pltpu.make_async_copy(held, out, sems.at[number])
        for number, (held, out) in enumerate(zip(scratch, outs))
    ]
    held = None
    for number, (rows, left_at, width, right_at, _, _) in enumerate(PRODUCTS):
        if left_at != held:
            left[:rows] = both[:, left_at : left_at + rows].astype(f32).T.astype(bf16)
            held = left_at
        quarter = rows // 8
        for part in range(2):
            out = scratch[2 * number + part]

            def body(step, carry):
                place = places_ref[number * 4 + part * 2 + step // 2]
                start = pl.multiple_of(((step % 2) * 4 + place) * quarter, quarter)
                target = pl.ds(pl.multiple_of(step * quarter, quarter), quarter)
                out[target] = dot_plain(
                    left[pl.ds(start, quarter)], both[:, right_at : right_at + width]
                ).astype(bf16)
                return carry

            lax.fori_loop(0, 4, body, 0)
            copies[2 * number + part].start()
    for copy in copies:
        copy.wait()


def weight_products(own, got):
    places = []
    for _, _, _, _, axis, order in PRODUCTS:
        for first, second in ((1, 0), (1, 1), (0, 0), (0, 1)):
            bits = {name: link_bit(axis + name) for name in "01"}
            bits[order[0]] = bits[order[0]] ^ first
            bits[order[1]] = bits[order[1]] ^ second
            places.append(ring_place((bits["1"], bits["0"])))
    flops = sum(2 * 2 * BLK * rows * width for rows, _, width, _, _, _ in PRODUCTS)
    return pl.pallas_call(
        products_kernel,
        name="weight_products",
        out_shape=[
            pltpu.HBM((rows // 2, width), bf16)
            for rows, _, width, _, _, _ in PRODUCTS
            for _ in range(2)
        ],
        in_specs=[smem, hbm, hbm],
        out_specs=[hbm] * 8,
        scratch_shapes=[
            pltpu.VMEM((2 * BLK, PACK), bf16),
            pltpu.VMEM((FF // 2, 2 * BLK), bf16),
            pltpu.SemaphoreType.DMA((10,)),
        ]
        + [
            pltpu.VMEM((rows // 2, width), bf16)
            for rows, _, width, _, _, _ in PRODUCTS
            for _ in range(2)
        ],
        compiler_params=pltpu.CompilerParams(vmem_limit_bytes=40 << 20),
        cost_estimate=pl.CostEstimate(flops=flops, bytes_accessed=16 << 20, transcendentals=0),
    )(jnp.stack(places).astype(jnp.int32), *in_hbm(own, got))


def place_kernel(core_ref, chunk_ref, *refs):
    gate_ref, up_ref, down_ref, out_ref = refs[-4:]
    for y in range(4):
        for zl in range(2):
            chunk = chunk_ref[y, 0, zl]
            start = (2 * y + zl) * GATE_ROWS
            rows = slice(start, start + GATE_ROWS)
            gate_ref[rows, :D] = chunk[:16].astype(f32)
            gate_ref[rows, D:] = chunk[16:32, : D // 2].astype(f32)
            up_ref[rows, : D // 2] = chunk[16:32, D // 2 :].astype(f32)
            up_ref[rows, D // 2 :] = chunk[32:48].astype(f32)
            down_ref[y, 24 * zl : 24 * zl + 24] = chunk[48:72].astype(f32)
            out_ref[y, 16 * zl : 16 * zl + 16] = chunk[72:].astype(f32)


def place_rows(core, chunks, earlier):
    def columns(x, core):
        return (x, core[0])

    def rows(x, core):
        return (core[0], x, 0)

    return pl.pallas_call(
        place_kernel,
        name="place_rows",
        out_shape=(
            jax.ShapeDtypeStruct((D // 2, FF), f32),
            jax.ShapeDtypeStruct((D // 2, FF), f32),
            jax.ShapeDtypeStruct((8, 4 * 48, D), f32),
            jax.ShapeDtypeStruct((8, 4 * 32, D), f32),
        ),
        grid_spec=pltpu.PrefetchScalarGridSpec(
            num_scalar_prefetch=1,
            grid=(4,),
            in_specs=[pl.BlockSpec((4, 1, 2, 88, D), lambda x, core: (0, x, 0, 0, 0))]
            + [hbm] * len(earlier),
            out_specs=[
                pl.BlockSpec((D // 8, FF // 2), columns),
                pl.BlockSpec((D // 8, FF // 2), columns),
                pl.BlockSpec((4, 48, D), rows),
                pl.BlockSpec((4, 32, D), rows),
            ],
        ),
        input_output_aliases={2 + number: number for number in range(len(earlier))},
        compiler_params=pltpu.CompilerParams(vmem_limit_bytes=32 << 20),
        cost_estimate=pl.CostEstimate(flops=3 << 20, bytes_accessed=18 << 20, transcendentals=0),
    )(core, chunks, *earlier)


def place_heads_kernel(core_ref, chunk_ref, *refs):
    query_ref, key_ref, value_ref = refs[-3:]
    for owner in range(8):
        part = chunk_ref[0, owner, :64].astype(f32)
        query_ref[:, owner * 2 * HD : (owner + 1) * 2 * HD] = part[:, : 2 * HD]
        key_ref[:, owner * HD : (owner + 1) * HD] = part[:, 2 * HD : 3 * HD]
        value_ref[:, owner * HD : (owner + 1) * HD] = part[:, 3 * HD :]


def place_heads(core, chunks, earlier):
    def rows(y, core):
        return (core[0] * 4 + y, 0)

    return pl.pallas_call(
        place_heads_kernel,
        name="place_heads",
        out_shape=(
            jax.ShapeDtypeStruct((D // 2, HQ), f32),
            jax.ShapeDtypeStruct((D // 2, HK), f32),
            jax.ShapeDtypeStruct((D // 2, HK), f32),
        ),
        grid_spec=pltpu.PrefetchScalarGridSpec(
            num_scalar_prefetch=1,
            grid=(4,),
            in_specs=[pl.BlockSpec((1, 8, 80, 4 * HD), lambda y, core: (y, 0, 0, 0))]
            + [hbm] * len(earlier),
            out_specs=[
                pl.BlockSpec((64, HQ), rows),
                pl.BlockSpec((64, HK), rows),
                pl.BlockSpec((64, HK), rows),
            ],
        ),
        input_output_aliases={2 + number: number for number in range(len(earlier))},
        compiler_params=pltpu.CompilerParams(vmem_limit_bytes=32 << 20),
        cost_estimate=pl.CostEstimate(flops=1 << 20, bytes_accessed=6 << 20, transcendentals=0),
    )(core, chunks, *earlier)


def per_device(
    tokens,
    doc_lengths,
    query_weight,
    key_weight,
    value_weight,
    out_weight,
    gate_weight,
    up_weight,
    down_weight,
    query_gain,
    key_gain,
    attn_gain,
    ffn_gain,
    cotangent,
):
    y, x, zl, co, zh = (lax.axis_index(name) for name in ("y", "x", "zl", "co", "zh"))
    head = x * 2 + zl
    lengths = doc_lengths[0]
    first_end = lengths[0]
    second_end = lengths[0] + lengths[1]
    info = jnp.stack([y, co, first_end, second_end]).astype(jnp.int32)
    source = tokens[0]

    gains = jnp.concatenate([query_gain, key_gain, attn_gain, ffn_gain])
    shards = (
        out_weight.reshape(32, OUT_ROWS, D),
        gate_weight.reshape(32, GATE_ROWS, FF),
        up_weight.reshape(32, GATE_ROWS, FF),
        down_weight.reshape(32, DOWN_ROWS, D),
    )
    group_tokens = jnp.broadcast_to(source[None], (8, BLK, D))
    places = jnp.stack([co * 16 + y * 4 + x, head, x * 2 + 1 - zl]).astype(jnp.int32)
    group_tokens, places = lax.optimization_barrier((group_tokens, places))
    own_slice, sent_slice, weight_chunk = collect(
        places,
        (query_weight, key_weight, value_weight),
        shards,
        gains,
    )
    got_slice = across(sent_slice, "zB")
    weight_chunk = across(weight_chunk, "zB")
    group_tokens = exchange(group_tokens, HEAD_AXES)
    mine_weights = lax.all_gather(weight_chunk[:CHUNK_ROWS], ("y", "x"), axis=0, tiled=False)
    other_gains = weight_chunk[CHUNK_ROWS:].reshape(-1)[: gains.shape[0]]

    def whole_gain(start, size):
        own = gains[start : start + size]
        got = other_gains[start : start + size]
        return jnp.where(zh == 0, jnp.concatenate([own, got]), jnp.concatenate([got, own]))

    query_scale = lax.dynamic_slice_in_dim(whole_gain(0, 1024), head * 2 * HD, 2 * HD).astype(f32)
    key_scale = lax.dynamic_slice_in_dim(whole_gain(1024, 512), head * HD, HD).astype(f32)
    attn_scale = whole_gain(1536, 512)
    ffn_scale = whole_gain(2048, 512)

    head_gain = jnp.concatenate([query_scale, key_scale])[None]

    index = jnp.arange(group_rows, dtype=jnp.int32)
    positions = jnp.concatenate(
        [half_positions(index, y, co, 0), half_positions(index, y, co, 1)]
    )
    doc_start = jnp.where(
        positions >= second_end, second_end, jnp.where(positions >= first_end, first_end, 0)
    )
    frequency = jnp.power(
        f32(rope_base), -jnp.arange(HD // 2, dtype=f32) * (2.0 / HD)
    )
    angles = (positions - doc_start).astype(f32)[:, None] * frequency[None, :]
    cosine, sine_table = jnp.cos(angles), jnp.sin(angles)
    tables = (
        jnp.concatenate([cosine, cosine], axis=1),
        jnp.concatenate([-sine_table, sine_table], axis=1),
    )

    raw, head_weight, squares = project(
        zh[None].astype(jnp.int32), group_tokens, own_slice, got_slice
    )
    squares = exchange(squares, HEAD_AXES)
    queries, kv = prepare(raw, squares, tables, head_gain)
    pairs = [
        jnp.stack([kv[half], across(kv[half], first)]) for half, first in enumerate(("y0", "y1"))
    ]
    pieces = [
        piece
        for pair, second in zip(pairs, ("y1", "y0"))
        for piece in (pair, across(pair, second))
    ]
    pieces += [across(piece, "co") for piece in pieces]
    pieces, mine_weights = lax.optimization_barrier((pieces, mine_weights))
    other_weights = across(mine_weights, "co")

    attended_low, attended_full, log_total = attention_forward(info, queries, pieces)
    attended_low = exchange(attended_low, HEAD_AXES)
    (
        output,
        own_pack,
        sent_pack,
        attended_grad,
        hidden_grad,
        norm_gain_grads,
    ) = own_rows(
        jnp.stack([zh, co]).astype(jnp.int32),
        attended_low,
        source,
        cotangent[0],
        attn_scale.astype(f32)[None],
        ffn_scale.astype(f32)[None],
        shards,
        mine_weights,
        other_weights,
    )

    grads = exchange(attended_grad, HEAD_AXES)

    products = weight_products(own_pack, across(sent_pack, "co"))
    sent_parts, rest_parts = products[0::2], products[1::2]
    grads, sent_parts = lax.optimization_barrier((grads, sent_parts))
    got_parts = [
        across(sent, axis + order[0])
        for sent, (_, _, _, _, axis, order) in zip(sent_parts, PRODUCTS)
    ]

    query_grad, sent, kept = attention_backward(
        info, queries, pieces, grads, attended_full, log_total
    )
    stage = lax.optimization_barrier
    own_core, other_core = co[None].astype(jnp.int32), (1 - co)[None].astype(jnp.int32)

    sent, got_parts = stage((sent, got_parts))
    got = across(sent, "co")
    second_sent = [
        (rest[rest.shape[0] // 2 :].astype(f32) + part[rest.shape[0] // 2 :].astype(f32)).astype(
            bf16
        )
        for rest, part in zip(rest_parts, got_parts)
    ]
    got, second_sent = stage((got, second_sent))
    orders = (("y1", "y0"), ("y0", "y1"))
    kv_got = [
        across((kept[half, 2:].astype(f32) + got[half, 2:].astype(f32)).astype(bf16), first)
        for half, (first, _) in enumerate(orders)
    ]
    second_got = [
        across(part, axis + order[1])
        for part, (_, _, _, _, axis, order) in zip(second_sent, PRODUCTS)
    ]

    def second_sum(number):
        rest, part = rest_parts[number], got_parts[number]
        middle = rest.shape[0] // 2
        kept_part = rest[:middle].astype(f32) + part[:middle].astype(f32)
        return (kept_part + second_got[number].astype(f32)).astype(bf16)

    kv_got, second_got[1], second_got[2] = stage((kv_got, second_got[1], second_got[2]))
    kv_both = [
        kept[half, :2].astype(f32) + got[half, :2].astype(f32) + kv_got[half].astype(f32)
        for half in range(2)
    ]
    kv_got = [
        across(kv_both[half][1].astype(bf16), second) for half, (_, second) in enumerate(orders)
    ]
    act_part = exchange(
        jnp.concatenate([second_sum(1), second_sum(2)], axis=1).reshape(16, 16, FF),
        ("zh", "y", "zl"),
    )
    kv_got, act_part, second_got[0], second_got[3] = stage(
        (kv_got, act_part, second_got[0], second_got[3])
    )
    rest_part = exchange(
        jnp.concatenate(
            [second_sum(0).reshape(16, 24, D), second_sum(3).reshape(16, 16, D)], axis=1
        ),
        ("zh", "x", "zl"),
    )
    kv_grad = jnp.concatenate(
        [both[0] + more.astype(f32) for both, more in zip(kv_both, kv_got)]
    )
    operands = (
        raw, squares, *tables, head_gain, query_grad.reshape(ROWS, 2 * HD), kv_grad,
    )
    means = projection_means(*operands)
    for link in ("x0", "x1", "zA"):
        means = means + across(means, link)
    act_part = wide_rows(jnp.sum(act_part.astype(f32), axis=0).astype(bf16))
    means, rest_part = stage((means, rest_part))
    chunk = jnp.concatenate([act_part, jnp.sum(rest_part.astype(f32), axis=0).astype(bf16)])
    chunk_got = across(chunk, "zA")
    chunk = jnp.where(zl == 0, jnp.stack([chunk, chunk_got]), jnp.stack([chunk_got, chunk]))
    chunks = lax.all_gather(chunk, ("y", "x"), axis=0, tiled=False).reshape(4, 4, 2, 88, D)
    by_owner, head_gain_grad = projection_grads(*operands, means)
    raw_low = by_owner.reshape(ROWS, 4 * HD)
    group_tokens = group_tokens.reshape(ROWS, D)

    def token_columns(side):
        return jnp.concatenate(
            [
                lax.dynamic_slice_in_dim(group_tokens, part * 512 + side * 256, 256, 1)
                for part in range(2)
            ],
            axis=1,
        )

    gain_sums = jnp.concatenate(
        [
            head_gain_grad,
            norm_gain_grads.reshape(4, 4 * HD),
            jnp.zeros((3, 4 * HD), f32),
        ]
    )
    by_side = by_owner.reshape(4, 2, BLK, 4 * HD)
    x_high, x_low = x // 2, x % 2

    def product(rows, part):
        columns = head_weight[part * (D // 2) : (part + 1) * (D // 2)]
        return dot_second(rows.reshape(4 * BLK, 4 * HD), columns)

    def pick(array, number):
        return lax.dynamic_index_in_dim(array, number, 0, keepdims=False)

    def pass_on(both, link, number):
        return pick(both, number).astype(f32), across(pick(both, 1 - number), link)

    def halves(both):
        return both.astype(bf16).reshape(2, both.shape[0] // 2, D // 2)

    heads_got = across(
        jnp.concatenate(
            [
                dot_first(token_columns(1 - co), raw_low).astype(bf16),
                high_low(gain_sums).reshape(16, 4 * HD),
            ]
        ),
        "co",
    )
    left_sent = product(lax.dynamic_slice_in_dim(by_owner, (1 - x_high) * 4, 4, 0), 0)
    left_got = across(left_sent.astype(bf16), "x1")
    right_sent = product(lax.dynamic_index_in_dim(by_side, 1 - zl, 1, keepdims=False), 1)
    right_got = across(right_sent.astype(bf16), "zA")
    head_chunk = dot_first(token_columns(co), raw_low)
    left = product(lax.dynamic_slice_in_dim(by_owner, x_high * 4, 4, 0), 0)
    right = product(lax.dynamic_index_in_dim(by_side, zl, 1, keepdims=False), 1)
    heads_got, left_got, right_got, head_chunk, left, right = stage(
        (heads_got, left_got, right_got, head_chunk, left, right)
    )
    heads_got = heads_got.astype(f32)
    gain_sums = gain_sums + heads_got[512:520] + heads_got[520:]
    head_chunk = jnp.concatenate(
        [
            (head_chunk + heads_got[:512]).astype(bf16).reshape(8, 64, 4 * HD),
            jnp.broadcast_to(high_low(gain_sums).reshape(1, 16, 4 * HD), (8, 16, 4 * HD)),
        ],
        axis=1,
    )
    head_chunk = exchange(head_chunk, ("zh", "y"))
    left, left_got = pass_on(halves(left + left_got.astype(f32)), "x0", x_low)
    right, right_got = pass_on(halves(right + right_got.astype(f32)), "x1", x_high)
    head_chunk, left_got, right_got = stage((head_chunk, left_got, right_got))
    head_chunk = jnp.sum(head_chunk.astype(f32), axis=0)
    gain_sums = head_chunk[64:72] + head_chunk[72:]
    head_chunk = jnp.concatenate(
        [head_chunk[:64].astype(bf16), high_low(gain_sums).reshape(16, 4 * HD)]
    )
    mine = gather_all(head_chunk, ("y", "x", "zl"), 32)
    left, left_got = pass_on(halves(left + left_got.astype(f32)), "zA", zl)
    right, right_got = pass_on(halves(right + right_got.astype(f32)), "x0", x_low)
    mine, left_got, right_got = stage((mine, left_got, right_got))
    tokens_grad = hidden_grad + jnp.concatenate(
        [left + left_got.astype(f32), right + right_got.astype(f32)], axis=1
    )

    mine = mine.reshape(4, 8, 80, 4 * HD)
    other_heads = across(mine, "co")
    placed_heads = place_heads(own_core, mine, ())
    query_weight_grad, key_weight_grad, value_weight_grad = place_heads(
        other_core, other_heads, placed_heads
    )
    gain_sums = mine[0, :, 64:72].astype(f32) + mine[0, :, 72:].astype(f32)
    query_gain_grad = gain_sums[:, 0, : 2 * HD].reshape(HQ)
    key_gain_grad = gain_sums[:, 0, 2 * HD : 3 * HD].reshape(HK)
    norm_gain_grads = jnp.sum(gain_sums[:, 1:5], axis=0).reshape(2, D)
    chunks, query_weight_grad, tokens_grad = stage((chunks, query_weight_grad, tokens_grad))
    placed = place_rows(own_core, chunks, ())
    gate_weight_grad, up_weight_grad, down_weight_grad, out_weight_grad = place_rows(
        other_core, across(chunks, "co"), placed
    )
    down_weight_grad = down_weight_grad.reshape(FF // 2, D)
    out_weight_grad = out_weight_grad.reshape(HQ // 2, D)

    def own_gain(gain_grad):
        size = gain_grad.shape[0] // 2
        return lax.dynamic_slice_in_dim(gain_grad, zh * size, size)

    return (
        output[None],
        tokens_grad[None],
        query_weight_grad,
        key_weight_grad,
        value_weight_grad,
        out_weight_grad,
        gate_weight_grad,
        up_weight_grad,
        down_weight_grad,
        own_gain(query_gain_grad.reshape(HQ)),
        own_gain(key_gain_grad.reshape(HK)),
        own_gain(norm_gain_grads[0]),
        own_gain(norm_gain_grads[1]),
    )


def solution(mesh):
    fine = Mesh(mesh.devices.reshape(4, 4, 2, 2, 2), ("y", "x", "zl", "co", "zh"))
    rows = P("zh", TOKEN_AXES, None)
    weight = P("zh", None)
    gain = P("zh")
    return jax.shard_map(
        per_device,
        mesh=fine,
        in_specs=(rows, weight) + (weight,) * 7 + (gain,) * 4 + (rows,),
        out_specs=(rows, rows) + (weight,) * 7 + (gain,) * 4,
        check_vma=False,
    )
```

time: 612 us -> 509 us (0.83)
  starting transfers between devices: 187 us -> 99.6 us
  matrix products: 58.8 us -> 3.33 us
  waiting for transfers between devices: 138 us -> 187 us
  Pallas kernels: 85.6 us -> 125 us
  other arithmetic: 69.4 us -> 32.8 us
  local copies, waits for them, and re-layouts: 57.1 us -> 34.7 us
  between operations: 5.68 us -> 16.9 us
    ppermute x125 -> x38, starting transfers between devices: 178 us -> 59.5 us  [across(): return lax.ppermute(array, axis, pairs)]
    pallas_call x4 -> x11, Pallas kernels: 26.2 us -> 65.3 us  [the longest x1 25.4 us: own_rows(): pl.pallas_call(rows_kernel, name='own_rows', out_shape=(shape(BLK, D), pl...]
    all_to_all x2 -> x8, waiting for transfers between devices: 0.73 us -> 37.2 us  [exchange(): return lax.all_to_all(array, axes, 0, 0, tiled=True)]
    all_to_all x2 -> x8, starting transfers between devices: 9.07 us -> 39.9 us  [exchange(): return lax.all_to_all(array, axes, 0, 0, tiled=True)]
    dot_general x16 -> x4, matrix products: 22.1 us -> 1.88 us  [dot_second(): lax.dot_general(left_op, right_op, (((1,), (1,)), ((), ())), preferred_el...]
    dot_general x13 -> x0, matrix products: 18 us -> none  [dot_plain(): return jnp.dot(left_op, right_op, preferred_element_type=f32)]
    select_n x44 -> x1, other arithmetic: 19.7 us -> 1.8 us  [per_device(): jnp.where(zl == 0, jnp.stack([chunk, chunk_got]), jnp.stack([chunk_got, c...]
    dot_general x14 -> x2, matrix products: 18.7 us -> 1.46 us  [dot_first(): lax.dot_general(left_op, right_op, (((0,), (0,)), ((), ())), preferred_el...]
  transfers between devices with their start and end apart: 127 -> 48, of which waited for: 56 -> 26; matrix products, arithmetic and copies ran while one was open for 24% -> 7% of each run, Pallas kernels for 13% -> 18%
where the time goes in v2:
time: 509 us; the launch traced here: 499 us
  waiting for transfers between devices  187 us (37%)
  Pallas kernels  125 us (25%)
  starting transfers between devices  99.6 us (20%)
  local copies, waits for them, and re-layouts  34.7 us (7%)
  other arithmetic  32.8 us (6%)
  between operations  16.9 us (3%)
    ppermute x38, waiting for transfers between devices, across(): return lax.ppermute(array, axis, pairs)  150 us
    ppermute x38, starting transfers between devices, across(): return lax.ppermute(array, axis, pairs)  59.5 us
    all_to_all x8, starting transfers between devices, exchange(): return lax.all_to_all(array, axes, 0, 0, tiled=True)  39.9 us
    all_to_all x8, waiting for transfers between devices, exchange(): return lax.all_to_all(array, axes, 0, 0, tiled=True)  37.2 us
    pallas_call x1, Pallas kernels, attention_backward(): pl.pallas_call(backward_kernel, name='attention_backward', out_shape=(jax...  34.7 us
    pallas_call x1, Pallas kernels, own_rows(): pl.pallas_call(rows_kernel, name='own_rows', out_shape=(shape(BLK, D), pl...  25.4 us
    pallas_call x1, Pallas kernels, attention_forward(): pl.pallas_call(forward_kernel, name='attention_forward', out_shape=(jax.S...  24.6 us
    unnamed x121, local copies, waits for them, and re-layouts  21.6 us
  transfers between devices with their start and end apart: 48, of which 26 were waited for; matrix products, arithmetic and copies ran while one was open for 7% of the time, Pallas kernels for 18%

profile of v2, /device:TPU:1, one launch (start us, length us, event | category | flops | bytes accessed | tf_op | source)
XLA Modules:
  0.0 498.8 jit_solution(9123059510771049872)
XLA Ops:
  14.9 4.7 collective-permute-start.1
  19.6 9.1 %collective-permute-done.1 = bf16[192,1024]{1,0:T(8,128)(2,1)S(1)} collective-permute-done((bf16[192,1024]{1,0:T(8,128)(2,1)}, bf16[192,1024]{1,0:T(8,128)(2,1)S(1)}, u32[]{:S(2)}, u32[]{:S(2)}) %collective-permute-start.1) | collective-permute-done | bytes 393248 | tf_op jit(solution)/shard_map/ppermute | solution.py:66
  29.5 4.0 all-to-all-start
  33.5 3.5 collective-permute-start
  42.4 5.1 %collective-permute-done.got_ref = bf16[512,512]{1,0:T(8,128)(2,1)} collective-permute-done((bf16[512,512]{1,0:T(8,128)(2,1)}, bf16[512,512]{1,0:T(8,128)(2,1)}, u32[]{:S(2)}, u32[]{:S(2)}) %collective-permute-start) | collective-permute-done | bytes 524320 | tf_op jit(solution)/shard_map/ppermute | solution.py:66
  47.5 21.4 %all-to-all-done.tokens_ref = bf16[8,128,1024]{2,1,0:T(8,128)(2,1)S(1)} async-done(((bf16[8,128,1024]{2,1,0:T(8,128)(2,1)}), bf16[8,128,1024]{2,1,0:T(8,128)(2,1)S(1)}, u32[]{:S(2)}, u32[]{:S(2)}) %all-to-all-start) | async-done | bytes 2097184 | tf_op jit(solution)/shard_map/all_to_all | solution.py:86
  80.8 5.3 %all-to-all-done.1.squares_ref = f32[8,2,1024]{2,1,0:T(2,128)S(1)} async-done(((f32[8,2,1024]{2,1,0:T(2,128)}), f32[8,2,1024]{2,1,0:T(2,128)S(1)}, u32[]{:S(2)}, u32[]{:S(2)}) %all-to-all-start.1) | async-done | bytes 65568 | tf_op jit(solution)/shard_map/all_to_all | solution.py:86
  89.6 11.7 %collective-permute-done.4 = bf16[512,256]{1,0:T(8,128)(2,1)S(1)} collective-permute-done((bf16[512,256]{1,0:T(8,128)(2,1)S(1)}, bf16[512,256]{1,0:T(8,128)(2,1)S(1)}, u32[]{:S(2)}, u32[]{:S(2)}) %collective-permute-start.4) | collective-permute-done | bytes 262176 | tf_op jit(solution)/shard_map/ppermute | solution.py:66
  105.1 7.5 %collective-permute-done.5.refs_3_ = bf16[2,512,256]{2,1,0:T(8,128)(2,1)S(1)} collective-permute-done((bf16[2,512,256]{2,1,0:T(8,128)(2,1)S(1)}, bf16[2,512,256]{2,1,0:T(8,128)(2,1)S(1)}, u32[]{:S(2)}, u32[]{:S(2)}) %collective-permute-start.5) | collective-permute-done | bytes 524320 | tf_op jit(solution)/shard_map/ppermute | solution.py:66
  121.0 24.6 %attention_forward.1 = (bf16[8,2,64,256]{3,2,1,0:T(8,128)(2,1)S(1)}, f32[2,2,128,512]{3,2,1,0:T(8,128)S(1)}, f32[2,2,1,512]{3,2,1,0:T(1,128)S(1)}) custom-call(s32[4]{0:T(128)S(1)} %pad_add_fusion.2.info_ref, bf16[2,512,256]{2,1,0:T(8,128)(2,1)S(1)} %copy-done.21, bf16[2,512,256]{2,1,0:T(8,128)(2,1)} %copy-done.40, bf16[2,512,256]{2,1,0:T(8,128)(2,1)} %copy-done.54, ...), custom_call_target="tpu_custom_call" | custom-call | flops 9663676416 | bytes 8388608 | tf_op jit(solution)/shard_map/attention_forward/pallas_call | solution.py:343
  147.4 4.2 all-to-all-start.2
  151.7 9.0 %all-to-all-done.2.att_ref = bf16[8,2,64,256]{3,2,1,0:T(8,128)(2,1)S(1)} async-done(((bf16[8,2,64,256]{3,2,1,0:T(8,128)(2,1)}), bf16[8,2,64,256]{3,2,1,0:T(8,128)(2,1)S(1)}, u32[]{:S(2)}, u32[]{:S(2)}) %all-to-all-start.2) | async-done | bytes 524320 | tf_op jit(solution)/shard_map/all_to_all | solution.py:86
  160.8 25.4 %own_rows.1 = (bf16[128,1024]{1,0:T(8,128)(2,1)}, bf16[128,8704]{1,0:T(8,128)(2,1)}, bf16[128,8704]{1,0:T(8,128)(2,1)}, bf16[8,2,64,256]{3,2,1,0:T(8,128)(2,1)S(...) custom-call(s32[2]{0:T(128)S(1)} %pad_add_fusion.1.info_ref, bf16[8,2,64,256]{3,2,1,0:T(8,128)(2,1)S(1)} %all-to-all-done.2.att_ref, ...), custom_call_target="tpu_custom_call" | custom-call | flops 5905580032 | bytes 27262976 | tf_op jit(solution)/shard_map/own_rows/pallas_call | solution.py:783
  188.2 3.5 all-to-all-start.3
  192.5 13.0 %weight_products.1 = (bf16[768,1024]{1,0:T(8,128)(2,1)}, bf16[768,1024]{1,0:T(8,128)(2,1)}, bf16[512,1536]{1,0:T(8,128)(2,1)}, bf16[512,1536]{1,0:T(8,128)(2,1)}...) custom-call(s32[16]{0:T(128)S(1)} %stack.137.places_ref, ...), custom_call_target="tpu_custom_call" | custom-call | flops 2952790016 | bytes 16777216 | tf_op jit(solution)/shard_map/weight_products/pallas_call | solution.py:882
  211.3 34.7 %attention_backward.1 = (f32[2,512,256]{2,1,0:T(8,128)S(1)}, bf16[2,4,512,256]{3,2,1,0:T(8,128)(2,1)}, bf16[2,4,512,256]{3,2,1,0:T(8,128)(2,1)}) custom-call(s32[4]{0:T(128)S(1)} %pad_add_fusion.2.info_ref, bf16[2,512,256]{2,1,0:T(8,128)(2,1)S(1)} %copy-done.22, bf16[8,2,64,256]{3,2,1,0:T(8,128)(2,1)S(1)} %all-to-all-done.3.grad_ref, ...), custom_call_target="tpu_custom_call" | custom-call | flops 24159191040 | bytes 12582912 | tf_op jit(solution)/shard_map/attention_backward/pallas_call | solution.py:369
  256.4 10.0 %collective-permute-done.18 = bf16[2,512,256]{2,1,0:T(8,128)(2,1)S(1)} collective-permute-done((bf16[2,512,256]{2,1,0:T(8,128)(2,1)S(1)}, bf16[2,512,256]{2,1,0:T(8,128)(2,1)S(1)}, u32[]{:S(2)}, u32[]{:S(2)}) %collective-permute-start.18) | collective-permute-done | bytes 524320 | tf_op jit(solution)/shard_map/ppermute | solution.py:66
  273.0 6.3 %all-to-all-start.4 = ((bf16[16,16,3072]{2,1,0:T(8,128)(2,1)}), bf16[16,16,3072]{2,1,0:T(8,128)(2,1)}, u32[]{:S(2)}, u32[]{:S(2)}) async-start(bf16[16,16,3072]{2,1,0:T(8,128)(2,1)} %bitcast.154), calls=%async_computation.4 | async-start | bytes 3145728 | tf_op jit(solution)/shard_map/all_to_all | solution.py:86
  286.6 20.8 %collective-permute-done.24 = bf16[256,1024]{1,0:T(8,128)(2,1)} collective-permute-done((bf16[256,1024]{1,0:T(8,128)(2,1)}, bf16[256,1024]{1,0:T(8,128)(2,1)}, u32[]{:S(2)}, u32[]{:S(2)}) %collective-permute-start.24) | collective-permute-done | bytes 524320 | tf_op jit(solution)/shard_map/ppermute | solution.py:66
  307.3 8.3 %collective-permute-done.23 = bf16[384,1024]{1,0:T(8,128)(2,1)} collective-permute-done((bf16[384,1024]{1,0:T(8,128)(2,1)}, bf16[384,1024]{1,0:T(8,128)(2,1)}, u32[]{:S(2)}, u32[]{:S(2)}) %collective-permute-start.23) | collective-permute-done | bytes 786464 | tf_op jit(solution)/shard_map/ppermute | solution.py:66
  315.7 5.5 %collective-permute-done.22 = bf16[512,256]{1,0:T(8,128)(2,1)S(1)} collective-permute-done((bf16[512,256]{1,0:T(8,128)(2,1)S(1)}, bf16[512,256]{1,0:T(8,128)(2,1)S(1)}, u32[]{:S(2)}, u32[]{:S(2)}) %collective-permute-start.22) | collective-permute-done | bytes 262176 | tf_op jit(solution)/shard_map/ppermute | solution.py:66
  326.0 5.2 %all-to-all-start.5 = ((bf16[16,40,1024]{2,1,0:T(8,128)(2,1)}), bf16[16,40,1024]{2,1,0:T(8,128)(2,1)}, u32[]{:S(2)}, u32[]{:S(2)}) async-start(bf16[16,40,1024]{2,1,0:T(8,128)(2,1)} %pad_maximum_fusion.1), calls=%async_computation.5 | async-start | bytes 2621440 | tf_op jit(solution)/shard_map/all_to_all | solution.py:86
  336.9 8.7 %collective-permute-done.25 = f32[2,1024]{1,0:T(2,128)S(1)} collective-permute-done((f32[2,1024]{1,0:T(2,128)S(1)}, f32[2,1024]{1,0:T(2,128)S(1)}, u32[]{:S(2)}, u32[]{:S(2)}) %collective-permute-start.25) | collective-permute-done | bytes 8224 | tf_op jit(solution)/shard_map/ppermute | solution.py:66
  370.8 5.8 %collective-permute-start.29 = (bf16[528,512]{1,0:T(8,128)(2,1)S(1)}, bf16[528,512]{1,0:T(8,128)(2,1)S(1)}, u32[]{:S(2)}, u32[]{:S(2)}) collective-permute-start(bf16[528,512]{1,0:T(8,128)(2,1)S(1)} %pad_maximum_fusion.4), channel_id=1, source_target_pairs={{0,2},{2,0},{1,3},{3,1},{4,6},{6,4},{5,7},{7,5},{8,10},{10,8},{9,1... | collective-permute-start | bytes 1622024 | tf_op jit(solution)/shard_map/ppermute | solution.py:66
  383.6 12.0 %collective-permute-done.30 = bf16[512,512]{1,0:T(8,128)(2,1)S(1)} collective-permute-done((bf16[512,512]{1,0:T(8,128)(2,1)S(1)}, bf16[512,512]{1,0:T(8,128)(2,1)S(1)}, u32[]{:S(2)}, u32[]{:S(2)}) %collective-permute-start.30) | collective-permute-done | bytes 524320 | tf_op jit(solution)/shard_map/ppermute | solution.py:66
  397.7 6.2 %all-to-all-start.6 = ((bf16[8,80,512]{2,1,0:T(8,128)(2,1)}), bf16[8,80,512]{2,1,0:T(8,128)(2,1)S(1)}, u32[]{:S(2)}, u32[]{:S(2)}) async-start(bf16[8,80,512]{2,1,0:T(8,128)(2,1)} %pad_maximum_fusion.3), calls=%async_computation.6 | async-start | bytes 1310720 | tf_op jit(solution)/shard_map/all_to_all | solution.py:86
  406.3 13.6 %collective-permute-done.33 = bf16[256,512]{1,0:T(8,128)(2,1)} collective-permute-done((bf16[256,512]{1,0:T(8,128)(2,1)S(1)}, bf16[256,512]{1,0:T(8,128)(2,1)}, u32[]{:S(2)}, u32[]{:S(2)}) %collective-permute-start.33) | collective-permute-done | bytes 262176 | tf_op jit(solution)/shard_map/ppermute | solution.py:66
  422.5 7.2 %all-to-all-start.7 = ((bf16[32,80,512]{2,1,0:T(8,128)(2,1)}), bf16[32,80,512]{2,1,0:T(8,128)(2,1)S(1)}, u32[]{:S(2)}, u32[]{:S(2)}) async-start(bf16[32,80,512]{2,1,0:T(8,128)(2,1)} %broadcast_in_dim.64), calls=%async_computation.7 | async-start | bytes 5242880 | tf_op jit(solution)/shard_map/all_to_all | solution.py:86
  434.4 26.4 %collective-permute-done.35 = bf16[128,512]{1,0:T(8,128)(2,1)S(1)} collective-permute-done((bf16[128,512]{1,0:T(8,128)(2,1)S(1)}, bf16[128,512]{1,0:T(8,128)(2,1)S(1)}, u32[]{:S(2)}, u32[]{:S(2)}) %collective-permute-start.35) | collective-permute-done | bytes 131104 | tf_op jit(solution)/shard_map/ppermute | solution.py:66
  461.7 5.3 %collective-permute-start.36 = (bf16[4,8,80,512]{3,2,1,0:T(8,128)(2,1)S(1)}, bf16[4,8,80,512]{3,2,1,0:T(8,128)(2,1)S(1)}, u32[]{:S(2)}, u32[]{:S(2)}) collective-permute-start(bf16[4,8,80,512]{3,2,1,0:T(8,128)(2,1)S(1)} %bitcast.130), channel_id=1, source_target_pairs={{0,2},{2,0},{1,3},{3,1},{4,6},{6,4},{5,7},{7,5},{8,10},{10,8},{9,1... | collective-permute-start | bytes 7864328 | tf_op jit(solution)/shard_map/ppermute | solution.py:66
  479.7 4.6 place_rows.2
  484.2 7.3 %place_rows.3 = (f32[512,3072]{1,0:T(8,128)}, f32[512,3072]{1,0:T(8,128)}, f32[8,192,1024]{2,1,0:T(8,128)}, f32[8,128,1024]{2,1,0:T(8,128)}) custom-call(s32[1]{0:T(128)} %bitcast.45.core_ref, bf16[4,4,2,88,1024]{4,3,2,1,0:T(8,128)(2,1)} %collective-permute-done.37.chunk_ref, ...), custom_call_target="tpu_custom_call", output_to_operand_aliasing={{0}: (2, {}), {1}: (3, {}), {2}: (4, {}), {3}: (5, {})} | custom-call | flops 3145728 | bytes 18874368 | tf_op jit(solution)/shard_map/place_rows/pallas_call | solution.py:929
  (303 shorter events, 142.0 us)
Async XLA Ops:
  7.2 111.8 %all-gather.6.cloned.1.call-start = ((), (), s32[]{:S(2)}) async-start(), calls=%async_computation.9 | async-start | bytes 6127616 | tf_op jit(solution)/shard_map/all_gather | solution.py:1037
  14.9 13.7 %collective-permute-start.1 = (bf16[192,1024]{1,0:T(8,128)(2,1)}, bf16[192,1024]{1,0:T(8,128)(2,1)S(1)}, u32[]{:S(2)}, u32[]{:S(2)}) collective-permute-start(bf16[192,1024]{1,0:T(8,128)(2,1)} %get-tuple-element.115), channel_id=1, source_target_pairs={{0,5},{5,0},{1,4},{4,1},{2,7},{7,2},{3,6},{6,3},{8,13},{13,8},{9,1... | collective-permute-start | bytes 1179656 | tf_op jit(solution)/shard_map/ppermute | solution.py:66
  29.5 39.4 %all-to-all-start = ((bf16[8,128,1024]{2,1,0:T(8,128)(2,1)}), bf16[8,128,1024]{2,1,0:T(8,128)(2,1)S(1)}, u32[]{:S(2)}, u32[]{:S(2)}) async-start(bf16[8,128,1024]{2,1,0:T(8,128)(2,1)} %broadcast_in_dim.54), calls=%async_computation | async-start | bytes 4194304 | tf_op jit(solution)/shard_map/all_to_all | solution.py:86
  33.5 14.0 %collective-permute-start = (bf16[512,512]{1,0:T(8,128)(2,1)}, bf16[512,512]{1,0:T(8,128)(2,1)}, u32[]{:S(2)}, u32[]{:S(2)}) collective-permute-start(bf16[512,512]{1,0:T(8,128)(2,1)} %get-tuple-element.112), channel_id=1, source_target_pairs={{0,5},{5,0},{1,4},{4,1},{2,7},{7,2},{3,6},{6,3},{8,13},{13,8},{9,1... | collective-permute-start | bytes 1572872 | tf_op jit(solution)/shard_map/ppermute | solution.py:66
  87.0 14.3 %collective-permute-start.4 = (bf16[512,256]{1,0:T(8,128)(2,1)S(1)}, bf16[512,256]{1,0:T(8,128)(2,1)S(1)}, u32[]{:S(2)}, u32[]{:S(2)}) collective-permute-start(bf16[512,256]{1,0:T(8,128)(2,1)S(1)} %get-tuple-element.223), channel_id=1, source_target_pairs={{32,64},{64,32},{96,0},{0,96},{33,65},{65,33},{97,1},{1,97},{34,66... | collective-permute-start | bytes 786440 | tf_op jit(solution)/shard_map/ppermute | solution.py:66
  101.5 14.2 %collective-permute-start.3 = (bf16[2,512,256]{2,1,0:T(8,128)(2,1)S(1)}, bf16[2,512,256]{2,1,0:T(8,128)(2,1)S(1)}, u32[]{:S(2)}, u32[]{:S(2)}) collective-permute-start(bf16[2,512,256]{2,1,0:T(8,128)(2,1)S(1)} %pad_maximum_fusion.7.refs_0_), channel_id=1, source_target_pairs={{32,64},{64,32},{96,0},{0,96},{33,65},{65,33},{97,1},{1,97},{34,66... | collective-permute-start | bytes 1572872 | tf_op jit(solution)/shard_map/ppermute | solution.py:66
  103.2 14.0 %collective-permute-start.8 = (bf16[2,512,256]{2,1,0:T(8,128)(2,1)S(1)}, bf16[2,512,256]{2,1,0:T(8,128)(2,1)S(1)}, u32[]{:S(2)}, u32[]{:S(2)}) collective-permute-start(bf16[2,512,256]{2,1,0:T(8,128)(2,1)S(1)} %pad_maximum_fusion.8.refs_2_), channel_id=1, source_target_pairs={{0,2},{2,0},{1,3},{3,1},{4,6},{6,4},{5,7},{7,5},{8,10},{10,8},{9,1... | collective-permute-start | bytes 1572872 | tf_op jit(solution)/shard_map/ppermute | solution.py:66
  119.0 41.8 %collective-permute-start.10 = (bf16[16,176,1024]{2,1,0:T(8,128)(2,1)}, bf16[16,176,1024]{2,1,0:T(8,128)(2,1)}, u32[]{:S(2)}, u32[]{:S(2)}) collective-permute-start(bf16[16,176,1024]{2,1,0:T(8,128)(2,1)} %bitcast.156), channel_id=1, source_target_pairs={{0,2},{2,0},{1,3},{3,1},{4,6},{6,4},{5,7},{7,5},{8,10},{10,8},{9,1... | collective-permute-start | bytes 17301512 | tf_op jit(solution)/shard_map/ppermute | solution.py:66
  147.4 13.4 %all-to-all-start.2 = ((bf16[8,2,64,256]{3,2,1,0:T(8,128)(2,1)}), bf16[8,2,64,256]{3,2,1,0:T(8,128)(2,1)S(1)}, u32[]{:S(2)}, u32[]{:S(2)}) async-start(bf16[8,2,64,256]{3,2,1,0:T(8,128)(2,1)} %copy-done.18), calls=%async_computation.2 | async-start | bytes 1048576 | tf_op jit(solution)/shard_map/all_to_all | solution.py:86
  188.2 17.3 %all-to-all-start.3 = ((bf16[8,2,64,256]{3,2,1,0:T(8,128)(2,1)}), bf16[8,2,64,256]{3,2,1,0:T(8,128)(2,1)S(1)}, u32[]{:S(2)}, u32[]{:S(2)}) async-start(bf16[8,2,64,256]{3,2,1,0:T(8,128)(2,1)} %copy-done.17), calls=%async_computation.3 | async-start | bytes 1048576 | tf_op jit(solution)/shard_map/all_to_all | solution.py:86
  205.5 40.6 %collective-permute-start.15 = (bf16[512,1024]{1,0:T(8,128)(2,1)}, bf16[512,1024]{1,0:T(8,128)(2,1)S(1)}, u32[]{:S(2)}, u32[]{:S(2)}) collective-permute-start(bf16[512,1024]{1,0:T(8,128)(2,1)} %get-tuple-element.144), channel_id=1, source_target_pairs={{32,64},{64,32},{96,0},{0,96},{33,65},{65,33},{97,1},{1,97},{34,66... | collective-permute-start | bytes 3145736 | tf_op jit(solution)/shard_map/ppermute | solution.py:66
  207.6 38.5 %collective-permute-start.12 = (bf16[768,1024]{1,0:T(8,128)(2,1)}, bf16[768,1024]{1,0:T(8,128)(2,1)S(1)}, u32[]{:S(2)}, u32[]{:S(2)}) collective-permute-start(bf16[768,1024]{1,0:T(8,128)(2,1)} %get-tuple-element.141), channel_id=1, source_target_pairs={{0,32},{32,0},{64,96},{96,64},{1,33},{33,1},{65,97},{97,65},{2,34}... | collective-permute-start | bytes 4718600 | tf_op jit(solution)/shard_map/ppermute | solution.py:66
  207.6 38.5 %collective-permute-start.13 = (bf16[512,1536]{1,0:T(8,128)(2,1)}, bf16[512,1536]{1,0:T(8,128)(2,1)S(1)}, u32[]{:S(2)}, u32[]{:S(2)}) collective-permute-start(bf16[512,1536]{1,0:T(8,128)(2,1)} %get-tuple-element.142), channel_id=1, source_target_pairs={{0,8},{8,0},{16,24},{24,16},{1,9},{9,1},{17,25},{25,17},{2,10},{10... | collective-permute-start | bytes 4718600 | tf_op jit(solution)/shard_map/ppermute | solution.py:66
  208.3 37.8 %collective-permute-start.14 = (bf16[512,1536]{1,0:T(8,128)(2,1)}, bf16[512,1536]{1,0:T(8,128)(2,1)S(1)}, u32[]{:S(2)}, u32[]{:S(2)}) collective-permute-start(bf16[512,1536]{1,0:T(8,128)(2,1)} %get-tuple-element.143), channel_id=1, source_target_pairs={{8,16},{16,8},{24,0},{0,24},{9,17},{17,9},{25,1},{1,25},{10,18},{1... | collective-permute-start | bytes 4718600 | tf_op jit(solution)/shard_map/ppermute | solution.py:66
  252.1 19.0 %collective-permute-start.19 = (bf16[256,1536]{1,0:T(8,128)(2,1)S(1)}, bf16[256,1536]{1,0:T(8,128)(2,1)S(1)}, u32[]{:S(2)}, u32[]{:S(2)}) collective-permute-start(bf16[256,1536]{1,0:T(8,128)(2,1)S(1)} %add_convert_fusion.4), channel_id=1, source_target_pairs={{8,16},{16,8},{24,0},{0,24},{9,17},{17,9},{25,1},{1,25},{10,18},{1... | collective-permute-start | bytes 2359304 | tf_op jit(solution)/shard_map/ppermute | solution.py:66
  253.0 18.1 %collective-permute-start.20 = (bf16[256,1536]{1,0:T(8,128)(2,1)S(1)}, bf16[256,1536]{1,0:T(8,128)(2,1)S(1)}, u32[]{:S(2)}, u32[]{:S(2)}) collective-permute-start(bf16[256,1536]{1,0:T(8,128)(2,1)S(1)} %add_convert_fusion.3), channel_id=1, source_target_pairs={{0,8},{8,0},{16,24},{24,16},{1,9},{9,1},{17,25},{25,17},{2,10},{10... | collective-permute-start | bytes 2359304 | tf_op jit(solution)/shard_map/ppermute | solution.py:66
  253.5 12.9 %collective-permute-start.18 = (bf16[2,512,256]{2,1,0:T(8,128)(2,1)S(1)}, bf16[2,512,256]{2,1,0:T(8,128)(2,1)S(1)}, u32[]{:S(2)}, u32[]{:S(2)}) collective-permute-start(bf16[2,512,256]{2,1,0:T(8,128)(2,1)S(1)} %get-tuple-element.209), channel_id=1, source_target_pairs={{0,32},{32,0},{64,96},{96,64},{1,33},{33,1},{65,97},{97,65},{2,34}... | collective-permute-start | bytes 1572872 | tf_op jit(solution)/shard_map/ppermute | solution.py:66
  273.0 48.1 %all-to-all-start.4 = ((bf16[16,16,3072]{2,1,0:T(8,128)(2,1)}), bf16[16,16,3072]{2,1,0:T(8,128)(2,1)}, u32[]{:S(2)}, u32[]{:S(2)}) async-start(bf16[16,16,3072]{2,1,0:T(8,128)(2,1)} %bitcast.154), calls=%async_computation.4 | async-start | bytes 3145728 | tf_op jit(solution)/shard_map/all_to_all | solution.py:86
  279.3 28.0 %collective-permute-start.24 = (bf16[256,1024]{1,0:T(8,128)(2,1)}, bf16[256,1024]{1,0:T(8,128)(2,1)}, u32[]{:S(2)}, u32[]{:S(2)}) collective-permute-start(bf16[256,1024]{1,0:T(8,128)(2,1)} %add_convert_fusion.11), channel_id=1, source_target_pairs={{0,32},{32,0},{64,96},{96,64},{1,33},{33,1},{65,97},{97,65},{2,34}... | collective-permute-start | bytes 1572872 | tf_op jit(solution)/shard_map/ppermute | solution.py:66
  280.7 35.0 %collective-permute-start.23 = (bf16[384,1024]{1,0:T(8,128)(2,1)}, bf16[384,1024]{1,0:T(8,128)(2,1)}, u32[]{:S(2)}, u32[]{:S(2)}) collective-permute-start(bf16[384,1024]{1,0:T(8,128)(2,1)} %add_convert_fusion.5), channel_id=1, source_target_pairs={{32,64},{64,32},{96,0},{0,96},{33,65},{65,33},{97,1},{1,97},{34,66... | collective-permute-start | bytes 2359304 | tf_op jit(solution)/shard_map/ppermute | solution.py:66
  285.6 35.6 %collective-permute-start.22 = (bf16[512,256]{1,0:T(8,128)(2,1)S(1)}, bf16[512,256]{1,0:T(8,128)(2,1)S(1)}, u32[]{:S(2)}, u32[]{:S(2)}) collective-permute-start(bf16[512,256]{1,0:T(8,128)(2,1)S(1)} %fusion.21), channel_id=1, source_target_pairs={{32,64},{64,32},{96,0},{0,96},{33,65},{65,33},{97,1},{1,97},{34,66... | collective-permute-start | bytes 786440 | tf_op jit(solution)/shard_map/ppermute | solution.py:66
  286.6 34.6 %collective-permute-start.21 = (bf16[512,256]{1,0:T(8,128)(2,1)S(1)}, bf16[512,256]{1,0:T(8,128)(2,1)}, u32[]{:S(2)}, u32[]{:S(2)}) collective-permute-start(bf16[512,256]{1,0:T(8,128)(2,1)S(1)} %fusion.20), channel_id=1, source_target_pairs={{0,32},{32,0},{64,96},{96,64},{1,33},{33,1},{65,97},{97,65},{2,34}... | collective-permute-start | bytes 786440 | tf_op jit(solution)/shard_map/ppermute | solution.py:66
  326.0 26.5 %all-to-all-start.5 = ((bf16[16,40,1024]{2,1,0:T(8,128)(2,1)}), bf16[16,40,1024]{2,1,0:T(8,128)(2,1)}, u32[]{:S(2)}, u32[]{:S(2)}) async-start(bf16[16,40,1024]{2,1,0:T(8,128)(2,1)} %pad_maximum_fusion.1), calls=%async_computation.5 | async-start | bytes 2621440 | tf_op jit(solution)/shard_map/all_to_all | solution.py:86
  331.2 142.8 %all-gather.4.cloned.1.call-start = ((), (), s32[]{:S(2)}) async-start(), calls=%async_computation.8 | async-start | bytes 6127616 | tf_op jit(solution)/shard_map/all_gather | solution.py:1183
  370.8 24.8 %collective-permute-start.29 = (bf16[528,512]{1,0:T(8,128)(2,1)S(1)}, bf16[528,512]{1,0:T(8,128)(2,1)S(1)}, u32[]{:S(2)}, u32[]{:S(2)}) collective-permute-start(bf16[528,512]{1,0:T(8,128)(2,1)S(1)} %pad_maximum_fusion.4), channel_id=1, source_target_pairs={{0,2},{2,0},{1,3},{3,1},{4,6},{6,4},{5,7},{7,5},{8,10},{10,8},{9,1... | collective-permute-start | bytes 1622024 | tf_op jit(solution)/shard_map/ppermute | solution.py:66
  377.2 18.4 %collective-permute-start.30 = (bf16[512,512]{1,0:T(8,128)(2,1)S(1)}, bf16[512,512]{1,0:T(8,128)(2,1)S(1)}, u32[]{:S(2)}, u32[]{:S(2)}) collective-permute-start(bf16[512,512]{1,0:T(8,128)(2,1)S(1)} %convolution_convert_fusion.1), channel_id=1, source_target_pairs={{8,16},{16,8},{24,0},{0,24},{9,17},{17,9},{25,1},{1,25},{10,18},{1... | collective-permute-start | bytes 1572872 | tf_op jit(solution)/shard_map/ppermute | solution.py:66
  379.7 15.9 %collective-permute-start.31 = (bf16[512,512]{1,0:T(8,128)(2,1)S(1)}, bf16[512,512]{1,0:T(8,128)(2,1)S(1)}, u32[]{:S(2)}, u32[]{:S(2)}) collective-permute-start(bf16[512,512]{1,0:T(8,128)(2,1)S(1)} %convolution_convert_fusion), channel_id=1, source_target_pairs={{0,4},{4,0},{1,5},{5,1},{2,6},{6,2},{3,7},{7,3},{8,12},{12,8},{9,1... | collective-permute-start | bytes 1572872 | tf_op jit(solution)/shard_map/ppermute | solution.py:66
  397.7 22.8 %all-to-all-start.6 = ((bf16[8,80,512]{2,1,0:T(8,128)(2,1)}), bf16[8,80,512]{2,1,0:T(8,128)(2,1)S(1)}, u32[]{:S(2)}, u32[]{:S(2)}) async-start(bf16[8,80,512]{2,1,0:T(8,128)(2,1)} %pad_maximum_fusion.3), calls=%async_computation.6 | async-start | bytes 1310720 | tf_op jit(solution)/shard_map/all_to_all | solution.py:86
  405.2 14.7 %collective-permute-start.33 = (bf16[256,512]{1,0:T(8,128)(2,1)S(1)}, bf16[256,512]{1,0:T(8,128)(2,1)}, u32[]{:S(2)}, u32[]{:S(2)}) collective-permute-start(bf16[256,512]{1,0:T(8,128)(2,1)S(1)} %dynamic-slice_bitcast_fusion), channel_id=1, source_target_pairs={{8,16},{16,8},{24,0},{0,24},{9,17},{17,9},{25,1},{1,25},{10,18},{1... | collective-permute-start | bytes 786440 | tf_op jit(solution)/shard_map/ppermute | solution.py:66
  422.5 39.2 %all-to-all-start.7 = ((bf16[32,80,512]{2,1,0:T(8,128)(2,1)}), bf16[32,80,512]{2,1,0:T(8,128)(2,1)S(1)}, u32[]{:S(2)}, u32[]{:S(2)}) async-start(bf16[32,80,512]{2,1,0:T(8,128)(2,1)} %broadcast_in_dim.64), calls=%async_computation.7 | async-start | bytes 5242880 | tf_op jit(solution)/shard_map/all_to_all | solution.py:86
  431.9 28.9 %collective-permute-start.35 = (bf16[128,512]{1,0:T(8,128)(2,1)S(1)}, bf16[128,512]{1,0:T(8,128)(2,1)S(1)}, u32[]{:S(2)}, u32[]{:S(2)}) collective-permute-start(bf16[128,512]{1,0:T(8,128)(2,1)S(1)} %dynamic-slice_bitcast_fusion.2), channel_id=1, source_target_pairs={{0,8},{8,0},{16,24},{24,16},{1,9},{9,1},{17,25},{25,17},{2,10},{10... | collective-permute-start | bytes 393224 | tf_op jit(solution)/shard_map/ppermute | solution.py:66
  433.2 27.6 %collective-permute-start.34 = (bf16[128,512]{1,0:T(8,128)(2,1)S(1)}, bf16[128,512]{1,0:T(8,128)(2,1)S(1)}, u32[]{:S(2)}, u32[]{:S(2)}) collective-permute-start(bf16[128,512]{1,0:T(8,128)(2,1)S(1)} %dynamic-slice_bitcast_fusion.3), channel_id=1, source_target_pairs={{0,4},{4,0},{1,5},{5,1},{2,6},{6,2},{3,7},{7,3},{8,12},{12,8},{9,1... | collective-permute-start | bytes 393224 | tf_op jit(solution)/shard_map/ppermute | solution.py:66
  (74 other events, 596.5 us)
Sparse Core Ops, SparseCore 0:
  29.6 72.9 all-gather.5
  362.2 71.2 all-gather.3

commit v3 on v2

--- a/solution.py
+++ b/solution.py
@@ -43,6 +43,7 @@
     "y1": ("y", edge_b),
     "zA": ("zl", swap),
     "zB": (("zl", "zh"), [(0, 3), (3, 0), (1, 2), (2, 1)]),
+    "zl": ("zl", swap),
     "co": ("co", swap),
     "zh": ("zh", swap),
 }
@@ -90,6 +91,16 @@
     return exchange(jnp.broadcast_to(array[None], (count, *array.shape)), axes)
 
 
+def double(array, link):
+    if link == "zA":
+        bit = link_bit(link)
+    else:
+        place = lax.axis_index(LINKS[link][0])
+        bit = place // 2 if link in ("x1", "y1") else place % 2
+    got = across(array, link)
+    return jnp.where(bit == 0, jnp.concatenate([array, got]), jnp.concatenate([got, array]))
+
+
 def high_low(values):
     high = values.astype(bf16)
     return jnp.stack([high, (values - high.astype(f32)).astype(bf16)])
@@ -177,31 +188,42 @@
             denom[head] = jnp.zeros((1, group_rows), f32)
             acc[head] = jnp.zeros((HD, group_rows), f32)
 
-        def step(group, key_half, masked):
-            slot = slot_of(group, key_half, y, co)
-            keys = kvs[(*slot, slice(None), slice(0, HD))]
-            values = kvs[(*slot, slice(None), slice(HD, 2 * HD))]
+        def step(chunks, masked):
+            slots = [slot_of(*chunk, y, co) for chunk in chunks]
+            keys = [kvs[(*slot, slice(None), slice(0, HD))] for slot in slots]
+            values = [kvs[(*slot, slice(None), slice(HD, 2 * HD))] for slot in slots]
             if masked:
-                mask = pair_mask(group, key_half, query_pos, query_start)
+                masks = [pair_mask(*chunk, query_pos, query_start) for chunk in chunks]
             for head in range(2):
-                scores = dot_plain(keys, qt[head])
+                scores = [dot_plain(part, qt[head]) for part in keys]
                 if masked:
-                    scores = jnp.where(mask, scores, masked_score)
+                    scores = [
+                        jnp.where(mask, part, masked_score) for mask, part in zip(masks, scores)
+                    ]
                 old_top = top[head]
-                new_top = jnp.maximum(old_top, jnp.max(scores, axis=0, keepdims=True))
-                weights = jnp.exp2(scores - new_top)
+                new_top = old_top
+                for part in scores:
+                    new_top = jnp.maximum(new_top, jnp.max(part, axis=0, keepdims=True))
+                weights = [jnp.exp2(part - new_top) for part in scores]
                 rescale = jnp.exp2(old_top - new_top)
-                denom[head] = denom[head] * rescale + jnp.sum(weights, axis=0, keepdims=True)
-                acc[head] = acc[head] * rescale + dot_first(values, weights.astype(bf16))
+                total = denom[head] * rescale
+                for part in weights:
+                    total += jnp.sum(part, axis=0, keepdims=True)
+                denom[head] = total
+                acc[head] = (
+                    acc[head] * rescale
+                    + dot_first(values[0], weights[0].astype(bf16))
+                    + dot_first(values[1], weights[1].astype(bf16))
+                )
                 top[head] = new_top
 
         count, chunk = open_steps(y, half)
 
         def open_body(number, inner):
-            step(*chunk(number), False)
+            step((chunk(2 * number), chunk(2 * number + 1)), False)
             return inner
 
-        lax.fori_loop(0, count, open_body, 0)
+        lax.fori_loop(0, count // 2, open_body, 0)
         for head in range(2):
             top[head] = jnp.where(last_doc, masked_score, top[head])
             denom[head] = jnp.where(last_doc, 0.0, denom[head])
@@ -209,10 +231,10 @@
         masked_count, masked_chunk = masked_steps(y, half)
 
         def masked_body(number, inner):
-            step(*masked_chunk(number), True)
+            step((masked_chunk(2 * number), masked_chunk(2 * number + 1)), True)
             return inner
 
-        lax.fori_loop(0, masked_count, masked_body, 0)
+        lax.fori_loop(0, masked_count // 2, masked_body, 0)
         for head in range(2):
             lanes = slice(head * HD, (head + 1) * HD)
             attended = acc[head] / denom[head]
@@ -252,47 +274,44 @@
             delta[head] = jnp.sum(grad_t * full_ref[half, head], axis=0, keepdims=True)
             dqt[head] = jnp.zeros((HD, group_rows), f32)
 
-        def step(group, key_half, masked):
-            slot = slot_of(group, key_half, y, co)
-            key_lanes = (*slot, slice(None), slice(0, HD))
-            value_lanes = (*slot, slice(None), slice(HD, 2 * HD))
-            keys = kvs[key_lanes]
-            values = kvs[value_lanes]
-            if masked:
-                mask = pair_mask(group, key_half, query_pos, query_start)
-            key_total = dkv[key_lanes]
-            value_total = dkv[value_lanes]
+        def step(chunks, masked):
             for head in range(2):
                 lanes = slice(head * HD, (head + 1) * HD)
-                scores = dot_plain(keys, qt[head])
                 total = total_ref[half, head]
-                if masked:
-                    scores = jnp.where(mask, scores, masked_score)
-                else:
+                if not masked:
                     total = jnp.where(last_doc, -masked_score, total)
-                probs = jnp.exp2(scores - total)
-                value_total += dot_plain(probs.astype(bf16), grads_of(half, lanes))
-                prob_grad = dot_plain(values, gt[head])
-                low = (probs * (prob_grad - delta[head])).astype(bf16)
-                key_total += dot_plain(low, query_ref[half, :, lanes])
-                dqt[head] += dot_first(keys, low)
-            dkv[key_lanes] = key_total
-            dkv[value_lanes] = value_total
+                query_total = dqt[head]
+                for chunk in chunks:
+                    slot = slot_of(*chunk, y, co)
+                    key_lanes = (*slot, slice(None), slice(0, HD))
+                    value_lanes = (*slot, slice(None), slice(HD, 2 * HD))
+                    keys = kvs[key_lanes]
+                    scores = dot_plain(keys, qt[head])
+                    if masked:
+                        mask = pair_mask(*chunk, query_pos, query_start)
+                        scores = jnp.where(mask, scores, masked_score)
+                    probs = jnp.exp2(scores - total)
+                    dkv[value_lanes] += dot_plain(probs.astype(bf16), grads_of(half, lanes))
+                    prob_grad = dot_plain(kvs[value_lanes], gt[head])
+                    low = (probs * (prob_grad - delta[head])).astype(bf16)
+                    dkv[key_lanes] += dot_plain(low, query_ref[half, :, lanes])
+                    query_total += dot_first(keys, low)
+                dqt[head] = query_total
 
         count, chunk = open_steps(y, half)
 
         def open_body(number, inner):
-            step(*chunk(number), False)
+            step((chunk(2 * number), chunk(2 * number + 1)), False)
             return inner
 
-        lax.fori_loop(0, count, open_body, 0)
+        lax.fori_loop(0, count // 2, open_body, 0)
         masked_count, masked_chunk = masked_steps(y, half)
 
         def masked_body(number, inner):
-            step(*masked_chunk(number), True)
+            step((masked_chunk(2 * number), masked_chunk(2 * number + 1)), True)
             return inner
 
-        lax.fori_loop(0, masked_count, masked_body, 0)
+        lax.fori_loop(0, masked_count // 2, masked_body, 0)
         for head in range(2):
             lanes = slice(head * HD, (head + 1) * HD)
             dq_ref[half, :, lanes] = dqt[head].T * score_scale
@@ -569,9 +588,12 @@
 
 
 def raw_grad_kernel(
-    raw_ref, squares_ref, cos_ref, sin_ref, gain_ref, dq_ref, dkv_ref, means_ref,
-    low_ref, gain_grad_ref,
+    info_ref, raw_ref, squares_ref, cos_ref, sin_ref, gain_ref, dq_ref, dkv_ref, means_ref,
+    tokens_ref, weight_ref, norm_gains_ref,
+    heads_sent_ref, heads_kept_ref, gains_ref, left_sent_ref, left_kept_ref, right_sent_ref,
+    right_kept_ref, low_ref,
 ):
+    co, x_high, zl = info_ref[0], info_ref[1], info_ref[2]
     means = (as_rows(means_ref[0:1]) / HQ, as_rows(means_ref[1:2]) / HK)
 
     def place(lanes, low):
@@ -582,14 +604,36 @@
                     start : start + half_blk
                 ]
 
+    gains_ref[...] = jnp.zeros((8, 4 * HD), f32)
     for head, lanes, upstream, normed, inverse in turned_back(
         raw_ref, squares_ref, cos_ref, sin_ref, dq_ref, dkv_ref
     ):
         mean = means[0] if head < 2 else means[1]
         place(lanes, (inverse * (upstream * gain_ref[:, lanes] - normed * mean)).astype(bf16))
-        gain_grad_ref[:, lanes] = jnp.sum(upstream * normed, axis=0, keepdims=True)
+        gains_ref[0:1, lanes] = jnp.sum(upstream * normed, axis=0, keepdims=True)
     place(slice(3 * HD, 4 * HD), dkv_ref[:, HD:].astype(bf16))
-    gain_grad_ref[:, 3 * HD :] = jnp.zeros((1, HD), f32)
+    for row in range(4):
+        part = slice((row % 2) * 4 * HD, (row % 2 + 1) * 4 * HD)
+        gains_ref[1 + row : 2 + row] = norm_gains_ref[row // 2 : row // 2 + 1, part]
+    gains = gains_ref[...]
+    high = gains.astype(bf16)
+    heads_sent_ref[512:] = jnp.concatenate([high, (gains - high.astype(f32)).astype(bf16)])
+
+    low = low_ref[...].reshape(ROWS, 4 * HD)
+    for part in range(2):
+        rows = slice(part * 256, (part + 1) * 256)
+        for ref, side in ((heads_sent_ref, 1 - co), (heads_kept_ref, co)):
+            lanes = pl.ds(pl.multiple_of(part * 512 + side * 256, 256), 256)
+            tokens = tokens_ref[:, :, lanes].reshape(ROWS, 256)
+            ref[rows] = dot_first(tokens, low).astype(ref.dtype)
+
+    for number in range(4):
+        for ref, side in ((left_sent_ref, 1 - x_high), (left_kept_ref, x_high)):
+            rows = low_ref[side * 4 + number]
+            ref[number] = dot_second(rows, weight_ref[: D // 2]).astype(bf16)
+        for ref, side in ((right_sent_ref, 1 - zl), (right_kept_ref, zl)):
+            rows = low_ref[2 * number + side]
+            ref[number] = dot_second(rows, weight_ref[D // 2 :]).astype(bf16)
 
 
 def projection_means(*operands):
@@ -604,19 +648,26 @@
     )(*operands)
 
 
-def projection_grads(*operands):
+def projection_grads(info, *operands):
+    part = jax.ShapeDtypeStruct((4, BLK, D // 2), bf16)
     return pl.pallas_call(
         raw_grad_kernel,
         name="projection_grads",
         out_shape=(
-            jax.ShapeDtypeStruct((8, BLK, 4 * HD), bf16),
-            jax.ShapeDtypeStruct((1, 4 * HD), f32),
-        ),
-        in_specs=[vmem] * 8,
-        out_specs=[vmem] * 2,
-        compiler_params=pltpu.CompilerParams(vmem_limit_bytes=32 << 20),
-        cost_estimate=pl.CostEstimate(flops=8 << 20, bytes_accessed=6 << 20, transcendentals=0),
-    )(*operands)
+            jax.ShapeDtypeStruct((512 + 16, 4 * HD), bf16),
+            jax.ShapeDtypeStruct((512, 4 * HD), f32),
+            jax.ShapeDtypeStruct((8, 4 * HD), f32),
+            part,
+            part,
+            part,
+            part,
+        ),
+        in_specs=[smem] + [vmem] * 11,
+        out_specs=[vmem] * 7,
+        scratch_shapes=[pltpu.VMEM((8, BLK, 4 * HD), bf16)],
+        compiler_params=pltpu.CompilerParams(vmem_limit_bytes=40 << 20),
+        cost_estimate=pl.CostEstimate(flops=4 << 30, bytes_accessed=16 << 20, transcendentals=0),
+    )(info, *operands)
 
 
 INNER_AT = 0
@@ -633,7 +684,7 @@
     info_ref, att_ref, tokens_ref, cot_ref, attn_gain_ref, ffn_gain_ref,
     out_own, gate_own, up_own, down_own, mine, other,
     output_ref, own_hbm, sent_hbm, att_grad_ref, hidden_grad_ref, gain_grad_ref,
-    own_ref, sent_ref, out_v, gate_v, up_v, down_v, gate_act, up_act, inner_ref, hidden_ref, down_out, sems,
+    own_ref, sent_ref, out_v, gate_v, up_v, down_v, gate_act, up_act, inner_ref, up_low_ref, hidden_ref, sems,
 ):
     zh, co = info_ref[0], info_ref[1]
     numbers = iter(range(22))
@@ -658,7 +709,7 @@
     gate_copies = pieces(gate_own, GATE_AT, GATE_ROWS, gate_v, BLOCKS)
     up_copies = pieces(up_own, UP_AT, GATE_ROWS, up_v, BLOCKS)
     down_copies = pieces(down_own, DOWN_AT, DOWN_ROWS, down_v, 1)
-    for item in out_copies + gate_copies + up_copies + down_copies:
+    for item in out_copies:
         item.start()
 
     def put(core, lanes, value):
@@ -674,26 +725,26 @@
         own_ref[:, start : start + D] = value
         sent_ref[:, start : start + D] = value
 
+    for head in range(8):
+        rows = att_ref[head].reshape(BLK, 2 * HD)
+        inner_ref[:, head * 2 * HD : (head + 1) * 2 * HD] = rows
+        start = ATT_AT + ((head // 4) * 2 + head % 2) * 2 * HD
+        put((head // 2) % 2, slice(start, start + 2 * HD), rows)
     for item in out_copies:
         item.wait()
-    hidden_grad_ref[...] = jnp.zeros((BLK, D), f32)
-
-    def mixed_body(head, carry):
-        rows = att_ref[head].reshape(BLK, 2 * HD)
-        column = (head // 4) * 2 + head % 2
-        put((head // 2) % 2, pl.ds(pl.multiple_of(ATT_AT + column * 2 * HD, HD), 2 * HD), rows)
-        hidden_grad_ref[...] += dot_plain(rows, out_v[pl.ds(head * 8, 8)].reshape(2 * HD, D))
-        return carry
-
-    lax.fori_loop(0, 8, mixed_body, 0)
+    for item in gate_copies + up_copies:
+        item.start()
     attn_gain = attn_gain_ref[...]
-    mixed = hidden_grad_ref[...]
+    mixed = dot_plain(inner_ref[:, :HQ], out_v[...].reshape(HQ, D))
+    hidden_grad_ref[...] = mixed
     attn_inverse = lax.rsqrt(jnp.mean(mixed * mixed, axis=-1, keepdims=True) + epsilon)
     hidden = tokens_ref[...].astype(f32) + mixed * attn_inverse * attn_gain
     hidden_ref[...] = hidden
     put_both(HIDDEN_AT, hidden.astype(bf16))
     for item in gate_copies + up_copies:
         item.wait()
+    for item in down_copies:
+        item.start()
     tile = 8 * DOWN_ROWS
 
     def act_body(step, carry):
@@ -712,16 +763,8 @@
     lax.fori_loop(0, FF // tile, act_body, 0)
     for item in down_copies:
         item.wait()
-    down_out[...] = jnp.zeros((BLK, D), f32)
-
-    def down_body(step, carry):
-        rows = down_v[pl.ds(step * 8, 8)].reshape(tile, D)
-        down_out[...] += dot_plain(inner_ref[:, pl.ds(step * tile, tile)], rows)
-        return carry
-
-    lax.fori_loop(0, FF // tile, down_body, 0)
     ffn_gain = ffn_gain_ref[...]
-    down = down_out[...]
+    down = dot_plain(inner_ref[...], down_v[...].reshape(FF, D))
     ffn_inverse = lax.rsqrt(jnp.mean(down * down, axis=-1, keepdims=True) + epsilon)
     normed = down * ffn_inverse
     output_ref[...] = (hidden_ref[...] + normed * ffn_gain).astype(bf16)
@@ -730,8 +773,6 @@
     gain_grad_ref[1:2, :] = jnp.sum(upstream * normed, axis=0, keepdims=True)
     down_low = ffn_inverse * (scaled - normed * jnp.mean(scaled * normed, axis=-1, keepdims=True))
     put_both(DOWN_LOW_AT, down_low.astype(bf16))
-    down_out[...] = upstream
-
     def back_body(step, carry):
         lanes = pl.ds(step * tile, tile)
         rows = down_v[pl.ds(step * 8, 8)].reshape(tile, D)
@@ -743,16 +784,19 @@
         column = (step % 4) * tile
         put(step // 4, pl.ds(pl.multiple_of(GATE_LOW_AT + column, HD), tile), gate_low)
         put(step // 4, pl.ds(pl.multiple_of(UP_LOW_AT + column, HD), tile), up_low)
-        down_out[...] += dot_second(gate_low, gate_v[:, :, lanes].reshape(D, tile)) + dot_second(
-            up_low, up_v[:, :, lanes].reshape(D, tile)
-        )
+        inner_ref[:, lanes] = gate_low
+        up_low_ref[:, lanes] = up_low
         return carry
 
     lax.fori_loop(0, FF // tile, back_body, 0)
     mixed = hidden_grad_ref[...]
     attn_inverse = lax.rsqrt(jnp.mean(mixed * mixed, axis=-1, keepdims=True) + epsilon)
     normed = mixed * attn_inverse
-    hidden_grad = down_out[...]
+    hidden_grad = (
+        cot_ref[...].astype(f32)
+        + dot_second(inner_ref[...], gate_v[...].reshape(D, FF))
+        + dot_second(up_low_ref[...], up_v[...].reshape(D, FF))
+    )
     scaled = hidden_grad * attn_gain_ref[...]
     gain_grad_ref[0:1, :] = jnp.sum(hidden_grad * normed, axis=0, keepdims=True)
     mixed_low = (
@@ -803,7 +847,7 @@
             pltpu.VMEM((BLK, FF), f32),
             pltpu.VMEM((BLK, FF), f32),
             pltpu.VMEM((BLK, FF), bf16),
-            pltpu.VMEM((BLK, D), f32),
+            pltpu.VMEM((BLK, FF), bf16),
             pltpu.VMEM((BLK, D), f32),
             pltpu.SemaphoreType.DMA((22,)),
         ],
@@ -827,15 +871,32 @@
 
 
 PRODUCTS = (
-    (FF // 2, INNER_AT, D, DOWN_LOW_AT, "y", "01"),
-    (D, HIDDEN_AT, FF // 2, GATE_LOW_AT, "x", "01"),
-    (D, HIDDEN_AT, FF // 2, UP_LOW_AT, "x", "10"),
-    (HQ // 2, ATT_AT, D, MIXED_LOW_AT, "y", "10"),
+    (FF // 2, INNER_AT, D, DOWN_LOW_AT, "zB", "zA"),
+    (D, HIDDEN_AT, FF // 2, GATE_LOW_AT, "x0", "x1"),
+    (D, HIDDEN_AT, FF // 2, UP_LOW_AT, "x1", "x0"),
+    (HQ // 2, ATT_AT, D, MIXED_LOW_AT, "zA", "zB"),
 )
 
 
+def product_places():
+    places = []
+    for *_, first_link, second_link in PRODUCTS:
+        for first, second in ((1, 0), (1, 1), (0, 0), (0, 1)):
+            bits = {
+                first_link: link_bit(first_link) ^ first,
+                second_link: link_bit(second_link) ^ second,
+            }
+            for part in range(2):
+                if "zA" in bits:
+                    places.append((bits["zB"] * 2 + bits["zA"]) * 2 + part)
+                else:
+                    places.append(part * 4 + ring_place((bits["x1"], bits["x0"])))
+    return jnp.stack(places).astype(jnp.int32)
+
+
 def products_kernel(places_ref, own_ref, got_ref, *refs):
-    outs, (both, left, sems), scratch = refs[:8], refs[8:11], refs[11:]
+    outs, (both, sems), lefts, scratch = refs[:8], refs[8:10], refs[10:13], refs[13:]
+    lefts = dict(zip((INNER_AT, HIDDEN_AT, ATT_AT), lefts))
     run_copies(
         [
             pltpu.make_async_copy(ref, both.at[pl.ds(core * BLK, BLK)], sems.at[8 + core])
@@ -846,77 +907,68 @@
         pltpu.make_async_copy(held, out, sems.at[number])
         for number, (held, out) in enumerate(zip(scratch, outs))
     ]
-    held = None
-    for number, (rows, left_at, width, right_at, _, _) in enumerate(PRODUCTS):
-        if left_at != held:
-            left[:rows] = both[:, left_at : left_at + rows].astype(f32).T.astype(bf16)
-            held = left_at
-        quarter = rows // 8
+    for left_at, left in lefts.items():
+        columns = slice(left_at, left_at + left.shape[0])
+        left[...] = both[:, columns].astype(f32).T.astype(bf16)
+    for number, (rows, left_at, width, right_at, *_) in enumerate(PRODUCTS):
+        left = lefts[left_at]
+        eighth = rows // 8
         for part in range(2):
             out = scratch[2 * number + part]
 
-            def body(step, carry):
-                place = places_ref[number * 4 + part * 2 + step // 2]
-                start = pl.multiple_of(((step % 2) * 4 + place) * quarter, quarter)
-                target = pl.ds(pl.multiple_of(step * quarter, quarter), quarter)
-                out[target] = dot_plain(
-                    left[pl.ds(start, quarter)], both[:, right_at : right_at + width]
-                ).astype(bf16)
-                return carry
-
-            lax.fori_loop(0, 4, body, 0)
+            starts = [
+                pl.multiple_of(places_ref[number * 8 + part * 4 + step] * eighth, eighth)
+                for step in range(4)
+            ]
+            picked = jnp.concatenate([left[pl.ds(start, eighth)] for start in starts])
+            out[...] = dot_plain(picked, both[:, right_at : right_at + width]).astype(bf16)
             copies[2 * number + part].start()
     for copy in copies:
         copy.wait()
 
 
 def weight_products(own, got):
-    places = []
-    for _, _, _, _, axis, order in PRODUCTS:
-        for first, second in ((1, 0), (1, 1), (0, 0), (0, 1)):
-            bits = {name: link_bit(axis + name) for name in "01"}
-            bits[order[0]] = bits[order[0]] ^ first
-            bits[order[1]] = bits[order[1]] ^ second
-            places.append(ring_place((bits["1"], bits["0"])))
-    flops = sum(2 * 2 * BLK * rows * width for rows, _, width, _, _, _ in PRODUCTS)
+    flops = sum(2 * 2 * BLK * rows * width for rows, _, width, *_ in PRODUCTS)
     return pl.pallas_call(
         products_kernel,
         name="weight_products",
         out_shape=[
             pltpu.HBM((rows // 2, width), bf16)
-            for rows, _, width, _, _, _ in PRODUCTS
+            for rows, _, width, *_ in PRODUCTS
             for _ in range(2)
         ],
         in_specs=[smem, hbm, hbm],
         out_specs=[hbm] * 8,
         scratch_shapes=[
             pltpu.VMEM((2 * BLK, PACK), bf16),
+            pltpu.SemaphoreType.DMA((10,)),
             pltpu.VMEM((FF // 2, 2 * BLK), bf16),
-            pltpu.SemaphoreType.DMA((10,)),
+            pltpu.VMEM((D, 2 * BLK), bf16),
+            pltpu.VMEM((HQ // 2, 2 * BLK), bf16),
         ]
         + [
             pltpu.VMEM((rows // 2, width), bf16)
-            for rows, _, width, _, _, _ in PRODUCTS
+            for rows, _, width, *_ in PRODUCTS
             for _ in range(2)
         ],
         compiler_params=pltpu.CompilerParams(vmem_limit_bytes=40 << 20),
         cost_estimate=pl.CostEstimate(flops=flops, bytes_accessed=16 << 20, transcendentals=0),
-    )(jnp.stack(places).astype(jnp.int32), *in_hbm(own, got))
+    )(product_places(), *in_hbm(own, got))
 
 
 def place_kernel(core_ref, chunk_ref, *refs):
     gate_ref, up_ref, down_ref, out_ref = refs[-4:]
     for y in range(4):
-        for zl in range(2):
-            chunk = chunk_ref[y, 0, zl]
-            start = (2 * y + zl) * GATE_ROWS
+        for part in range(2):
+            chunk = chunk_ref[y, 0, part]
+            start = (2 * y + part) * GATE_ROWS
             rows = slice(start, start + GATE_ROWS)
             gate_ref[rows, :D] = chunk[:16].astype(f32)
             gate_ref[rows, D:] = chunk[16:32, : D // 2].astype(f32)
             up_ref[rows, : D // 2] = chunk[16:32, D // 2 :].astype(f32)
             up_ref[rows, D // 2 :] = chunk[32:48].astype(f32)
-            down_ref[y, 24 * zl : 24 * zl + 24] = chunk[48:72].astype(f32)
-            out_ref[y, 16 * zl : 16 * zl + 16] = chunk[72:].astype(f32)
+            down_ref[part, y] = chunk[48:72].astype(f32)
+            out_ref[part, y] = chunk[72:].astype(f32)
 
 
 def place_rows(core, chunks, earlier):
@@ -924,7 +976,7 @@
         return (x, core[0])
 
     def rows(x, core):
-        return (core[0], x, 0)
+        return (core[0], 0, x, 0)
 
     return pl.pallas_call(
         place_kernel,
@@ -932,8 +984,8 @@
         out_shape=(
             jax.ShapeDtypeStruct((D // 2, FF), f32),
             jax.ShapeDtypeStruct((D // 2, FF), f32),
-            jax.ShapeDtypeStruct((8, 4 * 48, D), f32),
-            jax.ShapeDtypeStruct((8, 4 * 32, D), f32),
+            jax.ShapeDtypeStruct((4, 4, 4 * 24, D), f32),
+            jax.ShapeDtypeStruct((4, 4, 4 * 16, D), f32),
         ),
         grid_spec=pltpu.PrefetchScalarGridSpec(
             num_scalar_prefetch=1,
@@ -943,8 +995,8 @@
             out_specs=[
                 pl.BlockSpec((D // 8, FF // 2), columns),
                 pl.BlockSpec((D // 8, FF // 2), columns),
-                pl.BlockSpec((4, 48, D), rows),
-                pl.BlockSpec((4, 32, D), rows),
+                pl.BlockSpec((2, 4, 24, D), rows),
+                pl.BlockSpec((2, 4, 16, D), rows),
             ],
         ),
         input_output_aliases={2 + number: number for number in range(len(earlier))},
@@ -1110,8 +1162,8 @@
     sent_parts, rest_parts = products[0::2], products[1::2]
     grads, sent_parts = lax.optimization_barrier((grads, sent_parts))
     got_parts = [
-        across(sent, axis + order[0])
-        for sent, (_, _, _, _, axis, order) in zip(sent_parts, PRODUCTS)
+        across(sent, first_link)
+        for sent, (*_, first_link, _) in zip(sent_parts, PRODUCTS)
     ]
 
     query_grad, sent, kept = attention_backward(
@@ -1135,17 +1187,16 @@
         for half, (first, _) in enumerate(orders)
     ]
     second_got = [
-        across(part, axis + order[1])
-        for part, (_, _, _, _, axis, order) in zip(second_sent, PRODUCTS)
+        across(part, second_link) for part, (*_, second_link) in zip(second_sent, PRODUCTS)
     ]
 
-    def second_sum(number):
+    def second_sum(number, arrived):
         rest, part = rest_parts[number], got_parts[number]
         middle = rest.shape[0] // 2
         kept_part = rest[:middle].astype(f32) + part[:middle].astype(f32)
-        return (kept_part + second_got[number].astype(f32)).astype(bf16)
-
-    kv_got, second_got[1], second_got[2] = stage((kv_got, second_got[1], second_got[2]))
+        return (kept_part + arrived.astype(f32)).astype(bf16)
+
+    kv_got = stage(kv_got)
     kv_both = [
         kept[half, :2].astype(f32) + got[half, :2].astype(f32) + kv_got[half].astype(f32)
         for half in range(2)
@@ -1153,18 +1204,13 @@
     kv_got = [
         across(kv_both[half][1].astype(bf16), second) for half, (_, second) in enumerate(orders)
     ]
+    kv_got, second_got = stage((kv_got, second_got))
+    down_got, gate_got, up_got, out_got = second_got
     act_part = exchange(
-        jnp.concatenate([second_sum(1), second_sum(2)], axis=1).reshape(16, 16, FF),
+        jnp.concatenate([second_sum(1, gate_got), second_sum(2, up_got)], axis=1).reshape(
+            16, 16, FF
+        ),
         ("zh", "y", "zl"),
-    )
-    kv_got, act_part, second_got[0], second_got[3] = stage(
-        (kv_got, act_part, second_got[0], second_got[3])
-    )
-    rest_part = exchange(
-        jnp.concatenate(
-            [second_sum(0).reshape(16, 24, D), second_sum(3).reshape(16, 16, D)], axis=1
-        ),
-        ("zh", "x", "zl"),
     )
     kv_grad = jnp.concatenate(
         [both[0] + more.astype(f32) for both, more in zip(kv_both, kv_got)]
@@ -1175,38 +1221,24 @@
     means = projection_means(*operands)
     for link in ("x0", "x1", "zA"):
         means = means + across(means, link)
-    act_part = wide_rows(jnp.sum(act_part.astype(f32), axis=0).astype(bf16))
-    means, rest_part = stage((means, rest_part))
-    chunk = jnp.concatenate([act_part, jnp.sum(rest_part.astype(f32), axis=0).astype(bf16)])
-    chunk_got = across(chunk, "zA")
-    chunk = jnp.where(zl == 0, jnp.stack([chunk, chunk_got]), jnp.stack([chunk_got, chunk]))
-    chunks = lax.all_gather(chunk, ("y", "x"), axis=0, tiled=False).reshape(4, 4, 2, 88, D)
-    by_owner, head_gain_grad = projection_grads(*operands, means)
-    raw_low = by_owner.reshape(ROWS, 4 * HD)
-    group_tokens = group_tokens.reshape(ROWS, D)
-
-    def token_columns(side):
-        return jnp.concatenate(
-            [
-                lax.dynamic_slice_in_dim(group_tokens, part * 512 + side * 256, 256, 1)
-                for part in range(2)
-            ],
+    means, act_part, down_got, out_got = stage((means, act_part, down_got, out_got))
+    rest_part = exchange(
+        jnp.concatenate(
+            [second_sum(0, down_got).reshape(16, 24, D), second_sum(3, out_got).reshape(16, 16, D)],
             axis=1,
-        )
-
-    gain_sums = jnp.concatenate(
-        [
-            head_gain_grad,
-            norm_gain_grads.reshape(4, 4 * HD),
-            jnp.zeros((3, 4 * HD), f32),
-        ]
-    )
-    by_side = by_owner.reshape(4, 2, BLK, 4 * HD)
+        ),
+        ("y", "x"),
+    )
+
     x_high, x_low = x // 2, x % 2
-
-    def product(rows, part):
-        columns = head_weight[part * (D // 2) : (part + 1) * (D // 2)]
-        return dot_second(rows.reshape(4 * BLK, 4 * HD), columns)
+    heads_sent, heads_kept, gain_sums, left_sent, left, right_sent, right = projection_grads(
+        jnp.stack([co, x_high, zl]).astype(jnp.int32),
+        *operands,
+        means,
+        group_tokens,
+        head_weight,
+        norm_gain_grads,
+    )
 
     def pick(array, number):
         return lax.dynamic_index_in_dim(array, number, 0, keepdims=False)
@@ -1215,70 +1247,87 @@
         return pick(both, number).astype(f32), across(pick(both, 1 - number), link)
 
     def halves(both):
-        return both.astype(bf16).reshape(2, both.shape[0] // 2, D // 2)
-
-    heads_got = across(
-        jnp.concatenate(
-            [
-                dot_first(token_columns(1 - co), raw_low).astype(bf16),
-                high_low(gain_sums).reshape(16, 4 * HD),
-            ]
-        ),
-        "co",
-    )
-    left_sent = product(lax.dynamic_slice_in_dim(by_owner, (1 - x_high) * 4, 4, 0), 0)
-    left_got = across(left_sent.astype(bf16), "x1")
-    right_sent = product(lax.dynamic_index_in_dim(by_side, 1 - zl, 1, keepdims=False), 1)
-    right_got = across(right_sent.astype(bf16), "zA")
-    head_chunk = dot_first(token_columns(co), raw_low)
-    left = product(lax.dynamic_slice_in_dim(by_owner, x_high * 4, 4, 0), 0)
-    right = product(lax.dynamic_index_in_dim(by_side, zl, 1, keepdims=False), 1)
-    heads_got, left_got, right_got, head_chunk, left, right = stage(
-        (heads_got, left_got, right_got, head_chunk, left, right)
-    )
-    heads_got = heads_got.astype(f32)
-    gain_sums = gain_sums + heads_got[512:520] + heads_got[520:]
-    head_chunk = jnp.concatenate(
+        return both.astype(bf16).reshape(2, both.shape[0] // 2, *both.shape[1:])
+
+    def take_gains(got, kept, sums):
+        more = got[-16:].astype(f32)
+        return (kept + got[:-16].astype(f32)).astype(bf16), sums + more[:8] + more[8:]
+
+    def with_gains(array, sums):
+        return jnp.concatenate([array, high_low(sums).reshape(16, 4 * HD)])
+
+    def halve_heads(chunk, sums, link):
+        bit = link_bit(link)
+        chunk = chunk.reshape(2, chunk.shape[0] // 2, 4 * HD)
+        kept = pick(chunk, bit).astype(f32)
+        return kept, across(with_gains(pick(chunk, 1 - bit), sums), link)
+
+    heads_got = across(heads_sent, "co")
+    left_got = across(left_sent, "x1")
+    right_got = across(right_sent, "zA")
+    heads_got, left_got, right_got = stage((heads_got, left_got, right_got))
+    rest_part, _ = stage((rest_part, heads_sent))
+    chunk = jnp.concatenate(
         [
-            (head_chunk + heads_got[:512]).astype(bf16).reshape(8, 64, 4 * HD),
+            wide_rows(jnp.sum(act_part.astype(f32), axis=0).astype(bf16)),
+            jnp.sum(rest_part.astype(f32), axis=0).astype(bf16),
+        ]
+    )
+    chunk_got = across(chunk, "zA")
+    def beside(start, stop, bit):
+        mine, other = chunk[start:stop], chunk_got[start:stop]
+        return jnp.where(bit == 0, jnp.stack([mine, other]), jnp.stack([other, mine]))
+
+    chunks = lax.all_gather(
+        jnp.concatenate([beside(0, 48, zl), beside(48, 88, link_bit("zA"))], axis=1),
+        ("y", "x"),
+        axis=0,
+        tiled=False,
+    ).reshape(4, 4, 2, 88, D)
+    heads, gain_sums = take_gains(heads_got, heads_kept, gain_sums)
+    heads = jnp.concatenate(
+        [
+            heads.reshape(8, 64, 4 * HD),
             jnp.broadcast_to(high_low(gain_sums).reshape(1, 16, 4 * HD), (8, 16, 4 * HD)),
         ],
         axis=1,
     )
-    head_chunk = exchange(head_chunk, ("zh", "y"))
-    left, left_got = pass_on(halves(left + left_got.astype(f32)), "x0", x_low)
-    right, right_got = pass_on(halves(right + right_got.astype(f32)), "x1", x_high)
-    head_chunk, left_got, right_got = stage((head_chunk, left_got, right_got))
-    head_chunk = jnp.sum(head_chunk.astype(f32), axis=0)
-    gain_sums = head_chunk[64:72] + head_chunk[72:]
-    head_chunk = jnp.concatenate(
-        [head_chunk[:64].astype(bf16), high_low(gain_sums).reshape(16, 4 * HD)]
-    )
-    mine = gather_all(head_chunk, ("y", "x", "zl"), 32)
+    heads = exchange(heads, ("zh", "y"))
+    left, left_got = pass_on(halves(left.astype(f32) + left_got.astype(f32)), "x0", x_low)
+    right, right_got = pass_on(halves(right.astype(f32) + right_got.astype(f32)), "x1", x_high)
+    heads, left_got, right_got = stage((heads, left_got, right_got))
+
+    heads = jnp.sum(heads.astype(f32), axis=0)
+    gain_sums = heads[64:72] + heads[72:]
+    heads = jnp.concatenate([heads[:64].astype(bf16), high_low(gain_sums).reshape(16, 4 * HD)])
+    heads = gather_all(heads, ("y", "x", "zl"), 32).reshape(4, 8, 80, 4 * HD)
     left, left_got = pass_on(halves(left + left_got.astype(f32)), "zA", zl)
     right, right_got = pass_on(halves(right + right_got.astype(f32)), "x0", x_low)
-    mine, left_got, right_got = stage((mine, left_got, right_got))
     tokens_grad = hidden_grad + jnp.concatenate(
-        [left + left_got.astype(f32), right + right_got.astype(f32)], axis=1
-    )
-
-    mine = mine.reshape(4, 8, 80, 4 * HD)
-    other_heads = across(mine, "co")
-    placed_heads = place_heads(own_core, mine, ())
+        [
+            (left + left_got.astype(f32)).reshape(BLK, D // 2),
+            (right + right_got.astype(f32)).reshape(BLK, D // 2),
+        ],
+        axis=1,
+    )
+    heads, tokens_grad = stage((heads, tokens_grad))
+    other_heads = across(heads, "co")
+    placed_heads = place_heads(own_core, heads, ())
     query_weight_grad, key_weight_grad, value_weight_grad = place_heads(
         other_core, other_heads, placed_heads
     )
-    gain_sums = mine[0, :, 64:72].astype(f32) + mine[0, :, 72:].astype(f32)
+    chunks, query_weight_grad = stage((chunks, query_weight_grad))
+    other_chunks = across(chunks, "co")
+    placed = place_rows(own_core, chunks, ())
+    gate_weight_grad, up_weight_grad, down_weight_grad, out_weight_grad = place_rows(
+        other_core, other_chunks, placed
+    )
+    down_weight_grad = down_weight_grad.reshape(FF // 2, D)
+    out_weight_grad = out_weight_grad.reshape(HQ // 2, D)
+    gain_sums = heads[0, :, 64:72].astype(f32) + heads[0, :, 72:].astype(f32)
     query_gain_grad = gain_sums[:, 0, : 2 * HD].reshape(HQ)
     key_gain_grad = gain_sums[:, 0, 2 * HD : 3 * HD].reshape(HK)
     norm_gain_grads = jnp.sum(gain_sums[:, 1:5], axis=0).reshape(2, D)
-    chunks, query_weight_grad, tokens_grad = stage((chunks, query_weight_grad, tokens_grad))
-    placed = place_rows(own_core, chunks, ())
-    gate_weight_grad, up_weight_grad, down_weight_grad, out_weight_grad = place_rows(
-        other_core, across(chunks, "co"), placed
-    )
-    down_weight_grad = down_weight_grad.reshape(FF // 2, D)
-    out_weight_grad = out_weight_grad.reshape(HQ // 2, D)
 
     def own_gain(gain_grad):
         size = gain_grad.shape[0] // 2

time: 509 us -> 481 us (0.945)
  waiting for transfers between devices: 187 us -> 174 us
  other arithmetic: 32.8 us -> 24.8 us
  local copies, waits for them, and re-layouts: 34.7 us -> 42.3 us
  starting transfers between devices: 99.6 us -> 94.4 us
    ppermute x38, waiting for transfers between devices: 150 us -> 129 us  [across(): return lax.ppermute(array, axis, pairs)]
    unnamed x121 -> x133, local copies, waits for them, and re-layouts: 21.6 us -> 32 us
    all_to_all x8, waiting for transfers between devices: 37.2 us -> 44.9 us  [exchange(): return lax.all_to_all(array, axes, 0, 0, tiled=True)]
    all_to_all x8, starting transfers between devices: 39.9 us -> 34.8 us  [exchange(): return lax.all_to_all(array, axes, 0, 0, tiled=True)]
  transfers between devices with their start and end apart: 48 -> 48, of which waited for: 26 -> 27; matrix products, arithmetic and copies ran while one was open for 7% -> 4% of each run, Pallas kernels for 18% -> 18%
where the time goes in v3:
time: 481 us; the launch traced here: 472 us
  waiting for transfers between devices  174 us (36%)
  Pallas kernels  120 us (25%)
  starting transfers between devices  94.4 us (20%)
  local copies, waits for them, and re-layouts  42.3 us (9%)
  other arithmetic  24.8 us (5%)
  between operations  16.9 us (4%)
    ppermute x38, waiting for transfers between devices, across(): return lax.ppermute(array, axis, pairs)  129 us
    ppermute x38, starting transfers between devices, across(): return lax.ppermute(array, axis, pairs)  59.3 us
    all_to_all x8, waiting for transfers between devices, exchange(): return lax.all_to_all(array, axes, 0, 0, tiled=True)  44.9 us
    all_to_all x8, starting transfers between devices, exchange(): return lax.all_to_all(array, axes, 0, 0, tiled=True)  34.8 us
    unnamed x133, local copies, waits for them, and re-layouts  32 us
    pallas_call x1, Pallas kernels, attention_backward(): pl.pallas_call(backward_kernel, name='attention_backward', out_shape=(jax...  31.7 us
    pallas_call x1, Pallas kernels, own_rows(): pl.pallas_call(rows_kernel, name='own_rows', out_shape=(shape(BLK, D), pl...  23.9 us
    pallas_call x1, Pallas kernels, attention_forward(): pl.pallas_call(forward_kernel, name='attention_forward', out_shape=(jax.S...  21.9 us
  transfers between devices with their start and end apart: 48, of which 27 were waited for; matrix products, arithmetic and copies ran while one was open for 4% of the time, Pallas kernels for 18%

profile of v3, /device:TPU:1, one launch (start us, length us, event | category | flops | bytes accessed | tf_op | source)
XLA Modules:
  0.0 472.4 jit_solution(3585524786399153700)
XLA Ops:
  14.9 4.7 collective-permute-start.1
  19.6 9.1 %collective-permute-done.1 = bf16[192,1024]{1,0:T(8,128)(2,1)S(1)} collective-permute-done((bf16[192,1024]{1,0:T(8,128)(2,1)}, bf16[192,1024]{1,0:T(8,128)(2,1)S(1)}, u32[]{:S(2)}, u32[]{:S(2)}) %collective-permute-start.1) | collective-permute-done | bytes 393248 | tf_op jit(solution)/shard_map/ppermute | solution.py:67
  29.5 4.0 all-to-all-start
  42.4 5.1 %collective-permute-done.got_ref = bf16[512,512]{1,0:T(8,128)(2,1)} collective-permute-done((bf16[512,512]{1,0:T(8,128)(2,1)}, bf16[512,512]{1,0:T(8,128)(2,1)}, u32[]{:S(2)}, u32[]{:S(2)}) %collective-permute-start) | collective-permute-done | bytes 524320 | tf_op jit(solution)/shard_map/ppermute | solution.py:67
  47.5 21.4 %all-to-all-done.tokens_ref = bf16[8,128,1024]{2,1,0:T(8,128)(2,1)S(1)} async-done(((bf16[8,128,1024]{2,1,0:T(8,128)(2,1)}), bf16[8,128,1024]{2,1,0:T(8,128)(2,1)S(1)}, u32[]{:S(2)}, u32[]{:S(2)}) %all-to-all-start) | async-done | bytes 2097184 | tf_op jit(solution)/shard_map/all_to_all | solution.py:87
  80.8 5.3 %all-to-all-done.1.squares_ref = f32[8,2,1024]{2,1,0:T(2,128)S(1)} async-done(((f32[8,2,1024]{2,1,0:T(2,128)}), f32[8,2,1024]{2,1,0:T(2,128)S(1)}, u32[]{:S(2)}, u32[]{:S(2)}) %all-to-all-start.1) | async-done | bytes 65568 | tf_op jit(solution)/shard_map/all_to_all | solution.py:87
  89.6 11.7 %collective-permute-done.4 = bf16[512,256]{1,0:T(8,128)(2,1)S(1)} collective-permute-done((bf16[512,256]{1,0:T(8,128)(2,1)S(1)}, bf16[512,256]{1,0:T(8,128)(2,1)S(1)}, u32[]{:S(2)}, u32[]{:S(2)}) %collective-permute-start.4) | collective-permute-done | bytes 262176 | tf_op jit(solution)/shard_map/ppermute | solution.py:67
  105.1 7.6 %collective-permute-done.5.refs_3_ = bf16[2,512,256]{2,1,0:T(8,128)(2,1)S(1)} collective-permute-done((bf16[2,512,256]{2,1,0:T(8,128)(2,1)S(1)}, bf16[2,512,256]{2,1,0:T(8,128)(2,1)S(1)}, u32[]{:S(2)}, u32[]{:S(2)}) %collective-permute-start.5) | collective-permute-done | bytes 524320 | tf_op jit(solution)/shard_map/ppermute | solution.py:67
  121.4 21.9 %attention_forward.1 = (bf16[8,2,64,256]{3,2,1,0:T(8,128)(2,1)S(1)}, f32[2,2,128,512]{3,2,1,0:T(8,128)S(1)}, f32[2,2,1,512]{3,2,1,0:T(1,128)S(1)}) custom-call(s32[4]{0:T(128)S(1)} %pad_add_fusion.2.info_ref, bf16[2,512,256]{2,1,0:T(8,128)(2,1)S(1)} %copy-done.24, bf16[2,512,256]{2,1,0:T(8,128)(2,1)} %copy-done.49, bf16[2,512,256]{2,1,0:T(8,128)(2,1)} %copy-done.60, ...), custom_call_target="tpu_custom_call" | custom-call | flops 9663676416 | bytes 8388608 | tf_op jit(solution)/shard_map/attention_forward/pallas_call | solution.py:362
  145.1 4.1 all-to-all-start.2
  149.4 9.0 %all-to-all-done.2.att_ref = bf16[8,2,64,256]{3,2,1,0:T(8,128)(2,1)} async-done(((bf16[8,2,64,256]{3,2,1,0:T(8,128)(2,1)}), bf16[8,2,64,256]{3,2,1,0:T(8,128)(2,1)}, u32[]{:S(2)}, u32[]{:S(2)}) %all-to-all-start.2) | async-done | bytes 524320 | tf_op jit(solution)/shard_map/all_to_all | solution.py:87
  159.4 23.9 %own_rows.1 = (bf16[128,1024]{1,0:T(8,128)(2,1)}, bf16[128,8704]{1,0:T(8,128)(2,1)}, bf16[128,8704]{1,0:T(8,128)(2,1)}, bf16[8,2,64,256]{3,2,1,0:T(8,128)(2,1)S(...) custom-call(s32[2]{0:T(128)S(1)} %pad_add_fusion.1.info_ref, bf16[8,2,64,256]{3,2,1,0:T(8,128)(2,1)} %all-to-all-done.2.att_ref, ...), custom_call_target="tpu_custom_call" | custom-call | flops 5905580032 | bytes 27262976 | tf_op jit(solution)/shard_map/own_rows/pallas_call | solution.py:827
  186.1 4.3 all-to-all-start.3
  190.6 10.0 %weight_products.1 = (bf16[768,1024]{1,0:T(8,128)(2,1)}, bf16[768,1024]{1,0:T(8,128)(2,1)}, bf16[512,1536]{1,0:T(8,128)(2,1)}, bf16[512,1536]{1,0:T(8,128)(2,1)}...) custom-call(s32[32]{0:T(128)S(1)} %stack.199.places_ref, ...), custom_call_target="tpu_custom_call" | custom-call | flops 2952790016 | bytes 16777216 | tf_op jit(solution)/shard_map/weight_products/pallas_call | solution.py:932
  209.0 31.7 %attention_backward.1 = (f32[2,512,256]{2,1,0:T(8,128)S(1)}, bf16[2,4,512,256]{3,2,1,0:T(8,128)(2,1)}, bf16[2,4,512,256]{3,2,1,0:T(8,128)(2,1)}) custom-call(s32[4]{0:T(128)S(1)} %pad_add_fusion.2.info_ref, bf16[2,512,256]{2,1,0:T(8,128)(2,1)S(1)} %copy-done.25, bf16[8,2,64,256]{3,2,1,0:T(8,128)(2,1)} %all-to-all-done.3.grad_ref, ...), custom_call_target="tpu_custom_call" | custom-call | flops 24159191040 | bytes 12582912 | tf_op jit(solution)/shard_map/attention_backward/pallas_call | solution.py:388
  252.8 8.1 %collective-permute-done.18 = bf16[2,512,256]{2,1,0:T(8,128)(2,1)S(1)} collective-permute-done((bf16[2,512,256]{2,1,0:T(8,128)(2,1)S(1)}, bf16[2,512,256]{2,1,0:T(8,128)(2,1)S(1)}, u32[]{:S(2)}, u32[]{:S(2)}) %collective-permute-start.18) | collective-permute-done | bytes 524320 | tf_op jit(solution)/shard_map/ppermute | solution.py:67
  264.7 4.1 collective-permute-done.21
  270.0 8.7 %collective-permute-done.23 = bf16[256,1536]{1,0:T(8,128)(2,1)S(1)} collective-permute-done((bf16[256,1536]{1,0:T(8,128)(2,1)S(1)}, bf16[256,1536]{1,0:T(8,128)(2,1)S(1)}, u32[]{:S(2)}, u32[]{:S(2)}) %collective-permute-start.23) | collective-permute-done | bytes 786464 | tf_op jit(solution)/shard_map/ppermute | solution.py:67
  281.1 4.4 all-to-all-start.4
  300.2 5.8 %all-to-all-done.4 = bf16[16,16,3072]{2,1,0:T(8,128)(2,1)} async-done(((bf16[16,16,3072]{2,1,0:T(8,128)(2,1)}), bf16[16,16,3072]{2,1,0:T(8,128)(2,1)}, u32[]{:S(2)}, u32[]{:S(2)}) %all-to-all-start.4) | async-done | bytes 1572896 | tf_op jit(solution)/shard_map/all_to_all | solution.py:87
  310.8 4.4 all-to-all-start.7
  322.5 5.8 %projection_grads.1 = (bf16[528,512]{1,0:T(8,128)(2,1)S(1)}, f32[512,512]{1,0:T(8,128)S(1)}, f32[8,512]{1,0:T(8,128)S(1)}, bf16[4,128,512]{2,1,0:T(8,128)(2,1)S(...) custom-call(s32[3]{0:T(128)S(1)} %pad_add_fusion.4.info_ref, ...), custom_call_target="tpu_custom_call" | custom-call | flops 4294967296 | bytes 16777216 | tf_op jit(solution)/shard_map/projection_grads/pallas_call | solution.py:653
  335.6 3.7 collective-permute-done.35
  341.7 5.6 %collective-permute-start.28 = (bf16[528,512]{1,0:T(8,128)(2,1)S(1)}, bf16[528,512]{1,0:T(8,128)(2,1)S(1)}, u32[]{:S(2)}, u32[]{:S(2)}) collective-permute-start(bf16[528,512]{1,0:T(8,128)(2,1)S(1)} %copy-done.22), channel_id=1, source_target_pairs={{0,2},{2,0},{1,3},{3,1},{4,6},{6,4},{5,7},{7,5},{8,10},{10,8},{9,1... | collective-permute-start | bytes 1622024 | tf_op jit(solution)/shard_map/ppermute | solution.py:67
  350.4 13.5 %collective-permute-done.29 = bf16[4,128,512]{2,1,0:T(8,128)(2,1)} collective-permute-done((bf16[4,128,512]{2,1,0:T(8,128)(2,1)S(1)}, bf16[4,128,512]{2,1,0:T(8,128)(2,1)}, u32[]{:S(2)}, u32[]{:S(2)}) %collective-permute-start.29) | collective-permute-done | bytes 524320 | tf_op jit(solution)/shard_map/ppermute | solution.py:67
  365.0 4.5 all-to-all-start.5
  384.1 5.7 %all-to-all-start.6 = ((bf16[32,80,512]{2,1,0:T(8,128)(2,1)}), bf16[32,80,512]{2,1,0:T(8,128)(2,1)S(1)}, u32[]{:S(2)}, u32[]{:S(2)}) async-start(bf16[32,80,512]{2,1,0:T(8,128)(2,1)} %broadcast_in_dim.56), calls=%async_computation.6 | async-start | bytes 5242880 | tf_op jit(solution)/shard_map/all_to_all | solution.py:87
  393.7 38.7 %collective-permute-done.34 = bf16[1,128,512]{2,1,0:T(8,128)(2,1)S(1)} collective-permute-done((bf16[1,128,512]{2,1,0:T(8,128)(2,1)S(1)}, bf16[1,128,512]{2,1,0:T(8,128)(2,1)S(1)}, u32[]{:S(2)}, u32[]{:S(2)}) %collective-permute-start.34) | collective-permute-done | bytes 131104 | tf_op jit(solution)/shard_map/ppermute | solution.py:67
  434.5 4.1 collective-permute-start.36
  443.3 4.3 place_heads.3
  453.2 4.6 place_rows.2
  457.8 7.3 %place_rows.3 = (f32[512,3072]{1,0:T(8,128)}, f32[512,3072]{1,0:T(8,128)}, f32[4,4,96,1024]{3,2,1,0:T(8,128)}, f32[4,4,64,1024]{3,2,1,0:T(8,128)}) custom-call(s32[1]{0:T(128)} %bitcast.74.core_ref, bf16[4,4,2,88,1024]{4,3,2,1,0:T(8,128)(2,1)} %collective-permute-done.37.chunk_ref, ...), custom_call_target="tpu_custom_call", output_to_operand_aliasing={{0}: (2, {}), {1}: (3, {}), {2}: (4, {}), {3}: (5, {})} | custom-call | flops 3145728 | bytes 18874368 | tf_op jit(solution)/shard_map/place_rows/pallas_call | solution.py:981
  (304 shorter events, 148.7 us)
Async XLA Ops:
  7.2 111.8 %all-gather.5.cloned.1.call-start = ((), (), s32[]{:S(2)}) async-start(), calls=%async_computation.8 | async-start | bytes 6127616 | tf_op jit(solution)/shard_map/all_gather | solution.py:1089
  14.9 13.7 %collective-permute-start.1 = (bf16[192,1024]{1,0:T(8,128)(2,1)}, bf16[192,1024]{1,0:T(8,128)(2,1)S(1)}, u32[]{:S(2)}, u32[]{:S(2)}) collective-permute-start(bf16[192,1024]{1,0:T(8,128)(2,1)} %get-tuple-element.117), channel_id=1, source_target_pairs={{0,5},{5,0},{1,4},{4,1},{2,7},{7,2},{3,6},{6,3},{8,13},{13,8},{9,1... | collective-permute-start | bytes 1179656 | tf_op jit(solution)/shard_map/ppermute | solution.py:67
  29.5 39.4 %all-to-all-start = ((bf16[8,128,1024]{2,1,0:T(8,128)(2,1)}), bf16[8,128,1024]{2,1,0:T(8,128)(2,1)S(1)}, u32[]{:S(2)}, u32[]{:S(2)}) async-start(bf16[8,128,1024]{2,1,0:T(8,128)(2,1)} %broadcast_in_dim.49), calls=%async_computation | async-start | bytes 4194304 | tf_op jit(solution)/shard_map/all_to_all | solution.py:87
  33.5 14.0 %collective-permute-start = (bf16[512,512]{1,0:T(8,128)(2,1)}, bf16[512,512]{1,0:T(8,128)(2,1)}, u32[]{:S(2)}, u32[]{:S(2)}) collective-permute-start(bf16[512,512]{1,0:T(8,128)(2,1)} %get-tuple-element.114), channel_id=1, source_target_pairs={{0,5},{5,0},{1,4},{4,1},{2,7},{7,2},{3,6},{6,3},{8,13},{13,8},{9,1... | collective-permute-start | bytes 1572872 | tf_op jit(solution)/shard_map/ppermute | solution.py:67
  87.0 14.3 %collective-permute-start.4 = (bf16[512,256]{1,0:T(8,128)(2,1)S(1)}, bf16[512,256]{1,0:T(8,128)(2,1)S(1)}, u32[]{:S(2)}, u32[]{:S(2)}) collective-permute-start(bf16[512,256]{1,0:T(8,128)(2,1)S(1)} %get-tuple-element.217), channel_id=1, source_target_pairs={{32,64},{64,32},{96,0},{0,96},{33,65},{65,33},{97,1},{1,97},{34,66... | collective-permute-start | bytes 786440 | tf_op jit(solution)/shard_map/ppermute | solution.py:67
  101.6 14.2 %collective-permute-start.3 = (bf16[2,512,256]{2,1,0:T(8,128)(2,1)S(1)}, bf16[2,512,256]{2,1,0:T(8,128)(2,1)S(1)}, u32[]{:S(2)}, u32[]{:S(2)}) collective-permute-start(bf16[2,512,256]{2,1,0:T(8,128)(2,1)S(1)} %pad_maximum_fusion.6.refs_0_), channel_id=1, source_target_pairs={{32,64},{64,32},{96,0},{0,96},{33,65},{65,33},{97,1},{1,97},{34,66... | collective-permute-start | bytes 1572872 | tf_op jit(solution)/shard_map/ppermute | solution.py:67
  103.2 14.0 %collective-permute-start.8 = (bf16[2,512,256]{2,1,0:T(8,128)(2,1)S(1)}, bf16[2,512,256]{2,1,0:T(8,128)(2,1)S(1)}, u32[]{:S(2)}, u32[]{:S(2)}) collective-permute-start(bf16[2,512,256]{2,1,0:T(8,128)(2,1)S(1)} %pad_maximum_fusion.7.refs_2_), channel_id=1, source_target_pairs={{0,2},{2,0},{1,3},{3,1},{4,6},{6,4},{5,7},{7,5},{8,10},{10,8},{9,1... | collective-permute-start | bytes 1572872 | tf_op jit(solution)/shard_map/ppermute | solution.py:67
  119.0 39.4 %collective-permute-start.10 = (bf16[16,176,1024]{2,1,0:T(8,128)(2,1)}, bf16[16,176,1024]{2,1,0:T(8,128)(2,1)}, u32[]{:S(2)}, u32[]{:S(2)}) collective-permute-start(bf16[16,176,1024]{2,1,0:T(8,128)(2,1)} %bitcast.140), channel_id=1, source_target_pairs={{0,2},{2,0},{1,3},{3,1},{4,6},{6,4},{5,7},{7,5},{8,10},{10,8},{9,1... | collective-permute-start | bytes 17301512 | tf_op jit(solution)/shard_map/ppermute | solution.py:67
  145.1 13.3 %all-to-all-start.2 = ((bf16[8,2,64,256]{3,2,1,0:T(8,128)(2,1)}), bf16[8,2,64,256]{3,2,1,0:T(8,128)(2,1)}, u32[]{:S(2)}, u32[]{:S(2)}) async-start(bf16[8,2,64,256]{3,2,1,0:T(8,128)(2,1)} %copy-done.19), calls=%async_computation.2 | async-start | bytes 1048576 | tf_op jit(solution)/shard_map/all_to_all | solution.py:87
  186.1 14.4 %all-to-all-start.3 = ((bf16[8,2,64,256]{3,2,1,0:T(8,128)(2,1)}), bf16[8,2,64,256]{3,2,1,0:T(8,128)(2,1)}, u32[]{:S(2)}, u32[]{:S(2)}) async-start(bf16[8,2,64,256]{3,2,1,0:T(8,128)(2,1)} %copy-done.18), calls=%async_computation.3 | async-start | bytes 1048576 | tf_op jit(solution)/shard_map/all_to_all | solution.py:87
  200.5 40.2 %collective-permute-start.15 = (bf16[512,1024]{1,0:T(8,128)(2,1)}, bf16[512,1024]{1,0:T(8,128)(2,1)S(1)}, u32[]{:S(2)}, u32[]{:S(2)}) collective-permute-start(bf16[512,1024]{1,0:T(8,128)(2,1)} %get-tuple-element.147), channel_id=1, source_target_pairs={{0,4},{4,0},{1,5},{5,1},{2,6},{6,2},{3,7},{7,3},{8,12},{12,8},{9,1... | collective-permute-start | bytes 3145736 | tf_op jit(solution)/shard_map/ppermute | solution.py:67
  202.0 38.8 %collective-permute-start.12 = (bf16[768,1024]{1,0:T(8,128)(2,1)}, bf16[768,1024]{1,0:T(8,128)(2,1)S(1)}, u32[]{:S(2)}, u32[]{:S(2)}) collective-permute-start(bf16[768,1024]{1,0:T(8,128)(2,1)} %get-tuple-element.144), channel_id=1, source_target_pairs={{0,5},{5,0},{1,4},{4,1},{2,7},{7,2},{3,6},{6,3},{8,13},{13,8},{9,1... | collective-permute-start | bytes 4718600 | tf_op jit(solution)/shard_map/ppermute | solution.py:67
  203.6 37.2 %collective-permute-start.13 = (bf16[512,1536]{1,0:T(8,128)(2,1)}, bf16[512,1536]{1,0:T(8,128)(2,1)S(1)}, u32[]{:S(2)}, u32[]{:S(2)}) collective-permute-start(bf16[512,1536]{1,0:T(8,128)(2,1)} %get-tuple-element.145), channel_id=1, source_target_pairs={{0,8},{8,0},{16,24},{24,16},{1,9},{9,1},{17,25},{25,17},{2,10},{10... | collective-permute-start | bytes 4718600 | tf_op jit(solution)/shard_map/ppermute | solution.py:67
  204.9 36.2 %collective-permute-start.14 = (bf16[512,1536]{1,0:T(8,128)(2,1)}, bf16[512,1536]{1,0:T(8,128)(2,1)S(1)}, u32[]{:S(2)}, u32[]{:S(2)}) collective-permute-start(bf16[512,1536]{1,0:T(8,128)(2,1)} %get-tuple-element.146), channel_id=1, source_target_pairs={{8,16},{16,8},{24,0},{0,24},{9,17},{17,9},{25,1},{1,25},{10,18},{1... | collective-permute-start | bytes 4718600 | tf_op jit(solution)/shard_map/ppermute | solution.py:67
  247.7 13.2 %collective-permute-start.18 = (bf16[2,512,256]{2,1,0:T(8,128)(2,1)S(1)}, bf16[2,512,256]{2,1,0:T(8,128)(2,1)S(1)}, u32[]{:S(2)}, u32[]{:S(2)}) collective-permute-start(bf16[2,512,256]{2,1,0:T(8,128)(2,1)S(1)} %get-tuple-element.213), channel_id=1, source_target_pairs={{0,32},{32,0},{64,96},{96,64},{1,33},{33,1},{65,97},{97,65},{2,34}... | collective-permute-start | bytes 1572872 | tf_op jit(solution)/shard_map/ppermute | solution.py:67
  248.3 14.0 %collective-permute-start.17 = (bf16[2,512,256]{2,1,0:T(8,128)(2,1)S(1)}, bf16[2,512,256]{2,1,0:T(8,128)(2,1)S(1)}, u32[]{:S(2)}, u32[]{:S(2)}) collective-permute-start(bf16[2,512,256]{2,1,0:T(8,128)(2,1)S(1)} %get-tuple-element.214), channel_id=1, source_target_pairs={{32,64},{64,32},{96,0},{0,96},{33,65},{65,33},{97,1},{1,97},{34,66... | collective-permute-start | bytes 1572872 | tf_op jit(solution)/shard_map/ppermute | solution.py:67
  250.0 14.6 %collective-permute-start.24 = (bf16[256,1024]{1,0:T(8,128)(2,1)S(1)}, bf16[256,1024]{1,0:T(8,128)(2,1)S(1)}, u32[]{:S(2)}, u32[]{:S(2)}) collective-permute-start(bf16[256,1024]{1,0:T(8,128)(2,1)S(1)} %add_convert_fusion.12), channel_id=1, source_target_pairs={{0,5},{5,0},{1,4},{4,1},{2,7},{7,2},{3,6},{6,3},{8,13},{13,8},{9,1... | collective-permute-start | bytes 1572872 | tf_op jit(solution)/shard_map/ppermute | solution.py:67
  251.0 17.8 %collective-permute-start.21 = (bf16[384,1024]{1,0:T(8,128)(2,1)S(1)}, bf16[384,1024]{1,0:T(8,128)(2,1)S(1)}, u32[]{:S(2)}, u32[]{:S(2)}) collective-permute-start(bf16[384,1024]{1,0:T(8,128)(2,1)S(1)} %add_convert_fusion.5), channel_id=1, source_target_pairs={{0,4},{4,0},{1,5},{5,1},{2,6},{6,2},{3,7},{7,3},{8,12},{12,8},{9,1... | collective-permute-start | bytes 2359304 | tf_op jit(solution)/shard_map/ppermute | solution.py:67
  251.0 19.0 %collective-permute-start.22 = (bf16[256,1536]{1,0:T(8,128)(2,1)S(1)}, bf16[256,1536]{1,0:T(8,128)(2,1)S(1)}, u32[]{:S(2)}, u32[]{:S(2)}) collective-permute-start(bf16[256,1536]{1,0:T(8,128)(2,1)S(1)} %add_convert_fusion.4), channel_id=1, source_target_pairs={{8,16},{16,8},{24,0},{0,24},{9,17},{17,9},{25,1},{1,25},{10,18},{1... | collective-permute-start | bytes 2359304 | tf_op jit(solution)/shard_map/ppermute | solution.py:67
  260.9 17.8 %collective-permute-start.23 = (bf16[256,1536]{1,0:T(8,128)(2,1)S(1)}, bf16[256,1536]{1,0:T(8,128)(2,1)S(1)}, u32[]{:S(2)}, u32[]{:S(2)}) collective-permute-start(bf16[256,1536]{1,0:T(8,128)(2,1)S(1)} %add_convert_fusion.3), channel_id=1, source_target_pairs={{0,8},{8,0},{16,24},{24,16},{1,9},{9,1},{17,25},{25,17},{2,10},{10... | collective-permute-start | bytes 2359304 | tf_op jit(solution)/shard_map/ppermute | solution.py:67
  262.8 15.9 %collective-permute-start.20 = (bf16[512,256]{1,0:T(8,128)(2,1)S(1)}, bf16[512,256]{1,0:T(8,128)(2,1)S(1)}, u32[]{:S(2)}, u32[]{:S(2)}) collective-permute-start(bf16[512,256]{1,0:T(8,128)(2,1)S(1)} %fusion.7), channel_id=1, source_target_pairs={{32,64},{64,32},{96,0},{0,96},{33,65},{65,33},{97,1},{1,97},{34,66... | collective-permute-start | bytes 786440 | tf_op jit(solution)/shard_map/ppermute | solution.py:67
  264.6 14.1 %collective-permute-start.19 = (bf16[512,256]{1,0:T(8,128)(2,1)S(1)}, bf16[512,256]{1,0:T(8,128)(2,1)S(1)}, u32[]{:S(2)}, u32[]{:S(2)}) collective-permute-start(bf16[512,256]{1,0:T(8,128)(2,1)S(1)} %fusion.6), channel_id=1, source_target_pairs={{0,32},{32,0},{64,96},{96,64},{1,33},{33,1},{65,97},{97,65},{2,34}... | collective-permute-start | bytes 786440 | tf_op jit(solution)/shard_map/ppermute | solution.py:67
  281.1 24.9 %all-to-all-start.4 = ((bf16[16,16,3072]{2,1,0:T(8,128)(2,1)}), bf16[16,16,3072]{2,1,0:T(8,128)(2,1)}, u32[]{:S(2)}, u32[]{:S(2)}) async-start(bf16[16,16,3072]{2,1,0:T(8,128)(2,1)} %bitcast.138), calls=%async_computation.4 | async-start | bytes 3145728 | tf_op jit(solution)/shard_map/all_to_all | solution.py:87
  310.8 22.5 %all-to-all-start.7 = ((bf16[16,40,1024]{2,1,0:T(8,128)(2,1)}), bf16[16,40,1024]{2,1,0:T(8,128)(2,1)}, u32[]{:S(2)}, u32[]{:S(2)}) async-start(bf16[16,40,1024]{2,1,0:T(8,128)(2,1)} %pad_maximum_fusion.1), calls=%async_computation.7 | async-start | bytes 2621440 | tf_op jit(solution)/shard_map/all_to_all | solution.py:87
  315.2 132.4 %all-gather.7.cloned.1.call-start = ((), (), s32[]{:S(2)}) async-start(), calls=%async_computation.9 | async-start | bytes 6127616 | tf_op jit(solution)/shard_map/all_gather | solution.py:1281
  341.7 22.1 %collective-permute-start.28 = (bf16[528,512]{1,0:T(8,128)(2,1)S(1)}, bf16[528,512]{1,0:T(8,128)(2,1)S(1)}, u32[]{:S(2)}, u32[]{:S(2)}) collective-permute-start(bf16[528,512]{1,0:T(8,128)(2,1)S(1)} %copy-done.22), channel_id=1, source_target_pairs={{0,2},{2,0},{1,3},{3,1},{4,6},{6,4},{5,7},{7,5},{8,10},{10,8},{9,1... | collective-permute-start | bytes 1622024 | tf_op jit(solution)/shard_map/ppermute | solution.py:67
  347.3 16.5 %collective-permute-start.29 = (bf16[4,128,512]{2,1,0:T(8,128)(2,1)S(1)}, bf16[4,128,512]{2,1,0:T(8,128)(2,1)}, u32[]{:S(2)}, u32[]{:S(2)}) collective-permute-start(bf16[4,128,512]{2,1,0:T(8,128)(2,1)S(1)} %copy-done.30), channel_id=1, source_target_pairs={{8,16},{16,8},{24,0},{0,24},{9,17},{17,9},{25,1},{1,25},{10,18},{1... | collective-permute-start | bytes 1572872 | tf_op jit(solution)/shard_map/ppermute | solution.py:67
  350.0 13.8 %collective-permute-start.30 = (bf16[4,128,512]{2,1,0:T(8,128)(2,1)S(1)}, bf16[4,128,512]{2,1,0:T(8,128)(2,1)}, u32[]{:S(2)}, u32[]{:S(2)}) collective-permute-start(bf16[4,128,512]{2,1,0:T(8,128)(2,1)S(1)} %copy-done.28), channel_id=1, source_target_pairs={{0,4},{4,0},{1,5},{5,1},{2,6},{6,2},{3,7},{7,3},{8,12},{12,8},{9,1... | collective-permute-start | bytes 1572872 | tf_op jit(solution)/shard_map/ppermute | solution.py:67
  365.0 17.2 %all-to-all-start.5 = ((bf16[8,80,512]{2,1,0:T(8,128)(2,1)}), bf16[8,80,512]{2,1,0:T(8,128)(2,1)S(1)}, u32[]{:S(2)}, u32[]{:S(2)}) async-start(bf16[8,80,512]{2,1,0:T(8,128)(2,1)} %pad_maximum_fusion.3), calls=%async_computation.5 | async-start | bytes 1310720 | tf_op jit(solution)/shard_map/all_to_all | solution.py:87
  384.1 50.4 %all-to-all-start.6 = ((bf16[32,80,512]{2,1,0:T(8,128)(2,1)}), bf16[32,80,512]{2,1,0:T(8,128)(2,1)S(1)}, u32[]{:S(2)}, u32[]{:S(2)}) async-start(bf16[32,80,512]{2,1,0:T(8,128)(2,1)} %broadcast_in_dim.56), calls=%async_computation.6 | async-start | bytes 5242880 | tf_op jit(solution)/shard_map/all_to_all | solution.py:87
  391.0 41.3 %collective-permute-start.34 = (bf16[1,128,512]{2,1,0:T(8,128)(2,1)S(1)}, bf16[1,128,512]{2,1,0:T(8,128)(2,1)S(1)}, u32[]{:S(2)}, u32[]{:S(2)}) collective-permute-start(bf16[1,128,512]{2,1,0:T(8,128)(2,1)S(1)} %constant_dynamic-slice_fusion), channel_id=1, source_target_pairs={{0,8},{8,0},{16,24},{24,16},{1,9},{9,1},{17,25},{25,17},{2,10},{10... | collective-permute-start | bytes 393224 | tf_op jit(solution)/shard_map/ppermute | solution.py:67
  392.4 40.0 %collective-permute-start.33 = (bf16[1,128,512]{2,1,0:T(8,128)(2,1)S(1)}, bf16[1,128,512]{2,1,0:T(8,128)(2,1)S(1)}, u32[]{:S(2)}, u32[]{:S(2)}) collective-permute-start(bf16[1,128,512]{2,1,0:T(8,128)(2,1)S(1)} %constant_dynamic-slice_fusion.1), channel_id=1, source_target_pairs={{0,4},{4,0},{1,5},{5,1},{2,6},{6,2},{3,7},{7,3},{8,12},{12,8},{9,1... | collective-permute-start | bytes 393224 | tf_op jit(solution)/shard_map/ppermute | solution.py:67
  (80 other events, 531.2 us)
Sparse Core Ops, SparseCore 0:
  29.6 72.9 all-gather.4
  341.8 89.7 all-gather.6

commit v4 on v3

--- a/solution.py
+++ b/solution.py
@@ -487,11 +487,20 @@
     return tensor * cosine + pltpu.roll(tensor, HD // 2, 1) * sine
 
 
-def project_kernel(info_ref, tokens_ref, own_ref, got_ref, raw_ref, weight_ref, squares_ref):
+def project_kernel(
+    info_ref, tokens_hbm, own_ref, got_ref, raw_ref, weight_ref, squares_ref, tokens_ref, sems
+):
     zh = info_ref[0]
+    loads = [
+        pltpu.make_async_copy(tokens_hbm.at[owner], tokens_ref.at[owner], sems.at[owner])
+        for owner in range(8)
+    ]
+    for load in loads:
+        load.start()
     weight_ref[pl.ds(pl.multiple_of(zh * (D // 2), D // 2), D // 2)] = own_ref[...]
     weight_ref[pl.ds(pl.multiple_of((1 - zh) * (D // 2), D // 2), D // 2)] = got_ref[...]
     for owner in range(8):
+        loads[owner].wait()
         raw = dot_plain(tokens_ref[owner], weight_ref[...])
         for half in range(2):
             start = half * group_rows + owner * half_blk
@@ -514,13 +523,14 @@
             jax.ShapeDtypeStruct((D, 4 * HD), bf16),
             jax.ShapeDtypeStruct((8, 2, ROWS), f32),
         ),
-        in_specs=[smem] + [vmem] * 3,
+        in_specs=[smem, hbm, vmem, vmem],
         out_specs=[vmem] * 3,
+        scratch_shapes=[pltpu.VMEM((8, BLK, D), bf16), pltpu.SemaphoreType.DMA((8,))],
         compiler_params=pltpu.CompilerParams(vmem_limit_bytes=32 << 20),
         cost_estimate=pl.CostEstimate(
             flops=2 * ROWS * D * 4 * HD, bytes_accessed=6 << 20, transcendentals=0
         ),
-    )(info, tokens, own_slice, got_slice)
+    )(info, *in_hbm(tokens), own_slice, got_slice)
 
 
 def inverses(squares_ref):
@@ -588,11 +598,38 @@
 
 
 def raw_grad_kernel(
-    info_ref, raw_ref, squares_ref, cos_ref, sin_ref, gain_ref, dq_ref, dkv_ref, means_ref,
-    tokens_ref, weight_ref, norm_gains_ref,
-    heads_sent_ref, heads_kept_ref, gains_ref, left_sent_ref, left_kept_ref, right_sent_ref,
-    right_kept_ref, low_ref,
+    info_ref, squares_ref, gain_ref, dkv_ref, means_ref, norm_gains_ref,
+    raw_hbm, cos_hbm, sin_hbm, dq_hbm, tokens_hbm, weight_hbm,
+    gains_ref, *refs,
 ):
+    outs, held, (raw_ref, cos_ref, sin_ref, dq_ref, tokens_ref, weight_ref, low_ref, sems) = (
+        refs[:6],
+        refs[6:12],
+        refs[12:],
+    )
+    loads = [
+        pltpu.make_async_copy(source, target, sems.at[number])
+        for number, (source, target) in enumerate(
+            (
+                (raw_hbm, raw_ref),
+                (cos_hbm, cos_ref),
+                (sin_hbm, sin_ref),
+                (dq_hbm, dq_ref),
+                (tokens_hbm, tokens_ref),
+                (weight_hbm, weight_ref),
+            )
+        )
+    ]
+    for load in loads:
+        load.start()
+    stores = [
+        pltpu.make_async_copy(source, target, sems.at[6 + number])
+        for number, (source, target) in enumerate(zip(held, outs))
+    ]
+    heads_sent_ref, heads_kept_ref = held[:2]
+    left_sent_ref, left_kept_ref, right_sent_ref, right_kept_ref = held[2:]
+    for load in loads[:4]:
+        load.wait()
     co, x_high, zl = info_ref[0], info_ref[1], info_ref[2]
     means = (as_rows(means_ref[0:1]) / HQ, as_rows(means_ref[1:2]) / HK)
 
@@ -619,6 +656,8 @@
     high = gains.astype(bf16)
     heads_sent_ref[512:] = jnp.concatenate([high, (gains - high.astype(f32)).astype(bf16)])
 
+    for load in loads[4:]:
+        load.wait()
     low = low_ref[...].reshape(ROWS, 4 * HD)
     for part in range(2):
         rows = slice(part * 256, (part + 1) * 256)
@@ -626,6 +665,8 @@
             lanes = pl.ds(pl.multiple_of(part * 512 + side * 256, 256), 256)
             tokens = tokens_ref[:, :, lanes].reshape(ROWS, 256)
             ref[rows] = dot_first(tokens, low).astype(ref.dtype)
+    stores[0].start()
+    stores[1].start()
 
     for number in range(4):
         for ref, side in ((left_sent_ref, 1 - x_high), (left_kept_ref, x_high)):
@@ -634,6 +675,10 @@
         for ref, side in ((right_sent_ref, 1 - zl), (right_kept_ref, zl)):
             rows = low_ref[2 * number + side]
             ref[number] = dot_second(rows, weight_ref[D // 2 :]).astype(bf16)
+    for store in stores[2:]:
+        store.start()
+    for store in stores:
+        store.wait()
 
 
 def projection_means(*operands):
@@ -648,26 +693,24 @@
     )(*operands)
 
 
-def projection_grads(info, *operands):
-    part = jax.ShapeDtypeStruct((4, BLK, D // 2), bf16)
+def projection_grads(
+    info, raw, squares, cosine, sine, gain, dq, dkv, means, tokens, weight, norm_gains
+):
+    shapes = [((512 + 16, 4 * HD), bf16), ((512, 4 * HD), f32)] + [((4, BLK, D // 2), bf16)] * 4
+    large = (raw, cosine, sine, dq, tokens, weight)
     return pl.pallas_call(
         raw_grad_kernel,
         name="projection_grads",
-        out_shape=(
-            jax.ShapeDtypeStruct((512 + 16, 4 * HD), bf16),
-            jax.ShapeDtypeStruct((512, 4 * HD), f32),
-            jax.ShapeDtypeStruct((8, 4 * HD), f32),
-            part,
-            part,
-            part,
-            part,
-        ),
-        in_specs=[smem] + [vmem] * 11,
-        out_specs=[vmem] * 7,
-        scratch_shapes=[pltpu.VMEM((8, BLK, 4 * HD), bf16)],
+        out_shape=[jax.ShapeDtypeStruct((8, 4 * HD), f32)]
+        + [pltpu.HBM(shape, dtype) for shape, dtype in shapes],
+        in_specs=[smem] + [vmem] * 5 + [hbm] * 6,
+        out_specs=[vmem] + [hbm] * 6,
+        scratch_shapes=[pltpu.VMEM(shape, dtype) for shape, dtype in shapes]
+        + [pltpu.VMEM(array.shape, array.dtype) for array in large]
+        + [pltpu.VMEM((8, BLK, 4 * HD), bf16), pltpu.SemaphoreType.DMA((12,))],
         compiler_params=pltpu.CompilerParams(vmem_limit_bytes=40 << 20),
         cost_estimate=pl.CostEstimate(flops=4 << 30, bytes_accessed=16 << 20, transcendentals=0),
-    )(info, *operands)
+    )(info, squares, gain, dkv, means, norm_gains, *in_hbm(*large))
 
 
 INNER_AT = 0
@@ -1005,16 +1048,17 @@
     )(core, chunks, *earlier)
 
 
-def place_heads_kernel(core_ref, chunk_ref, *refs):
+def place_heads_kernel(core_ref, query_chunk_ref, rest_chunk_ref, *refs):
     query_ref, key_ref, value_ref = refs[-3:]
     for owner in range(8):
-        part = chunk_ref[0, owner, :64].astype(f32)
-        query_ref[:, owner * 2 * HD : (owner + 1) * 2 * HD] = part[:, : 2 * HD]
-        key_ref[:, owner * HD : (owner + 1) * HD] = part[:, 2 * HD : 3 * HD]
-        value_ref[:, owner * HD : (owner + 1) * HD] = part[:, 3 * HD :]
-
-
-def place_heads(core, chunks, earlier):
+        query = query_chunk_ref[owner // 2, 0, owner % 2, :64].astype(f32)
+        rest = rest_chunk_ref[0, owner // 2, owner % 2, :64].astype(f32)
+        query_ref[:, owner * 2 * HD : (owner + 1) * 2 * HD] = query
+        key_ref[:, owner * HD : (owner + 1) * HD] = rest[:, :HD]
+        value_ref[:, owner * HD : (owner + 1) * HD] = rest[:, HD:]
+
+
+def place_heads(core, query, rest, earlier):
     def rows(y, core):
         return (core[0] * 4 + y, 0)
 
@@ -1029,7 +1073,10 @@
         grid_spec=pltpu.PrefetchScalarGridSpec(
             num_scalar_prefetch=1,
             grid=(4,),
-            in_specs=[pl.BlockSpec((1, 8, 80, 4 * HD), lambda y, core: (y, 0, 0, 0))]
+            in_specs=[
+                pl.BlockSpec((4, 1, 2, 80, 2 * HD), lambda y, core: (0, y, 0, 0, 0)),
+                pl.BlockSpec((1, 4, 2, 80, 2 * HD), lambda y, core: (y, 0, 0, 0, 0)),
+            ]
             + [hbm] * len(earlier),
             out_specs=[
                 pl.BlockSpec((64, HQ), rows),
@@ -1037,10 +1084,10 @@
                 pl.BlockSpec((64, HK), rows),
             ],
         ),
-        input_output_aliases={2 + number: number for number in range(len(earlier))},
+        input_output_aliases={3 + number: number for number in range(len(earlier))},
         compiler_params=pltpu.CompilerParams(vmem_limit_bytes=32 << 20),
         cost_estimate=pl.CostEstimate(flops=1 << 20, bytes_accessed=6 << 20, transcendentals=0),
-    )(core, chunks, *earlier)
+    )(core, query, rest, *earlier)
 
 
 def per_device(
@@ -1204,7 +1251,14 @@
     kv_got = [
         across(kv_both[half][1].astype(bf16), second) for half, (_, second) in enumerate(orders)
     ]
-    kv_got, second_got = stage((kv_got, second_got))
+    kv_grad = jnp.concatenate(
+        [both[0] + more.astype(f32) for both, more in zip(kv_both, kv_got)]
+    )
+    operands = (
+        raw, squares, *tables, head_gain, query_grad.reshape(ROWS, 2 * HD), kv_grad,
+    )
+    means = projection_means(*operands)
+    second_got, _ = stage((second_got, means))
     down_got, gate_got, up_got, out_got = second_got
     act_part = exchange(
         jnp.concatenate([second_sum(1, gate_got), second_sum(2, up_got)], axis=1).reshape(
@@ -1212,13 +1266,6 @@
         ),
         ("zh", "y", "zl"),
     )
-    kv_grad = jnp.concatenate(
-        [both[0] + more.astype(f32) for both, more in zip(kv_both, kv_got)]
-    )
-    operands = (
-        raw, squares, *tables, head_gain, query_grad.reshape(ROWS, 2 * HD), kv_grad,
-    )
-    means = projection_means(*operands)
     for link in ("x0", "x1", "zA"):
         means = means + across(means, link)
     means, act_part, down_got, out_got = stage((means, act_part, down_got, out_got))
@@ -1231,7 +1278,7 @@
     )
 
     x_high, x_low = x // 2, x % 2
-    heads_sent, heads_kept, gain_sums, left_sent, left, right_sent, right = projection_grads(
+    gain_sums, heads_sent, heads_kept, left_sent, left, right_sent, right = projection_grads(
         jnp.stack([co, x_high, zl]).astype(jnp.int32),
         *operands,
         means,
@@ -1265,8 +1312,7 @@
     heads_got = across(heads_sent, "co")
     left_got = across(left_sent, "x1")
     right_got = across(right_sent, "zA")
-    heads_got, left_got, right_got = stage((heads_got, left_got, right_got))
-    rest_part, _ = stage((rest_part, heads_sent))
+    rest_part, heads_got = stage((rest_part, heads_got))
     chunk = jnp.concatenate(
         [
             wide_rows(jnp.sum(act_part.astype(f32), axis=0).astype(bf16)),
@@ -1296,11 +1342,15 @@
     left, left_got = pass_on(halves(left.astype(f32) + left_got.astype(f32)), "x0", x_low)
     right, right_got = pass_on(halves(right.astype(f32) + right_got.astype(f32)), "x1", x_high)
     heads, left_got, right_got = stage((heads, left_got, right_got))
-
     heads = jnp.sum(heads.astype(f32), axis=0)
     gain_sums = heads[64:72] + heads[72:]
     heads = jnp.concatenate([heads[:64].astype(bf16), high_low(gain_sums).reshape(16, 4 * HD)])
-    heads = gather_all(heads, ("y", "x", "zl"), 32).reshape(4, 8, 80, 4 * HD)
+    heads = double(heads[None], "zl")
+    head_query, head_rest = heads[:, :, : 2 * HD], heads[:, :, 2 * HD :]
+    for query_link, rest_link in (("y0", "x0"), ("y1", "x1"), ("x0", "y0"), ("x1", "y1")):
+        head_query, head_rest = double(head_query, query_link), double(head_rest, rest_link)
+    head_query = head_query.reshape(4, 4, 2, 80, 2 * HD)
+    head_rest = head_rest.reshape(4, 4, 2, 80, 2 * HD)
     left, left_got = pass_on(halves(left + left_got.astype(f32)), "zA", zl)
     right, right_got = pass_on(halves(right + right_got.astype(f32)), "x0", x_low)
     tokens_grad = hidden_grad + jnp.concatenate(
@@ -1310,24 +1360,35 @@
         ],
         axis=1,
     )
-    heads, tokens_grad = stage((heads, tokens_grad))
-    other_heads = across(heads, "co")
-    placed_heads = place_heads(own_core, heads, ())
-    query_weight_grad, key_weight_grad, value_weight_grad = place_heads(
-        other_core, other_heads, placed_heads
-    )
-    chunks, query_weight_grad = stage((chunks, query_weight_grad))
+    head_query, head_rest, tokens_grad, chunks = stage(
+        (head_query, head_rest, tokens_grad, chunks)
+    )
     other_chunks = across(chunks, "co")
+    other_heads = across(head_query, "co"), across(head_rest, "co")
     placed = place_rows(own_core, chunks, ())
+    placed_heads = place_heads(own_core, head_query, head_rest, ())
     gate_weight_grad, up_weight_grad, down_weight_grad, out_weight_grad = place_rows(
         other_core, other_chunks, placed
     )
+    query_weight_grad, key_weight_grad, value_weight_grad = place_heads(
+        other_core, *other_heads, placed_heads
+    )
     down_weight_grad = down_weight_grad.reshape(FF // 2, D)
     out_weight_grad = out_weight_grad.reshape(HQ // 2, D)
-    gain_sums = heads[0, :, 64:72].astype(f32) + heads[0, :, 72:].astype(f32)
-    query_gain_grad = gain_sums[:, 0, : 2 * HD].reshape(HQ)
-    key_gain_grad = gain_sums[:, 0, 2 * HD : 3 * HD].reshape(HK)
-    norm_gain_grads = jnp.sum(gain_sums[:, 1:5], axis=0).reshape(2, D)
+    def gain_of(rows):
+        return rows[..., 64, :].astype(f32) + rows[..., 72, :].astype(f32)
+
+    query_gain_grad = gain_of(head_query[:, 0]).reshape(HQ)
+    key_gain_grad = gain_of(head_rest[0])[..., :HD].reshape(HK)
+
+    def norm_gains(rows):
+        return jnp.sum(
+            rows[:, :, 65:69].astype(f32) + rows[:, :, 73:77].astype(f32), axis=(0, 1)
+        )
+
+    norm_gain_grads = jnp.concatenate(
+        [norm_gains(head_query[:, 0]), norm_gains(head_rest[0])], axis=1
+    ).reshape(2, D)
 
     def own_gain(gain_grad):
         size = gain_grad.shape[0] // 2

time: 481 us -> 464 us (0.965)
  local copies, waits for them, and re-layouts: 42.3 us -> 26.4 us
  other arithmetic: 24.8 us -> 19 us
  Pallas kernels: 120 us -> 125 us
    unnamed x133 -> x105, local copies, waits for them, and re-layouts: 32 us -> 18.8 us
    all_to_all x8 -> x7, waiting for transfers between devices: 44.9 us -> 52.3 us  [exchange(): return lax.all_to_all(array, axes, 0, 0, tiled=True)]
    ppermute x38 -> x48, waiting for transfers between devices: 129 us -> 124 us  [across(): return lax.ppermute(array, axis, pairs)]
    all_to_all x8 -> x7, starting transfers between devices: 34.8 us -> 31 us  [exchange(): return lax.all_to_all(array, axes, 0, 0, tiled=True)]
    ppermute x38 -> x48, starting transfers between devices: 59.3 us -> 59.9 us  [across(): return lax.ppermute(array, axis, pairs)]
  transfers between devices with their start and end apart: 48 -> 57, of which waited for: 27 -> 33; matrix products, arithmetic and copies ran while one was open for 4% -> 3% of each run, Pallas kernels for 18% -> 20%
where the time goes in v4:
time: 464 us; the launch traced here: 455 us
  waiting for transfers between devices  177 us (38%)
  Pallas kernels  125 us (27%)
  starting transfers between devices  91.1 us (20%)
  local copies, waits for them, and re-layouts  26.4 us (6%)
  other arithmetic  19 us (4%)
  between operations  17 us (4%)
    ppermute x48, waiting for transfers between devices, across(): return lax.ppermute(array, axis, pairs)  124 us
    ppermute x48, starting transfers between devices, across(): return lax.ppermute(array, axis, pairs)  59.9 us
    all_to_all x7, waiting for transfers between devices, exchange(): return lax.all_to_all(array, axes, 0, 0, tiled=True)  52.3 us
    pallas_call x1, Pallas kernels, attention_backward(): pl.pallas_call(backward_kernel, name='attention_backward', out_shape=(jax...  31.7 us
    all_to_all x7, starting transfers between devices, exchange(): return lax.all_to_all(array, axes, 0, 0, tiled=True)  31 us
    pallas_call x1, Pallas kernels, own_rows(): pl.pallas_call(rows_kernel, name='own_rows', out_shape=(shape(BLK, D), pl...  23.8 us
    pallas_call x1, Pallas kernels, attention_forward(): pl.pallas_call(forward_kernel, name='attention_forward', out_shape=(jax.S...  21.9 us
    unnamed x105, local copies, waits for them, and re-layouts  18.8 us
  transfers between devices with their start and end apart: 57, of which 33 were waited for; matrix products, arithmetic and copies ran while one was open for 3% of the time, Pallas kernels for 20%

profile of v4, /device:TPU:1, one launch (start us, length us, event | category | flops | bytes accessed | tf_op | source)
XLA Modules:
  0.0 455.5 jit_solution(11862443326381548390)
XLA Ops:
  14.3 4.7 %collective-permute-start.1 = (bf16[192,1024]{1,0:T(8,128)(2,1)}, bf16[192,1024]{1,0:T(8,128)(2,1)S(1)}, u32[]{:S(2)}, u32[]{:S(2)}) collective-permute-start(bf16[192,1024]{1,0:T(8,128)(2,1)} %get-tuple-element.113), channel_id=1, source_target_pairs={{0,5},{5,0},{1,4},{4,1},{2,7},{7,2},{3,6},{6,3},{8,13},{13,8},{9,1... | collective-permute-start | bytes 1179656 | tf_op jit(solution)/shard_map/ppermute | solution.py:67
  19.0 9.1 %collective-permute-done.1 = bf16[192,1024]{1,0:T(8,128)(2,1)S(1)} collective-permute-done((bf16[192,1024]{1,0:T(8,128)(2,1)}, bf16[192,1024]{1,0:T(8,128)(2,1)S(1)}, u32[]{:S(2)}, u32[]{:S(2)}) %collective-permute-start.1) | collective-permute-done | bytes 393248 | tf_op jit(solution)/shard_map/ppermute | solution.py:67
  28.8 4.5 all-to-all-start
  41.7 5.0 %collective-permute-done.got_ref = bf16[512,512]{1,0:T(8,128)(2,1)S(1)} collective-permute-done((bf16[512,512]{1,0:T(8,128)(2,1)S(1)}, bf16[512,512]{1,0:T(8,128)(2,1)S(1)}, u32[]{:S(2)}, u32[]{:S(2)}) %collective-permute-start) | collective-permute-done | bytes 524320 | tf_op jit(solution)/shard_map/ppermute | solution.py:67
  47.5 21.2 %all-to-all-done.tokens_hbm = bf16[8,128,1024]{2,1,0:T(8,128)(2,1)} async-done(((bf16[8,128,1024]{2,1,0:T(8,128)(2,1)}), bf16[8,128,1024]{2,1,0:T(8,128)(2,1)}, u32[]{:S(2)}, u32[]{:S(2)}) %all-to-all-start) | async-done | bytes 2097184 | tf_op jit(solution)/shard_map/all_to_all | solution.py:87
  70.8 4.6 %project.1 = (f32[1024,512]{1,0:T(8,128)S(1)}, bf16[1024,512]{1,0:T(8,128)(2,1)S(1)}, f32[8,2,1024]{2,1,0:T(2,128)}) custom-call(s32[1]{0:T(128)} %bitcast.info_ref, bf16[8,128,1024]{2,1,0:T(8,128)(2,1)} %all-to-all-done.tokens_hbm, bf16[512,512]{1,0:T(8,128)(2,1)S(1)} %copy-done.16, bf16[512,512]{1,0:T(8,128)(2,1)S(1)} %copy-done.18), custom_call_target="tpu_custom_call" | custom-call | flops 1073741824 | bytes 6291456 | tf_op jit(solution)/shard_map/project/pallas_call | solution.py:518
  79.7 5.3 %all-to-all-done.1.squares_ref = f32[8,2,1024]{2,1,0:T(2,128)S(1)} async-done(((f32[8,2,1024]{2,1,0:T(2,128)}), f32[8,2,1024]{2,1,0:T(2,128)S(1)}, u32[]{:S(2)}, u32[]{:S(2)}) %all-to-all-start.1) | async-done | bytes 65568 | tf_op jit(solution)/shard_map/all_to_all | solution.py:87
  88.7 7.9 %collective-permute-done.4 = bf16[512,256]{1,0:T(8,128)(2,1)S(1)} collective-permute-done((bf16[512,256]{1,0:T(8,128)(2,1)S(1)}, bf16[512,256]{1,0:T(8,128)(2,1)S(1)}, u32[]{:S(2)}, u32[]{:S(2)}) %collective-permute-start.4) | collective-permute-done | bytes 262176 | tf_op jit(solution)/shard_map/ppermute | solution.py:67
  100.7 7.5 %collective-permute-done.5.refs_3_ = bf16[2,512,256]{2,1,0:T(8,128)(2,1)S(1)} collective-permute-done((bf16[2,512,256]{2,1,0:T(8,128)(2,1)S(1)}, bf16[2,512,256]{2,1,0:T(8,128)(2,1)S(1)}, u32[]{:S(2)}, u32[]{:S(2)}) %collective-permute-start.5) | collective-permute-done | bytes 524320 | tf_op jit(solution)/shard_map/ppermute | solution.py:67
  116.8 21.9 %attention_forward.1 = (bf16[8,2,64,256]{3,2,1,0:T(8,128)(2,1)S(1)}, f32[2,2,128,512]{3,2,1,0:T(8,128)S(1)}, f32[2,2,1,512]{3,2,1,0:T(1,128)S(1)}) custom-call(s32[4]{0:T(128)S(1)} %pad_add_fusion.2.info_ref, bf16[2,512,256]{2,1,0:T(8,128)(2,1)S(1)} %copy-done.14, bf16[2,512,256]{2,1,0:T(8,128)(2,1)} %copy-done.36, bf16[2,512,256]{2,1,0:T(8,128)(2,1)} %copy-done.45, ...), custom_call_target="tpu_custom_call" | custom-call | flops 9663676416 | bytes 8388608 | tf_op jit(solution)/shard_map/attention_forward/pallas_call | solution.py:362
  140.4 5.2 %all-to-all-start.2 = ((bf16[8,2,64,256]{3,2,1,0:T(8,128)(2,1)}), bf16[8,2,64,256]{3,2,1,0:T(8,128)(2,1)}, u32[]{:S(2)}, u32[]{:S(2)}) async-start(bf16[8,2,64,256]{3,2,1,0:T(8,128)(2,1)} %copy-done.11), calls=%async_computation.2 | async-start | bytes 1048576 | tf_op jit(solution)/shard_map/all_to_all | solution.py:87
  145.8 9.2 %all-to-all-done.2.att_ref = bf16[8,2,64,256]{3,2,1,0:T(8,128)(2,1)} async-done(((bf16[8,2,64,256]{3,2,1,0:T(8,128)(2,1)}), bf16[8,2,64,256]{3,2,1,0:T(8,128)(2,1)}, u32[]{:S(2)}, u32[]{:S(2)}) %all-to-all-start.2) | async-done | bytes 524320 | tf_op jit(solution)/shard_map/all_to_all | solution.py:87
  155.9 23.8 %own_rows.1 = (bf16[128,1024]{1,0:T(8,128)(2,1)}, bf16[128,8704]{1,0:T(8,128)(2,1)}, bf16[128,8704]{1,0:T(8,128)(2,1)}, bf16[8,2,64,256]{3,2,1,0:T(8,128)(2,1)S(...) custom-call(s32[2]{0:T(128)S(1)} %pad_add_fusion.1.info_ref, bf16[8,2,64,256]{3,2,1,0:T(8,128)(2,1)} %all-to-all-done.2.att_ref, ...), custom_call_target="tpu_custom_call" | custom-call | flops 5905580032 | bytes 27262976 | tf_op jit(solution)/shard_map/own_rows/pallas_call | solution.py:870
  182.6 4.3 all-to-all-start.3
  187.1 10.0 %weight_products.1 = (bf16[768,1024]{1,0:T(8,128)(2,1)}, bf16[768,1024]{1,0:T(8,128)(2,1)}, bf16[512,1536]{1,0:T(8,128)(2,1)}, bf16[512,1536]{1,0:T(8,128)(2,1)}...) custom-call(s32[32]{0:T(128)S(1)} %stack.199.places_ref, ...), custom_call_target="tpu_custom_call" | custom-call | flops 2952790016 | bytes 16777216 | tf_op jit(solution)/shard_map/weight_products/pallas_call | solution.py:975
  205.2 31.7 %attention_backward.1 = (f32[2,512,256]{2,1,0:T(8,128)S(1)}, bf16[2,4,512,256]{3,2,1,0:T(8,128)(2,1)}, bf16[2,4,512,256]{3,2,1,0:T(8,128)(2,1)}) custom-call(s32[4]{0:T(128)S(1)} %pad_add_fusion.2.info_ref, bf16[2,512,256]{2,1,0:T(8,128)(2,1)S(1)} %copy-done.15, bf16[8,2,64,256]{3,2,1,0:T(8,128)(2,1)} %all-to-all-done.3.grad_ref, ...), custom_call_target="tpu_custom_call" | custom-call | flops 24159191040 | bytes 12582912 | tf_op jit(solution)/shard_map/attention_backward/pallas_call | solution.py:388
  245.1 13.1 %collective-permute-done.17 = bf16[2,512,256]{2,1,0:T(8,128)(2,1)S(1)} collective-permute-done((bf16[2,512,256]{2,1,0:T(8,128)(2,1)S(1)}, bf16[2,512,256]{2,1,0:T(8,128)(2,1)S(1)}, u32[]{:S(2)}, u32[]{:S(2)}) %collective-permute-start.17) | collective-permute-done | bytes 524320 | tf_op jit(solution)/shard_map/ppermute | solution.py:67
  269.8 8.1 %collective-permute-done.27 = bf16[256,1024]{1,0:T(8,128)(2,1)S(1)} collective-permute-done((bf16[256,1024]{1,0:T(8,128)(2,1)S(1)}, bf16[256,1024]{1,0:T(8,128)(2,1)S(1)}, u32[]{:S(2)}, u32[]{:S(2)}) %collective-permute-start.27) | collective-permute-done | bytes 524320 | tf_op jit(solution)/shard_map/ppermute | solution.py:67
  293.6 10.0 %all-to-all-done.4 = bf16[16,16,3072]{2,1,0:T(8,128)(2,1)S(1)} async-done(((bf16[16,16,3072]{2,1,0:T(8,128)(2,1)}), bf16[16,16,3072]{2,1,0:T(8,128)(2,1)S(1)}, u32[]{:S(2)}, u32[]{:S(2)}) %all-to-all-start.4) | async-done | bytes 1572896 | tf_op jit(solution)/shard_map/all_to_all | solution.py:87
  307.4 5.1 %all-to-all-start.5 = ((bf16[16,40,1024]{2,1,0:T(8,128)(2,1)}), bf16[16,40,1024]{2,1,0:T(8,128)(2,1)}, u32[]{:S(2)}, u32[]{:S(2)}) async-start(bf16[16,40,1024]{2,1,0:T(8,128)(2,1)} %pad_maximum_fusion.1), calls=%async_computation.5 | async-start | bytes 2621440 | tf_op jit(solution)/shard_map/all_to_all | solution.py:87
  312.6 9.0 %projection_grads.1 = (f32[8,512]{1,0:T(8,128)S(1)}, bf16[528,512]{1,0:T(8,128)(2,1)}, f32[512,512]{1,0:T(8,128)}, bf16[4,128,512]{2,1,0:T(8,128)(2,1)}, bf16[4,...) custom-call(s32[3]{0:T(128)S(1)} %pad_add_fusion.4.info_ref, ...), custom_call_target="tpu_custom_call" | custom-call | flops 4294967296 | bytes 16777216 | tf_op jit(solution)/shard_map/projection_grads/pallas_call | solution.py:701
  321.6 5.2 %collective-permute-start.28 = (bf16[528,512]{1,0:T(8,128)(2,1)}, bf16[528,512]{1,0:T(8,128)(2,1)S(1)}, u32[]{:S(2)}, u32[]{:S(2)}) collective-permute-start(bf16[528,512]{1,0:T(8,128)(2,1)} %get-tuple-element.170), channel_id=1, source_target_pairs={{0,2},{2,0},{1,3},{3,1},{4,6},{6,4},{5,7},{7,5},{8,10},{10,8},{9,1... | collective-permute-start | bytes 1622024 | tf_op jit(solution)/shard_map/ppermute | solution.py:67
  338.5 7.2 %collective-permute-done.31 = bf16[4,128,512]{2,1,0:T(8,128)(2,1)S(1)} collective-permute-done((bf16[4,128,512]{2,1,0:T(8,128)(2,1)}, bf16[4,128,512]{2,1,0:T(8,128)(2,1)S(1)}, u32[]{:S(2)}, u32[]{:S(2)}) %collective-permute-start.31) | collective-permute-done | bytes 524320 | tf_op jit(solution)/shard_map/ppermute | solution.py:67
  349.7 4.9 %all-to-all-start.6 = ((bf16[8,80,512]{2,1,0:T(8,128)(2,1)}), bf16[8,80,512]{2,1,0:T(8,128)(2,1)S(1)}, u32[]{:S(2)}, u32[]{:S(2)}) async-start(bf16[8,80,512]{2,1,0:T(8,128)(2,1)} %pad_maximum_fusion.3), calls=%async_computation.6 | async-start | bytes 1310720 | tf_op jit(solution)/shard_map/all_to_all | solution.py:87
  358.0 5.6 %collective-permute-done.30 = bf16[2,128,512]{2,1,0:T(8,128)(2,1)S(1)} collective-permute-done((bf16[2,128,512]{2,1,0:T(8,128)(2,1)S(1)}, bf16[2,128,512]{2,1,0:T(8,128)(2,1)S(1)}, u32[]{:S(2)}, u32[]{:S(2)}) %collective-permute-start.30) | collective-permute-done | bytes 262176 | tf_op jit(solution)/shard_map/ppermute | solution.py:67
  363.6 6.7 %all-to-all-done.6 = bf16[8,80,512]{2,1,0:T(8,128)(2,1)S(1)} async-done(((bf16[8,80,512]{2,1,0:T(8,128)(2,1)}), bf16[8,80,512]{2,1,0:T(8,128)(2,1)S(1)}, u32[]{:S(2)}, u32[]{:S(2)}) %all-to-all-start.6) | async-done | bytes 655392 | tf_op jit(solution)/shard_map/all_to_all | solution.py:87
  380.2 8.5 %collective-permute-done.39 = bf16[4,80,256]{2,1,0:T(8,128)(2,1)S(1)} collective-permute-done((bf16[4,80,256]{2,1,0:T(8,128)(2,1)S(1)}, bf16[4,80,256]{2,1,0:T(8,128)(2,1)S(1)}, u32[]{:S(2)}, u32[]{:S(2)}) %collective-permute-start.39) | collective-permute-done | bytes 163872 | tf_op jit(solution)/shard_map/ppermute | solution.py:67
  391.4 12.4 %collective-permute-done.40 = bf16[8,80,256]{2,1,0:T(8,128)(2,1)S(1)} collective-permute-done((bf16[8,80,256]{2,1,0:T(8,128)(2,1)S(1)}, bf16[8,80,256]{2,1,0:T(8,128)(2,1)S(1)}, u32[]{:S(2)}, u32[]{:S(2)}) %collective-permute-start.40) | collective-permute-done | bytes 327712 | tf_op jit(solution)/shard_map/ppermute | solution.py:67
  409.6 7.6 %collective-permute-done.41 = bf16[16,80,256]{2,1,0:T(8,128)(2,1)S(1)} collective-permute-done((bf16[16,80,256]{2,1,0:T(8,128)(2,1)S(1)}, bf16[16,80,256]{2,1,0:T(8,128)(2,1)S(1)}, u32[]{:S(2)}, u32[]{:S(2)}) %collective-permute-start.41) | collective-permute-done | bytes 655392 | tf_op jit(solution)/shard_map/ppermute | solution.py:67
  418.0 5.7 %collective-permute-start.47 = (bf16[4,4,2,88,1024]{4,3,2,1,0:T(8,128)(2,1)}, bf16[4,4,2,88,1024]{4,3,2,1,0:T(8,128)(2,1)}, u32[]{:S(2)}, u32[]{:S(2)}) collective-permute-start(bf16[4,4,2,88,1024]{4,3,2,1,0:T(8,128)(2,1)} %bitcast.134), channel_id=1, source_target_pairs={{0,2},{2,0},{1,3},{3,1},{4,6},{6,4},{5,7},{7,5},{8,10},{10,8},{9,1... | collective-permute-start | bytes 17301512 | tf_op jit(solution)/shard_map/ppermute | solution.py:67
  432.1 4.6 %place_rows.2 = (f32[512,3072]{1,0:T(8,128)}, f32[512,3072]{1,0:T(8,128)}, f32[4,4,96,1024]{3,2,1,0:T(8,128)}, f32[4,4,64,1024]{3,2,1,0:T(8,128)}) custom-call(s32[1]{0:T(128)} %bitcast.1.core_ref, bf16[4,4,2,88,1024]{4,3,2,1,0:T(8,128)(2,1)S(1)} %bitcast.135), custom_call_target="tpu_custom_call" | custom-call | flops 3145728 | bytes 18874368 | tf_op jit(solution)/shard_map/place_rows/pallas_call | solution.py:1024
  440.9 7.3 %place_rows.3 = (f32[512,3072]{1,0:T(8,128)}, f32[512,3072]{1,0:T(8,128)}, f32[4,4,96,1024]{3,2,1,0:T(8,128)}, f32[4,4,64,1024]{3,2,1,0:T(8,128)}) custom-call(s32[1]{0:T(128)} %bitcast.76.core_ref, bf16[4,4,2,88,1024]{4,3,2,1,0:T(8,128)(2,1)} %collective-permute-done.47.chunk_ref, ...), custom_call_target="tpu_custom_call", output_to_operand_aliasing={{0}: (2, {}), {1}: (3, {}), {2}: (4, {}), {3}: (5, {})} | custom-call | flops 3145728 | bytes 18874368 | tf_op jit(solution)/shard_map/place_rows/pallas_call | solution.py:1024
  (307 shorter events, 141.8 us)
Async XLA Ops:
  7.2 107.1 %all-gather.5.cloned.1.call-start = ((), (), s32[]{:S(2)}) async-start(), calls=%async_computation.7 | async-start | bytes 6127616 | tf_op jit(solution)/shard_map/all_gather | solution.py:1136
  14.3 13.7 %collective-permute-start.1 = (bf16[192,1024]{1,0:T(8,128)(2,1)}, bf16[192,1024]{1,0:T(8,128)(2,1)S(1)}, u32[]{:S(2)}, u32[]{:S(2)}) collective-permute-start(bf16[192,1024]{1,0:T(8,128)(2,1)} %get-tuple-element.113), channel_id=1, source_target_pairs={{0,5},{5,0},{1,4},{4,1},{2,7},{7,2},{3,6},{6,3},{8,13},{13,8},{9,1... | collective-permute-start | bytes 1179656 | tf_op jit(solution)/shard_map/ppermute | solution.py:67
  28.8 39.9 %all-to-all-start = ((bf16[8,128,1024]{2,1,0:T(8,128)(2,1)}), bf16[8,128,1024]{2,1,0:T(8,128)(2,1)}, u32[]{:S(2)}, u32[]{:S(2)}) async-start(bf16[8,128,1024]{2,1,0:T(8,128)(2,1)} %broadcast_in_dim.46), calls=%async_computation | async-start | bytes 4194304 | tf_op jit(solution)/shard_map/all_to_all | solution.py:87
  33.3 13.4 %collective-permute-start = (bf16[512,512]{1,0:T(8,128)(2,1)S(1)}, bf16[512,512]{1,0:T(8,128)(2,1)S(1)}, u32[]{:S(2)}, u32[]{:S(2)}) collective-permute-start(bf16[512,512]{1,0:T(8,128)(2,1)S(1)} %copy-done.49), channel_id=1, source_target_pairs={{0,5},{5,0},{1,4},{4,1},{2,7},{7,2},{3,6},{6,3},{8,13},{13,8},{9,1... | collective-permute-start | bytes 1572872 | tf_op jit(solution)/shard_map/ppermute | solution.py:67
  96.9 14.2 %collective-permute-start.3 = (bf16[2,512,256]{2,1,0:T(8,128)(2,1)S(1)}, bf16[2,512,256]{2,1,0:T(8,128)(2,1)S(1)}, u32[]{:S(2)}, u32[]{:S(2)}) collective-permute-start(bf16[2,512,256]{2,1,0:T(8,128)(2,1)S(1)} %pad_maximum_fusion.6.refs_0_), channel_id=1, source_target_pairs={{32,64},{64,32},{96,0},{0,96},{33,65},{65,33},{97,1},{1,97},{34,66... | collective-permute-start | bytes 1572872 | tf_op jit(solution)/shard_map/ppermute | solution.py:67
  97.5 15.0 %collective-permute-start.8 = (bf16[2,512,256]{2,1,0:T(8,128)(2,1)S(1)}, bf16[2,512,256]{2,1,0:T(8,128)(2,1)S(1)}, u32[]{:S(2)}, u32[]{:S(2)}) collective-permute-start(bf16[2,512,256]{2,1,0:T(8,128)(2,1)S(1)} %pad_maximum_fusion.7.refs_2_), channel_id=1, source_target_pairs={{0,2},{2,0},{1,3},{3,1},{4,6},{6,4},{5,7},{7,5},{8,10},{10,8},{9,1... | collective-permute-start | bytes 1572872 | tf_op jit(solution)/shard_map/ppermute | solution.py:67
  114.3 40.7 %collective-permute-start.10 = (bf16[16,176,1024]{2,1,0:T(8,128)(2,1)}, bf16[16,176,1024]{2,1,0:T(8,128)(2,1)}, u32[]{:S(2)}, u32[]{:S(2)}) collective-permute-start(bf16[16,176,1024]{2,1,0:T(8,128)(2,1)} %bitcast.151), channel_id=1, source_target_pairs={{0,2},{2,0},{1,3},{3,1},{4,6},{6,4},{5,7},{7,5},{8,10},{10,8},{9,1... | collective-permute-start | bytes 17301512 | tf_op jit(solution)/shard_map/ppermute | solution.py:67
  140.4 14.5 %all-to-all-start.2 = ((bf16[8,2,64,256]{3,2,1,0:T(8,128)(2,1)}), bf16[8,2,64,256]{3,2,1,0:T(8,128)(2,1)}, u32[]{:S(2)}, u32[]{:S(2)}) async-start(bf16[8,2,64,256]{3,2,1,0:T(8,128)(2,1)} %copy-done.11), calls=%async_computation.2 | async-start | bytes 1048576 | tf_op jit(solution)/shard_map/all_to_all | solution.py:87
  182.6 14.4 %all-to-all-start.3 = ((bf16[8,2,64,256]{3,2,1,0:T(8,128)(2,1)}), bf16[8,2,64,256]{3,2,1,0:T(8,128)(2,1)}, u32[]{:S(2)}, u32[]{:S(2)}) async-start(bf16[8,2,64,256]{3,2,1,0:T(8,128)(2,1)} %copy-done.10), calls=%async_computation.3 | async-start | bytes 1048576 | tf_op jit(solution)/shard_map/all_to_all | solution.py:87
  197.1 39.9 %collective-permute-start.12 = (bf16[768,1024]{1,0:T(8,128)(2,1)}, bf16[768,1024]{1,0:T(8,128)(2,1)S(1)}, u32[]{:S(2)}, u32[]{:S(2)}) collective-permute-start(bf16[768,1024]{1,0:T(8,128)(2,1)} %get-tuple-element.139), channel_id=1, source_target_pairs={{0,5},{5,0},{1,4},{4,1},{2,7},{7,2},{3,6},{6,3},{8,13},{13,8},{9,1... | collective-permute-start | bytes 4718600 | tf_op jit(solution)/shard_map/ppermute | solution.py:67
  199.9 37.1 %collective-permute-start.13 = (bf16[512,1536]{1,0:T(8,128)(2,1)}, bf16[512,1536]{1,0:T(8,128)(2,1)S(1)}, u32[]{:S(2)}, u32[]{:S(2)}) collective-permute-start(bf16[512,1536]{1,0:T(8,128)(2,1)} %get-tuple-element.140), channel_id=1, source_target_pairs={{0,8},{8,0},{16,24},{24,16},{1,9},{9,1},{17,25},{25,17},{2,10},{10... | collective-permute-start | bytes 4718600 | tf_op jit(solution)/shard_map/ppermute | solution.py:67
  201.1 36.5 %collective-permute-start.14 = (bf16[512,1536]{1,0:T(8,128)(2,1)}, bf16[512,1536]{1,0:T(8,128)(2,1)S(1)}, u32[]{:S(2)}, u32[]{:S(2)}) collective-permute-start(bf16[512,1536]{1,0:T(8,128)(2,1)} %get-tuple-element.141), channel_id=1, source_target_pairs={{8,16},{16,8},{24,0},{0,24},{9,17},{17,9},{25,1},{1,25},{10,18},{1... | collective-permute-start | bytes 4718600 | tf_op jit(solution)/shard_map/ppermute | solution.py:67
  202.9 34.0 %collective-permute-start.15 = (bf16[512,1024]{1,0:T(8,128)(2,1)}, bf16[512,1024]{1,0:T(8,128)(2,1)S(1)}, u32[]{:S(2)}, u32[]{:S(2)}) collective-permute-start(bf16[512,1024]{1,0:T(8,128)(2,1)} %get-tuple-element.142), channel_id=1, source_target_pairs={{0,4},{4,0},{1,5},{5,1},{2,6},{6,2},{3,7},{7,3},{8,12},{12,8},{9,1... | collective-permute-start | bytes 3145736 | tf_op jit(solution)/shard_map/ppermute | solution.py:67
  243.9 14.4 %collective-permute-start.17 = (bf16[2,512,256]{2,1,0:T(8,128)(2,1)S(1)}, bf16[2,512,256]{2,1,0:T(8,128)(2,1)S(1)}, u32[]{:S(2)}, u32[]{:S(2)}) collective-permute-start(bf16[2,512,256]{2,1,0:T(8,128)(2,1)S(1)} %get-tuple-element.206), channel_id=1, source_target_pairs={{32,64},{64,32},{96,0},{0,96},{33,65},{65,33},{97,1},{1,97},{34,66... | collective-permute-start | bytes 1572872 | tf_op jit(solution)/shard_map/ppermute | solution.py:67
  245.1 13.2 %collective-permute-start.18 = (bf16[2,512,256]{2,1,0:T(8,128)(2,1)S(1)}, bf16[2,512,256]{2,1,0:T(8,128)(2,1)S(1)}, u32[]{:S(2)}, u32[]{:S(2)}) collective-permute-start(bf16[2,512,256]{2,1,0:T(8,128)(2,1)S(1)} %get-tuple-element.205), channel_id=1, source_target_pairs={{0,32},{32,0},{64,96},{96,64},{1,33},{33,1},{65,97},{97,65},{2,34}... | collective-permute-start | bytes 1572872 | tf_op jit(solution)/shard_map/ppermute | solution.py:67
  258.8 19.1 %collective-permute-start.24 = (bf16[384,1024]{1,0:T(8,128)(2,1)S(1)}, bf16[384,1024]{1,0:T(8,128)(2,1)S(1)}, u32[]{:S(2)}, u32[]{:S(2)}) collective-permute-start(bf16[384,1024]{1,0:T(8,128)(2,1)S(1)} %add_convert_fusion.5), channel_id=1, source_target_pairs={{0,4},{4,0},{1,5},{5,1},{2,6},{6,2},{3,7},{7,3},{8,12},{12,8},{9,1... | collective-permute-start | bytes 2359304 | tf_op jit(solution)/shard_map/ppermute | solution.py:67
  259.4 18.5 %collective-permute-start.25 = (bf16[256,1536]{1,0:T(8,128)(2,1)S(1)}, bf16[256,1536]{1,0:T(8,128)(2,1)S(1)}, u32[]{:S(2)}, u32[]{:S(2)}) collective-permute-start(bf16[256,1536]{1,0:T(8,128)(2,1)S(1)} %add_convert_fusion.4), channel_id=1, source_target_pairs={{8,16},{16,8},{24,0},{0,24},{9,17},{17,9},{25,1},{1,25},{10,18},{1... | collective-permute-start | bytes 2359304 | tf_op jit(solution)/shard_map/ppermute | solution.py:67
  260.8 17.1 %collective-permute-start.26 = (bf16[256,1536]{1,0:T(8,128)(2,1)S(1)}, bf16[256,1536]{1,0:T(8,128)(2,1)S(1)}, u32[]{:S(2)}, u32[]{:S(2)}) collective-permute-start(bf16[256,1536]{1,0:T(8,128)(2,1)S(1)} %add_convert_fusion.3), channel_id=1, source_target_pairs={{0,8},{8,0},{16,24},{24,16},{1,9},{9,1},{17,25},{25,17},{2,10},{10... | collective-permute-start | bytes 2359304 | tf_op jit(solution)/shard_map/ppermute | solution.py:67
  280.5 23.0 %all-to-all-start.4 = ((bf16[16,16,3072]{2,1,0:T(8,128)(2,1)}), bf16[16,16,3072]{2,1,0:T(8,128)(2,1)S(1)}, u32[]{:S(2)}, u32[]{:S(2)}) async-start(bf16[16,16,3072]{2,1,0:T(8,128)(2,1)} %bitcast.149), calls=%async_computation.4 | async-start | bytes 3145728 | tf_op jit(solution)/shard_map/all_to_all | solution.py:87
  307.4 21.2 %all-to-all-start.5 = ((bf16[16,40,1024]{2,1,0:T(8,128)(2,1)}), bf16[16,40,1024]{2,1,0:T(8,128)(2,1)}, u32[]{:S(2)}, u32[]{:S(2)}) async-start(bf16[16,40,1024]{2,1,0:T(8,128)(2,1)} %pad_maximum_fusion.1), calls=%async_computation.5 | async-start | bytes 2621440 | tf_op jit(solution)/shard_map/all_to_all | solution.py:87
  312.5 105.5 %all-gather.7.cloned.1.call-start = ((), (), s32[]{:S(2)}) async-start(), calls=%async_computation.8 | async-start | bytes 6127616 | tf_op jit(solution)/shard_map/all_gather | solution.py:1327
  335.8 18.7 %collective-permute-start.29 = (bf16[4,128,512]{2,1,0:T(8,128)(2,1)}, bf16[4,128,512]{2,1,0:T(8,128)(2,1)}, u32[]{:S(2)}, u32[]{:S(2)}) collective-permute-start(bf16[4,128,512]{2,1,0:T(8,128)(2,1)} %get-tuple-element.174), channel_id=1, source_target_pairs={{8,16},{16,8},{24,0},{0,24},{9,17},{17,9},{25,1},{1,25},{10,18},{1... | collective-permute-start | bytes 1572872 | tf_op jit(solution)/shard_map/ppermute | solution.py:67
  349.7 20.6 %all-to-all-start.6 = ((bf16[8,80,512]{2,1,0:T(8,128)(2,1)}), bf16[8,80,512]{2,1,0:T(8,128)(2,1)S(1)}, u32[]{:S(2)}, u32[]{:S(2)}) async-start(bf16[8,80,512]{2,1,0:T(8,128)(2,1)} %pad_maximum_fusion.3), calls=%async_computation.6 | async-start | bytes 1310720 | tf_op jit(solution)/shard_map/all_to_all | solution.py:87
  379.4 29.3 %collective-permute-start.42 = (bf16[1,128,512]{2,1,0:T(8,128)(2,1)S(1)}, bf16[1,128,512]{2,1,0:T(8,128)(2,1)S(1)}, u32[]{:S(2)}, u32[]{:S(2)}) collective-permute-start(bf16[1,128,512]{2,1,0:T(8,128)(2,1)S(1)} %constant_dynamic-slice_fusion.1), channel_id=1, source_target_pairs={{0,4},{4,0},{1,5},{5,1},{2,6},{6,2},{3,7},{7,3},{8,12},{12,8},{9,1... | collective-permute-start | bytes 393224 | tf_op jit(solution)/shard_map/ppermute | solution.py:67
  388.7 15.2 %collective-permute-start.40 = (bf16[8,80,256]{2,1,0:T(8,128)(2,1)S(1)}, bf16[8,80,256]{2,1,0:T(8,128)(2,1)S(1)}, u32[]{:S(2)}, u32[]{:S(2)}) collective-permute-start(bf16[8,80,256]{2,1,0:T(8,128)(2,1)S(1)} %maximum_select_fusion.5), channel_id=1, source_target_pairs={{0,32},{32,0},{64,96},{96,64},{1,33},{33,1},{65,97},{97,65},{2,34}... | collective-permute-start | bytes 983048 | tf_op jit(solution)/shard_map/ppermute | solution.py:67
  389.7 15.1 %collective-permute-start.36 = (bf16[8,80,256]{2,1,0:T(8,128)(2,1)S(1)}, bf16[8,80,256]{2,1,0:T(8,128)(2,1)S(1)}, u32[]{:S(2)}, u32[]{:S(2)}) collective-permute-start(bf16[8,80,256]{2,1,0:T(8,128)(2,1)S(1)} %maximum_select_fusion.4), channel_id=1, source_target_pairs={{0,8},{8,0},{16,24},{24,16},{1,9},{9,1},{17,25},{25,17},{2,10},{10... | collective-permute-start | bytes 983048 | tf_op jit(solution)/shard_map/ppermute | solution.py:67
  390.6 18.1 %collective-permute-start.43 = (bf16[1,128,512]{2,1,0:T(8,128)(2,1)S(1)}, bf16[1,128,512]{2,1,0:T(8,128)(2,1)S(1)}, u32[]{:S(2)}, u32[]{:S(2)}) collective-permute-start(bf16[1,128,512]{2,1,0:T(8,128)(2,1)S(1)} %constant_dynamic-slice_fusion), channel_id=1, source_target_pairs={{0,8},{8,0},{16,24},{24,16},{1,9},{9,1},{17,25},{25,17},{2,10},{10... | collective-permute-start | bytes 393224 | tf_op jit(solution)/shard_map/ppermute | solution.py:67
  403.9 13.3 %collective-permute-start.41 = (bf16[16,80,256]{2,1,0:T(8,128)(2,1)S(1)}, bf16[16,80,256]{2,1,0:T(8,128)(2,1)S(1)}, u32[]{:S(2)}, u32[]{:S(2)}) collective-permute-start(bf16[16,80,256]{2,1,0:T(8,128)(2,1)S(1)} %maximum_select_fusion.3), channel_id=1, source_target_pairs={{32,64},{64,32},{96,0},{0,96},{33,65},{65,33},{97,1},{1,97},{34,66... | collective-permute-start | bytes 1966088 | tf_op jit(solution)/shard_map/ppermute | solution.py:67
  404.9 12.8 %collective-permute-start.37 = (bf16[16,80,256]{2,1,0:T(8,128)(2,1)S(1)}, bf16[16,80,256]{2,1,0:T(8,128)(2,1)S(1)}, u32[]{:S(2)}, u32[]{:S(2)}) collective-permute-start(bf16[16,80,256]{2,1,0:T(8,128)(2,1)S(1)} %maximum_select_fusion.2), channel_id=1, source_target_pairs={{8,16},{16,8},{24,0},{0,24},{9,17},{17,9},{25,1},{1,25},{10,18},{1... | collective-permute-start | bytes 1966088 | tf_op jit(solution)/shard_map/ppermute | solution.py:67
  418.0 22.9 %collective-permute-start.47 = (bf16[4,4,2,88,1024]{4,3,2,1,0:T(8,128)(2,1)}, bf16[4,4,2,88,1024]{4,3,2,1,0:T(8,128)(2,1)}, u32[]{:S(2)}, u32[]{:S(2)}) collective-permute-start(bf16[4,4,2,88,1024]{4,3,2,1,0:T(8,128)(2,1)} %bitcast.134), channel_id=1, source_target_pairs={{0,2},{2,0},{1,3},{3,1},{4,6},{6,4},{5,7},{7,5},{8,10},{10,8},{9,1... | collective-permute-start | bytes 17301512 | tf_op jit(solution)/shard_map/ppermute | solution.py:67
  423.6 13.0 %collective-permute-start.45 = (bf16[4,4,2,80,256]{4,3,2,1,0:T(8,128)(2,1)S(1)}, bf16[4,4,2,80,256]{4,3,2,1,0:T(8,128)(2,1)}, u32[]{:S(2)}, u32[]{:S(2)}) collective-permute-start(bf16[4,4,2,80,256]{4,3,2,1,0:T(8,128)(2,1)S(1)} %bitcast.131), channel_id=1, source_target_pairs={{0,2},{2,0},{1,3},{3,1},{4,6},{6,4},{5,7},{7,5},{8,10},{10,8},{9,1... | collective-permute-start | bytes 3932168 | tf_op jit(solution)/shard_map/ppermute | solution.py:67
  423.7 12.9 %collective-permute-start.46 = (bf16[4,4,2,80,256]{4,3,2,1,0:T(8,128)(2,1)S(1)}, bf16[4,4,2,80,256]{4,3,2,1,0:T(8,128)(2,1)}, u32[]{:S(2)}, u32[]{:S(2)}) collective-permute-start(bf16[4,4,2,80,256]{4,3,2,1,0:T(8,128)(2,1)S(1)} %bitcast.128), channel_id=1, source_target_pairs={{0,2},{2,0},{1,3},{3,1},{4,6},{6,4},{5,7},{7,5},{8,10},{10,8},{9,1... | collective-permute-start | bytes 3932168 | tf_op jit(solution)/shard_map/ppermute | solution.py:67
  (75 other events, 1088.2 us)
Sparse Core Ops, SparseCore 0:
  28.9 65.3 all-gather.4
  335.6 71.4 all-gather.6
